TPU v7x, 128 devices: a whole 4x4x4 slice. The times are simulated.
128 devices in a mesh: video: 4 (over z), frame: 32 (over y, x, core).
Axes of the slice: x: 4, y: 4, z: 4, core: 2. Of those that a mesh axis runs over, the one named last changes fastest.
Arguments:
- patches: bfloat16 [4, 46656, 1152], P('video', 'frame'), may hold values from -6 to 6
- latents: bfloat16 [4, 64, 1152], P('video'), may hold values from -600 to 600
- gain: bfloat16 [1152], replicated, may hold values from 0.25 to 1.75
- w_query: bfloat16 [1152, 1152], replicated, may hold values from -0.1875 to 0.1875
- w_key: bfloat16 [1152, 1152], replicated, may hold values from -0.1875 to 0.1875
- w_value: bfloat16 [1152, 1152], replicated, may hold values from -0.1875 to 0.1875
- w_out: bfloat16 [1152, 1152], P(None, 'frame'), may hold values from -0.1875 to 0.1875
- cotangent: bfloat16 [4, 64, 1152], P('video', None, 'frame'), may hold values from -6 to 6
Outputs:
- attended: bfloat16 [4, 64, 1152], P('video', None, 'frame')
- patch_grad: bfloat16 [4, 46656, 1152], P('video', 'frame')
- kv_grad: float32 [1152, 2304], P(('video', 'frame'))
All inputs are finite; a program needn't handle non-finite values.
Results may differ from a plain program's by a relative error of at most 0.04.
Values sent between devices are 32-bit elements; how exact they have to be, the bound alone decides.
No kernel may reach another device: no remote copies, remote signals or barrier semaphores. Data moves between devices by JAX's collectives and lax.ppermute only.
A program may use at most 192 MiB of HBM per device.

v0:
```python
import functools

import jax
import jax.numpy as jnp
from jax import lax
from jax.experimental import pallas as pl
from jax.experimental.pallas import tpu as pltpu
from jax.sharding import Mesh, PartitionSpec as P

HEADS = 16
BLOCK = 9
CHUNK = 40
F32, BF16 = jnp.float32, jnp.bfloat16


def dot(a, b, ca=1, cb=0):
    return lax.dot_general(a, b, (((ca,), (cb,)), ((), ())), preferred_element_type=F32)


def shift(value, axis, step):
    n = lax.axis_size(axis)
    return lax.ppermute(value, axis, [(i, (i + step) % n) for i in range(n)])


def spread(part, width):
    columns = part.shape[1]
    nlat = columns // HEADS
    row = lax.broadcasted_iota(jnp.int32, (HEADS * width, columns), 0) // width
    col = lax.broadcasted_iota(jnp.int32, (HEADS * width, columns), 1) // nlat
    return jnp.where(row == col, jnp.tile(part, (HEADS, 1)), 0.0).astype(BF16)


def by_head(flat, width):
    nlat = flat.shape[1]
    return flat.reshape(HEADS, width, nlat).transpose(1, 0, 2).reshape(width, HEADS * nlat)


def chosen_rows(d):
    v, y, x, c = (lax.axis_index(a) for a in ("v", "y", "x", "c"))
    at = lax.broadcasted_iota(jnp.int32, (32 * CHUNK, 1), 0)
    place, inner = at // CHUNK, at % CHUNK
    dv, i = inner // BLOCK, inner % BLOCK
    dc, dx, dy = place // 16, (place // 4) % 4, place % 4
    owner = ((((v + dv) % 4) * 4 + (y + dy) % 4) * 4 + (x + dx) % 4) * 2 + (c + dc) % 2
    row = jnp.where(inner < 4 * BLOCK, owner * BLOCK + i, -1)
    return (row == lax.broadcasted_iota(jnp.int32, (32 * CHUNK, d), 1)).astype(BF16)


def merge(parts, top_row):
    tops = [p[top_row : top_row + 1] for p in parts]
    top = tops[0]
    for t in tops[1:]:
        top = jnp.maximum(top, t)
    total = sum(p * jnp.exp(t - top) for p, t in zip(parts, tops))
    row = lax.broadcasted_iota(jnp.int32, total.shape, 0)
    return jnp.where(row == top_row, top, total)


def after(value, *others):
    return lax.optimization_barrier((value, *others))[0]


STEP = 256
GROUP = 4
WINDOW = 384


def group(j, width, nlat):
    start = GROUP * width * j // 128 * 128
    return slice(start, start + WINDOW), slice(GROUP * nlat * j, GROUP * nlat * (j + 1))


def call(body, steps, ins, outs, scratch, flops, moved, name):
    specs = [
        pl.BlockSpec(b, m, pipeline_mode=pl.Buffered(1)) if m is whole_block else pl.BlockSpec(b, m)
        for _, b, m in ins
    ]
    return pl.pallas_call(
        body,
        grid=(steps,),
        in_specs=specs,
        out_specs=[pl.BlockSpec(b, m) for _, _, b, m in outs],
        out_shape=[jax.ShapeDtypeStruct(s, t) for s, t, _, _ in outs],
        scratch_shapes=scratch,
        compiler_params=pltpu.CompilerParams(vmem_limit_bytes=56 * 2**20),
        cost_estimate=pl.CostEstimate(flops=flops, bytes_accessed=moved, transcendentals=0),
        name=name,
    )(*[a for a, _, _ in ins])


def whole_block(i):
    return (0, 0)


def row_block(i):
    return (i, 0)


def col_block(i):
    return (0, i)


def softmax_kernel(
    rows,
    width,
    nlat,
    x_ref,
    gain_ref,
    wk_ref,
    wv_ref,
    sq_ref,
    n_ref,
    v_ref,
    e_ref,
    pack_ref,
    s_all,
    v_all,
    acc_ref,
    state_ref,
):
    step, steps = pl.program_id(0), pl.num_programs(0) // 2
    at = pl.multiple_of((step % steps) * STEP, STEP)
    here = pl.ds(at, STEP)

    def valid(columns):
        return lax.broadcasted_iota(jnp.int32, (STEP, columns), 0) + at < rows

    @pl.when(step == 0)
    def _():
        acc_ref[...] = jnp.zeros_like(acc_ref)
        row = lax.broadcasted_iota(jnp.int32, state_ref.shape, 0)
        state_ref[...] = jnp.where(row == 0, -jnp.inf, 0.0)

    @pl.when(step < steps)
    def _():
        x = x_ref[...].astype(F32)
        centred = x - jnp.mean(x, axis=-1, keepdims=True)
        rstd = lax.rsqrt(jnp.mean(centred * centred, axis=-1, keepdims=True) + 1e-06)
        normed = centred * rstd * gain_ref[...].astype(F32)
        normed = jnp.where(valid(x.shape[1]), normed, 0.0).astype(BF16)
        n_ref[...] = normed
        keys = dot(normed, wk_ref[...]).astype(BF16)
        values = dot(normed, wv_ref[...]).astype(BF16)
        v_ref[...] = values
        v_all[here, :] = values
        for j in range(HEADS // GROUP):
            feat, cols = group(j, width, nlat)
            s = dot(keys[:, feat], sq_ref[feat, cols]) * (1.0 / width**0.5)
            s = jnp.where(valid(s.shape[1]), s, -jnp.inf)
            s_all[here, cols] = s
            state_ref[0:1, cols] = jnp.maximum(
                state_ref[0:1, cols], jnp.max(s, axis=0, keepdims=True)
            )

    @pl.when(step >= steps)
    def _():
        for j in range(HEADS // GROUP):
            feat, cols = group(j, width, nlat)
            e = jnp.exp(s_all[here, cols] - state_ref[0:1, cols])
            state_ref[1:2, cols] += jnp.sum(e, axis=0, keepdims=True)
            e = e.astype(BF16)
            e_ref[:, cols] = e
            acc_ref[j] += dot(v_all[here, feat], e, 0, 0)

    @pl.when(step == 2 * steps - 1)
    def _():
        for j in range(HEADS // GROUP):
            feat, cols = group(j, width, nlat)
            lane = lax.broadcasted_iota(jnp.int32, (width, GROUP * nlat), 1) // nlat
            out = jnp.zeros((width, GROUP * nlat), F32)
            for g in range(GROUP):
                start = (GROUP * j + g) * width - feat.start
                out = out + jnp.where(lane == g, acc_ref[j, start : start + width, :], 0.0)
            pack_ref[:width, cols] = out
        pack_ref[width:, :] = state_ref[...]


def grad_kernel(width, nlat, v_ref, sl_ref, e_ref, state_ref, t_ref, d_ref, keep_ref, send_ref):
    @pl.when(pl.program_id(0) == 0)
    def _():
        keep_ref[...] = jnp.zeros_like(keep_ref)
        send_ref[...] = jnp.zeros_like(send_ref)

    for j in range(HEADS // GROUP):
        feat, cols = group(j, width, nlat)
        dprob = dot(v_ref[:, feat], sl_ref[feat, cols])
        grad = e_ref[:, cols].astype(F32) * (dprob - state_ref[0:1, cols]) * state_ref[1:2, cols]
        d_ref[:, cols] = grad.astype(BF16)
    half = keep_ref.shape[0]
    keep_ref[...] += dot(t_ref[:half, :], d_ref[...])
    send_ref[...] += dot(t_ref[half:, :], d_ref[...])


def back_kernel(d_ref, e_ref, qk_ref, qv_ref, state_ref, x_ref, gain_ref, out_ref, scaled_ref):
    @pl.when(pl.program_id(0) == 0)
    def _():
        scaled_ref[...] = (qv_ref[...].astype(F32) * state_ref[2:3, :]).astype(BF16)

    normed_cot = dot(d_ref[...], qk_ref[...], 1, 1) + dot(e_ref[...], scaled_ref[...], 1, 1)
    x = x_ref[...].astype(F32)
    centred = x - jnp.mean(x, axis=-1, keepdims=True)
    rstd = lax.rsqrt(jnp.mean(centred * centred, axis=-1, keepdims=True) + 1e-06)
    xhat = centred * rstd
    dxhat = normed_cot * gain_ref[...].astype(F32)
    mean = jnp.mean(dxhat, axis=-1, keepdims=True)
    slope = jnp.mean(dxhat * xhat, axis=-1, keepdims=True)
    out_ref[...] = ((dxhat - mean - xhat * slope) * rstd).astype(BF16)


def split_kernel(keep_ref, got_ref, *outs):
    for k in range(4):
        for n in range(4):
            place = slice((4 * k + n) * CHUNK, (4 * k + n + 1) * CHUNK)
            outs[n][k * CHUNK : (k + 1) * CHUNK, :] = keep_ref[place, :] + got_ref[place, :]


def per_device(patches, latents, gain, w_query, w_key, w_value, w_out, cotangent):
    core = lax.axis_index("c")
    frames, latent_rows = patches[0], latents[0]
    rows, d = frames.shape
    nlat = latent_rows.shape[0]
    width = d // HEADS
    scale = 1.0 / width**0.5
    cols = HEADS * nlat
    steps = -(-rows // STEP)
    padded = steps * STEP
    half_rows = 16 * CHUNK
    gain_row = gain.reshape(1, d)

    def own_half(value):
        return lax.dynamic_slice_in_dim(value, core * (cols // 2), cols // 2, 1)

    def whole(half, other):
        return jnp.where(
            core == 0, jnp.concatenate([half, other], 1), jnp.concatenate([other, half], 1)
        )

    lc = by_head(dot(w_out, cotangent[0], 1, 1), width)
    lc = own_half(lc + shift(lc, "c", 1))

    query = dot(w_query, latent_rows, 0, 1).astype(BF16)
    spread_q = spread(by_head(query, width).astype(F32), width)
    frames_1, spread_1 = lax.optimization_barrier((frames, spread_q, lc))[:2]
    lc_y = [shift(lc, "y", k) for k in (1, 2, 3)]

    def first(i):
        return (jnp.minimum(i, steps - 1), 0)

    def second(i):
        return (jnp.maximum(i - steps, 0), 0)

    normed, values, expo, pack = call(
        functools.partial(softmax_kernel, rows, width, nlat),
        2 * steps,
        [
            (frames_1, (STEP, d), first),
            (gain_row, (1, d), whole_block),
            (w_key, (d, d), whole_block),
            (w_value, (d, d), whole_block),
            (spread_1, (d, cols), whole_block),
        ],
        [
            ((padded, d), BF16, (STEP, d), first),
            ((padded, d), BF16, (STEP, d), first),
            ((padded, cols), BF16, (STEP, cols), second),
            ((width + 8, cols), F32, (width + 8, cols), whole_block),
        ],
        [
            pltpu.VMEM((padded, cols), F32),
            pltpu.VMEM((padded, d), BF16),
            pltpu.VMEM((HEADS // GROUP, WINDOW, GROUP * nlat), F32),
            pltpu.VMEM((8, cols), F32),
        ],
        4 * padded * (d * d + WINDOW * cols),
        6 * padded * d + 2 * padded * cols + 2 * d * (2 * d + cols),
        "softmax",
    )
    lc = sum(lc_y, after(lc, pack))
    pack = after(pack, lc)
    paired = shift(pack, "c", 1)
    top, top_pair = pack[width : width + 1], paired[width : width + 1]
    top2 = jnp.maximum(top, top_pair)
    half = own_half(merge([pack, paired], width))

    turned = dot(chosen_rows(d), after(normed, half), 1, 1).astype(BF16)
    half = jnp.concatenate([half, jnp.tile(top2.reshape(2, cols // 2), (4, 1)), lc], axis=0)
    halves = [half] + [shift(half, "x", k) for k in (1, 2, 3)]
    tops = [h[width + 8 : width + 10].reshape(1, cols) for h in halves]
    top3 = jnp.maximum(jnp.maximum(tops[0], tops[1]), jnp.maximum(tops[2], tops[3]))
    halves[0] = after(halves[0], turned)
    half = merge([h[: width + 8] for h in halves], width)
    lc = sum(h[width + 16 :] for h in halves)
    lc = whole(lc, shift(lc, "c", 1))
    spread_lc = spread(lc, width)

    half_y = [shift(half, "y", k) for k in (1, 2, 3)]
    u_send = dot(turned[half_rows:], after(expo, half))
    u_got = shift(u_send, "c", 1)
    u = dot(turned[:half_rows], after(expo, u_send))
    half = merge([after(half, u, spread_lc)] + half_y, width)
    pack = whole(half, shift(half, "c", 1))
    gtop, gtotal = pack[width : width + 1], pack[width + 1 : width + 2]
    attn = pack[:width] / gtotal
    factor = jnp.exp(top - gtop) / gtotal
    drift = jnp.sum(lc * attn, axis=0, keepdims=True)
    state = jnp.concatenate([drift, factor * scale, factor, jnp.zeros((5, cols), F32)], axis=0)

    dscore, w, w_send = call(
        functools.partial(grad_kernel, width, nlat),
        steps,
        [
            (values, (STEP, d), row_block),
            (spread_lc, (d, cols), whole_block),
            (expo, (STEP, cols), row_block),
            (state, (8, cols), whole_block),
            (turned, (2 * half_rows, STEP), col_block),
        ],
        [
            ((padded, cols), BF16, (STEP, cols), row_block),
            ((half_rows, cols), F32, (half_rows, cols), whole_block),
            ((half_rows, cols), F32, (half_rows, cols), whole_block),
        ],
        [],
        2 * padded * cols * (WINDOW + 2 * half_rows),
        2 * padded * (2 * d + 2 * cols) + 12 * half_rows * cols,
        "gradient",
    )
    w_got = shift(w_send, "c", 1)
    u = after(u, w_send) * jnp.exp(top - top2) + u_got * jnp.exp(top_pair - top2)
    u = u.reshape(4, 4, CHUNK, cols)
    u_x = [shift(u[k], "x", k) for k in (1, 2, 3)]
    cut = jax.ShapeDtypeStruct((4 * CHUNK, cols), F32)
    parts = pl.pallas_call(
        split_kernel,
        out_shape=[cut] * 4,
        compiler_params=pltpu.CompilerParams(vmem_limit_bytes=56 * 2**20),
        cost_estimate=pl.CostEstimate(
            flops=half_rows * cols, bytes_accessed=12 * half_rows * cols, transcendentals=0
        ),
        name="split",
    )(w, w_got)


    q_key = dot(after(w_key, parts[0]), spread_q).astype(BF16)
    q_value = dot(after(w_value, parts[0]), spread_lc).astype(BF16)
    patch_grad = call(
        back_kernel,
        steps,
        [
            (after(dscore, parts[0]), (STEP, cols), row_block),
            (expo, (STEP, cols), row_block),
            (q_key, (d, cols), whole_block),
            (q_value, (d, cols), whole_block),
            (state, (8, cols), whole_block),
            (frames, (STEP, d), row_block),
            (gain_row, (1, d), whole_block),
        ],
        [((rows, d), BF16, (STEP, d), row_block)],
        [pltpu.VMEM((d, cols), BF16)],
        4 * padded * d * cols,
        4 * padded * (d + cols) + 4 * d * cols,
        "back",
    )[0]
    attn_rows = attn.reshape(width, HEADS, nlat).transpose(1, 0, 2).reshape(d, nlat).astype(BF16)
    attended = dot(attn_rows, w_out, 0, 0).astype(BF16)

    u = after(u[0], patch_grad) * jnp.exp(tops[0] - top3) + sum(
        u_x[k - 1] * jnp.exp(tops[k] - top3) for k in (1, 2, 3)
    )
    u = u * (jnp.exp(top3 - gtop) / gtotal)
    w = after(parts[0], patch_grad)
    w = w + shift(parts[1], "y", 1) + shift(parts[2], "y", 2) + shift(parts[3], "y", 3)
    w = w.reshape(4, CHUNK, cols)
    w = w[0] + shift(w[1], "x", 1) + shift(w[2], "x", 2) + shift(w[3], "x", 3)
    u = u[0] + shift(u[1], "y", 1) + shift(u[2], "y", 2) + shift(u[3], "y", 3)
    kv = jnp.concatenate(
        [dot(w.astype(BF16), spread_q, 1, 1), dot(u.astype(BF16), spread_lc, 1, 1)], axis=1
    )
    kv = [kv[k * BLOCK : (k + 1) * BLOCK] for k in range(4)]
    kv_grad = kv[0] + shift(kv[1], "v", 1) + shift(kv[2], "v", 2) + shift(kv[3], "v", 3)
    return (attended[None], patch_grad[None], kv_grad)


def solution(mesh):
    grid = Mesh(mesh.devices.reshape(4, 4, 4, 2), ("v", "y", "x", "c"))
    frame = ("y", "x", "c")
    return jax.shard_map(
        per_device,
        mesh=grid,
        in_specs=(
            P("v", frame, None),
            P("v", None, None),
            P(),
            P(),
            P(),
            P(),
            P(None, frame),
            P("v", None, frame),
        ),
        out_specs=(
            P("v", None, frame),
            P("v", frame, None),
            P(("v", "y", "x", "c"), None),
        ),
        check_vma=False,
    )
```

profile of v0, /device:TPU:0, one launch (start us, length us, event | category | flops | bytes accessed | tf_op | source)
XLA Modules:
  0.0 167.3 jit_solution(3881681659711136256)
XLA Ops:
  0.6 1.3 dot_general.33
  2.0 1.0 fusion.22
  3.2 1.3 reshape.502.gain_ref
  4.5 1.5 fusion.3
  6.0 0.5 reshape.508
  6.5 0.4 copy.13
  7.2 1.9 %fusion.1.sq_ref = bf16[1152,1024]{1,0:T(8,128)(2,1)} fusion(bf16[72,1024]{1,0:T(8,128)(2,1)S(1)} %reshape.507, s32[1024]{0:T(1024)S(1)} %get-tuple-element.100, s32[1024]{0:T(1024)S(1)} %get-tuple-element.101, s32[1152]{0:T(1024)S(1)} %get-tuple-element.98, s32[1152]{0:T(1024)S(1)} %get-tuple-element.99, pred[1152]{0:T(1024)(128)(4,1)S(1)} %fusion.69, ...), kind=kLoop, calls=%fused_computation.5 | loop fusion | flops 4718592 | bytes 2526336 | tf_op jit(solution)/shard_map/convert_element_type | solution.py:30
  9.1 3.4 %collective-permute-start.2 = (f32[72,512]{1,0:T(8,128)S(1)}, f32[72,512]{1,0:T(8,128)S(1)}, u32[]{:S(2)}, u32[]{:S(2)}) collective-permute-start(f32[72,512]{1,0:T(8,128)S(1)} %dynamic-slice_add_fusion), channel_id=1, source_target_pairs={{0,16},{8,24},{16,0},{24,8},{1,17},{9,25},{17,1},{25,9},{2,18},{10... | collective-permute-start | bytes 442376 | tf_op jit(solution)/shard_map/ppermute | solution.py:22
  12.5 0.7 collective-permute-start.1
  13.2 2.6 %collective-permute-start.3 = (f32[72,512]{1,0:T(8,128)S(1)}, f32[72,512]{1,0:T(8,128)S(1)}, u32[]{:S(2)}, u32[]{:S(2)}) collective-permute-start(f32[72,512]{1,0:T(8,128)S(1)} %dynamic-slice_add_fusion), channel_id=1, source_target_pairs={{0,24},{8,0},{16,8},{24,16},{1,25},{9,1},{17,9},{25,17},{2,26},{10... | collective-permute-start | bytes 442376 | tf_op jit(solution)/shard_map/ppermute | solution.py:22
  15.7 23.6 %softmax.1 = (bf16[1536,1152]{1,0:T(8,128)(2,1)}, bf16[1536,1152]{1,0:T(8,128)(2,1)}, bf16[1536,1024]{1,0:T(8,128)(2,1)}, f32[80,1024]{1,0:T(8,128)}) custom-call(bf16[1458,1152]{1,0:T(8,128)(2,1)} %bitcast.130, bf16[1,1152]{1,0:T(2,128)(2,1)} %reshape.502.gain_ref, bf16[1152,1152]{1,0:T(8,128)(2,1)} %wk_ref.1, bf16[1152,1152]{1,0:T(8,128)(2,1)} %wv_ref.1, ...), custom_call_target="tpu_custom_call" | custom-call | flops 10569646080 | bytes 21430272 | tf_op jit(solution)/shard_map/softmax/pallas_call | solution.py:78
  39.7 1.7 collective-permute-done.4
  41.3 0.8 subtract_exponential_fusion.5
  42.3 0.5 broadcast.419
  42.8 0.7 subtract_exponential_fusion.4
  43.6 1.0 fusion.21
  44.6 2.8 %collective-permute-start.7 = (f32[160,512]{1,0:T(8,128)S(1)}, f32[160,512]{1,0:T(8,128)S(1)}, u32[]{:S(2)}, u32[]{:S(2)}) collective-permute-start(f32[160,512]{1,0:T(8,128)S(1)} %pad_maximum_fusion), channel_id=1, source_target_pairs={{0,6},{2,0},{4,2},{6,4},{1,7},{3,1},{5,3},{7,5},{8,14},{10,8},{12,... | collective-permute-start | bytes 983048 | tf_op jit(solution)/shard_map/ppermute | solution.py:22
  47.4 0.8 collective-permute-start.6
  48.2 0.9 collective-permute-start.5
  49.1 7.8 %convolution_convert_fusion.t_ref = bf16[1280,1536]{1,0:T(8,128)(2,1)S(1)} fusion(bf16[1536,1152]{1,0:T(8,128)(2,1)} %get-tuple-element.35, s32[1280]{0:T(1024)S(1)} %fusion.47), kind=kOutput, calls=%fused_computation | convolution fusion | flops 4533288960 | bytes 7476224 | tf_op jit(solution)/shard_map/dot_general | solution.py:17
  56.9 4.8 %collective-permute-done.7 = f32[160,512]{1,0:T(8,128)S(1)} collective-permute-done((f32[160,512]{1,0:T(8,128)S(1)}, f32[160,512]{1,0:T(8,128)S(1)}, u32[]{:S(2)}, u32[]{:S(2)}) %collective-permute-start.7) | collective-permute-done | bytes 327712 | tf_op jit(solution)/shard_map/ppermute | solution.py:22
  61.8 3.7 %collective-permute-done.5 = f32[160,512]{1,0:T(8,128)S(1)} collective-permute-done((f32[160,512]{1,0:T(8,128)S(1)}, f32[160,512]{1,0:T(8,128)S(1)}, u32[]{:S(2)}, u32[]{:S(2)}) %collective-permute-start.5) | collective-permute-done | bytes 327712 | tf_op jit(solution)/shard_map/ppermute | solution.py:22
  65.7 1.5 collective-permute-start.10
  67.2 0.5 collective-permute-start.9
  67.7 3.8 %fusion.4 = f32[640,1024]{1,0:T(8,128)} fusion(bf16[1536,1024]{1,0:T(8,128)(2,1)S(1)} %copy-done.8, bf16[1280,1536]{1,0:T(8,128)(2,1)S(1)} %convolution_convert_fusion.t_ref), kind=kOutput, calls=%fused_computation.13 | convolution fusion | flops 2013265920 | bytes 7733248 | tf_op jit(solution)/shard_map/dot_general | solution.py:17
  71.5 0.6 collective-permute-start.8
  72.1 3.8 %fusion.6 = f32[640,1024]{1,0:T(8,128)} fusion(bf16[1536,1024]{1,0:T(8,128)(2,1)S(1)} %copy-done.8, bf16[1280,1536]{1,0:T(8,128)(2,1)S(1)} %convolution_convert_fusion.t_ref), kind=kOutput, calls=%fused_computation.15 | convolution fusion | flops 2013265920 | bytes 7733248 | tf_op jit(solution)/shard_map/dot_general | solution.py:17
  75.9 0.3 collective-permute-done.8
  76.2 2.0 %fusion.sl_ref = bf16[1152,1024]{1,0:T(8,128)(2,1)} fusion(f32[72,1024]{1,0:T(8,128)S(1)} %maximum_select_fusion.1, s32[1024]{0:T(1024)S(1)} %get-tuple-element.100, s32[1024]{0:T(1024)S(1)} %get-tuple-element.101, s32[1152]{0:T(1024)S(1)} %get-tuple-element.98, s32[1152]{0:T(1024)S(1)} %get-tuple-element.99, pred[1152]{0:T(1024)(128)(4,1)S(1)} %fusion.69, ...), kind=kLoop, calls=%fused_computation.3 | loop fusion | flops 4718592 | bytes 2673792 | tf_op jit(solution)/shard_map/convert_element_type | solution.py:30
  78.4 0.5 collective-permute-start.12
  78.9 1.0 collective-permute-done.12
  79.9 0.8 broadcast_multiply_fusion
  80.8 0.7 maximum_maximum_fusion.state_ref
  81.5 12.4 %gradient.1 = (bf16[1536,1024]{1,0:T(8,128)(2,1)}, f32[640,1024]{1,0:T(8,128)}, f32[640,1024]{1,0:T(8,128)}) custom-call(bf16[1536,1152]{1,0:T(8,128)(2,1)} %get-tuple-element.41.v_ref, bf16[1152,1024]{1,0:T(8,128)(2,1)} %fusion.sl_ref, bf16[1536,1024]{1,0:T(8,128)(2,1)} %get-tuple-element.39.e_ref, f32[8,1024]{1,0:T(8,128)} %maximum_maximum_fusion.state_ref, ...), custom_call_target="tpu_custom_call" | custom-call | flops 5234491392 | bytes 21233664 | tf_op jit(solution)/shard_map/gradient/pallas_call | solution.py:78
  93.9 0.4 collective-permute-start.13
  94.5 0.4 copy.16
  95.2 2.4 %multiply_add_fusion = f32[640,1024]{1,0:T(8,128)S(1)} fusion(f32[640,1024]{1,0:T(8,128)S(1)} %collective-permute-done.20, f32[640,1024]{1,0:T(8,128)} %fusion.6, f32[1024]{0:T(1024)S(1)} %bitcast.114, f32[1024]{0:T(1024)S(1)} %bitcast.112), kind=kLoop, calls=%fused_computation.10 | loop fusion | flops 1966080 | bytes 7872512 | tf_op jit(solution)/shard_map/add | solution.py:329
  97.6 0.3 fusion.75
  97.9 0.7 collective-permute-start.23
  98.6 0.8 collective-permute-start.22
  99.4 0.8 collective-permute-start.21
  100.2 4.1 %split.1 = (f32[160,1024]{1,0:T(8,128)}, f32[160,1024]{1,0:T(8,128)}, f32[160,1024]{1,0:T(8,128)}, f32[160,1024]{1,0:T(8,128)}) custom-call(f32[640,1024]{1,0:T(8,128)} %get-tuple-element.43.keep_ref, f32[640,1024]{1,0:T(8,128)} %collective-permute-done.13.got_ref), custom_call_target="tpu_custom_call" | custom-call | flops 655360 | bytes 7864320 | tf_op jit(solution)/shard_map/split/pallas_call | solution.py:333
  104.2 1.6 collective-permute-start.14
  105.8 2.9 %collective-permute-start.15 = (f32[160,1024]{1,0:T(8,128)}, f32[160,1024]{1,0:T(8,128)}, u32[]{:S(2)}, u32[]{:S(2)}) collective-permute-start(f32[160,1024]{1,0:T(8,128)} %get-tuple-element.51), channel_id=1, source_target_pairs={{0,16},{8,24},{16,0},{24,8},{1,17},{9,25},{17,1},{25,9},{2,18},{10... | collective-permute-start | bytes 1966088 | tf_op jit(solution)/shard_map/ppermute | solution.py:22
  108.7 6.3 %convolution_convert_fusion.2.qk_ref = bf16[1152,1024]{1,0:T(8,128)(2,1)} fusion(bf16[1152,1152]{1,0:T(8,128)(2,1)} %wk_ref.1, bf16[1152,1024]{1,0:T(8,128)(2,1)S(1)} %copy-done.2), kind=kOutput, calls=%fused_computation.8 | convolution fusion | flops 2719088640 | bytes 7372800 | tf_op jit(solution)/shard_map/dot_general | solution.py:17
  115.0 4.5 %convolution_convert_fusion.1.qv_ref = bf16[1152,1024]{1,0:T(8,128)(2,1)} fusion(bf16[1152,1152]{1,0:T(8,128)(2,1)S(1)} %copy-done.6, bf16[1152,1024]{1,0:T(8,128)(2,1)S(1)} %copy-done.3), kind=kOutput, calls=%fused_computation.7 | convolution fusion | flops 2719088640 | bytes 7372800 | tf_op jit(solution)/shard_map/dot_general | solution.py:17
  119.5 2.3 %collective-permute-start.16 = (f32[160,1024]{1,0:T(8,128)}, f32[160,1024]{1,0:T(8,128)}, u32[]{:S(2)}, u32[]{:S(2)}) collective-permute-start(f32[160,1024]{1,0:T(8,128)} %get-tuple-element.52), channel_id=1, source_target_pairs={{0,24},{8,0},{16,8},{24,16},{1,25},{9,1},{17,9},{25,17},{2,26},{10... | collective-permute-start | bytes 1966088 | tf_op jit(solution)/shard_map/ppermute | solution.py:22
  121.8 15.7 %back.1 = bf16[1458,1152]{1,0:T(8,128)(2,1)} custom-call(bf16[1536,1024]{1,0:T(8,128)(2,1)} %get-tuple-element.46.d_ref, bf16[1536,1024]{1,0:T(8,128)(2,1)} %get-tuple-element.39.e_ref, bf16[1152,1024]{1,0:T(8,128)(2,1)} %convolution_convert_fusion.2.qk_ref, bf16[1152,1024]{1,0:T(8,128)(2,1)} %convolution_convert_fusion.1.qv_ref, ...), custom_call_target="tpu_custom_call" | custom-call | flops 7247757312 | bytes 18087936 | tf_op jit(solution)/shard_map/back/pallas_call | solution.py:78
  137.5 1.8 %add_multiply_fusion = f32[4,40,1024]{2,1,0:T(8,128)S(1)} fusion(f32[4,40,1024]{2,1,0:T(8,128)} %collective-permute-done.23, f32[4,40,1024]{2,1,0:T(8,128)} %collective-permute-done.22, f32[4,40,1024]{2,1,0:T(8,128)} %collective-permute-done.21, f32[4,40,1024]{2,1,0:T(8,128)S(1)} %bitcast.96, f32[1024]{0:T(1024)S(1)} %bitcast.117, ...), kind=kLoop, calls=%fused_computation.19 | loop fusion | flops 1310720 | bytes 3297280 | tf_op jit(solution)/shard_map/mul | solution.py:370
  139.4 3.2 %collective-permute-start.26 = (f32[40,1024]{1,0:T(8,128)S(1)}, f32[40,1024]{1,0:T(8,128)S(1)}, u32[]{:S(2)}, u32[]{:S(2)}) collective-permute-start(f32[40,1024]{1,0:T(8,128)S(1)} %get-tuple-element.73), channel_id=1, source_target_pairs={{0,24},{8,0},{16,8},{24,16},{1,25},{9,1},{17,9},{25,17},{2,26},{10... | collective-permute-start | bytes 491528 | tf_op jit(solution)/shard_map/ppermute | solution.py:22
  142.7 1.5 add_add_fusion
  144.3 1.9 %collective-permute-start.17 = (f32[40,1024]{1,0:T(8,128)S(1)}, f32[40,1024]{1,0:T(8,128)S(1)}, u32[]{:S(2)}, u32[]{:S(2)}) collective-permute-start(f32[40,1024]{1,0:T(8,128)S(1)} %get-tuple-element.69), channel_id=1, source_target_pairs={{0,2},{2,4},{4,6},{6,0},{1,3},{3,5},{5,7},{7,1},{8,10},{10,12},{12... | collective-permute-start | bytes 491528 | tf_op jit(solution)/shard_map/ppermute | solution.py:22
  146.2 1.4 collective-permute-start.19
  147.7 3.9 %collective-permute-start.18 = (f32[40,1024]{1,0:T(8,128)S(1)}, f32[40,1024]{1,0:T(8,128)S(1)}, u32[]{:S(2)}, u32[]{:S(2)}) collective-permute-start(f32[40,1024]{1,0:T(8,128)S(1)} %get-tuple-element.71), channel_id=1, source_target_pairs={{0,4},{2,6},{4,0},{6,2},{1,5},{3,7},{5,1},{7,3},{8,12},{10,14},{12... | collective-permute-start | bytes 491528 | tf_op jit(solution)/shard_map/ppermute | solution.py:22
  151.7 0.8 fusion.34
  152.6 2.3 %collective-permute-done.18 = f32[40,1024]{1,0:T(8,128)S(1)} collective-permute-done((f32[40,1024]{1,0:T(8,128)S(1)}, f32[40,1024]{1,0:T(8,128)S(1)}, u32[]{:S(2)}, u32[]{:S(2)}) %collective-permute-start.18) | collective-permute-done | bytes 163872 | tf_op jit(solution)/shard_map/ppermute | solution.py:22
  155.0 0.8 fusion.32
  155.8 2.0 %collective-permute-start.27 = (f32[9,2304]{1,0:T(8,128)S(1)}, f32[9,2304]{1,0:T(8,128)S(1)}, u32[]{:S(2)}, u32[]{:S(2)}) collective-permute-start(f32[9,2304]{1,0:T(8,128)S(1)} %get-tuple-element.75), channel_id=1, source_target_pairs={{0,32},{32,64},{64,96},{96,0},{1,33},{33,65},{65,97},{97,1},{2,34}... | collective-permute-start | bytes 248840 | tf_op jit(solution)/shard_map/ppermute | solution.py:22
  157.8 2.2 %collective-permute-start.29 = (f32[9,2304]{1,0:T(8,128)S(1)}, f32[9,2304]{1,0:T(8,128)S(1)}, u32[]{:S(2)}, u32[]{:S(2)}) collective-permute-start(f32[9,2304]{1,0:T(8,128)S(1)} %get-tuple-element.76), channel_id=1, source_target_pairs={{0,96},{32,0},{64,32},{96,64},{1,97},{33,1},{65,33},{97,65},{2,98}... | collective-permute-start | bytes 248840 | tf_op jit(solution)/shard_map/ppermute | solution.py:22
  160.0 1.8 %collective-permute-start.28 = (f32[9,2304]{1,0:T(8,128)S(1)}, f32[9,2304]{1,0:T(8,128)S(1)}, u32[]{:S(2)}, u32[]{:S(2)}) collective-permute-start(f32[9,2304]{1,0:T(8,128)S(1)} %get-tuple-element.77), channel_id=1, source_target_pairs={{0,64},{32,96},{64,0},{96,32},{1,65},{33,97},{65,1},{97,33},{2,66}... | collective-permute-start | bytes 248840 | tf_op jit(solution)/shard_map/ppermute | solution.py:22
  161.8 0.8 fusion.8
  162.6 1.2 collective-permute-done.27
  163.8 2.9 %collective-permute-done.28 = f32[9,2304]{1,0:T(8,128)S(1)} collective-permute-done((f32[9,2304]{1,0:T(8,128)S(1)}, f32[9,2304]{1,0:T(8,128)S(1)}, u32[]{:S(2)}, u32[]{:S(2)}) %collective-permute-start.28) | collective-permute-done | bytes 82976 | tf_op jit(solution)/shard_map/ppermute | solution.py:22
  166.6 0.7 fusion.28
  (89 shorter events, 2.7 us)
Async XLA Ops:
  0.6 3.9 %copy-start = (bf16[1152,1152]{1,0:T(8,128)(2,1)S(1)}, bf16[1152,1152]{1,0:T(8,128)(2,1)}, u32[]{:S(2)}) copy-start(bf16[1152,1152]{1,0:T(8,128)(2,1)} %param.11) | copy-start | bytes 7962628
  3.1 6.0 %collective-permute-start = (f32[72,1024]{1,0:T(8,128)S(1)}, f32[72,1024]{1,0:T(8,128)S(1)}, u32[]{:S(2)}, u32[]{:S(2)}) collective-permute-start(f32[72,1024]{1,0:T(8,128)S(1)} %copy.17), channel_id=1, source_target_pairs={{0,1},{1,0},{2,3},{3,2},{4,5},{5,4},{6,7},{7,6},{8,9},{9,8},{10,11... | collective-permute-start | bytes 884744 | tf_op jit(solution)/shard_map/ppermute | solution.py:22
  9.1 30.2 %collective-permute-start.2 = (f32[72,512]{1,0:T(8,128)S(1)}, f32[72,512]{1,0:T(8,128)S(1)}, u32[]{:S(2)}, u32[]{:S(2)}) collective-permute-start(f32[72,512]{1,0:T(8,128)S(1)} %dynamic-slice_add_fusion), channel_id=1, source_target_pairs={{0,16},{8,24},{16,0},{24,8},{1,17},{9,25},{17,1},{25,9},{2,18},{10... | collective-permute-start | bytes 442376 | tf_op jit(solution)/shard_map/ppermute | solution.py:22
  12.5 26.9 %collective-permute-start.1 = (f32[72,512]{1,0:T(8,128)S(1)}, f32[72,512]{1,0:T(8,128)S(1)}, u32[]{:S(2)}, u32[]{:S(2)}) collective-permute-start(f32[72,512]{1,0:T(8,128)S(1)} %dynamic-slice_add_fusion), channel_id=1, source_target_pairs={{0,8},{8,16},{16,24},{24,0},{1,9},{9,17},{17,25},{25,1},{2,10},{10... | collective-permute-start | bytes 442376 | tf_op jit(solution)/shard_map/ppermute | solution.py:22
  13.2 26.2 %collective-permute-start.3 = (f32[72,512]{1,0:T(8,128)S(1)}, f32[72,512]{1,0:T(8,128)S(1)}, u32[]{:S(2)}, u32[]{:S(2)}) collective-permute-start(f32[72,512]{1,0:T(8,128)S(1)} %dynamic-slice_add_fusion), channel_id=1, source_target_pairs={{0,24},{8,0},{16,8},{24,16},{1,25},{9,1},{17,9},{25,17},{2,26},{10... | collective-permute-start | bytes 442376 | tf_op jit(solution)/shard_map/ppermute | solution.py:22
  39.4 1.9 %collective-permute-start.4 = (f32[80,1024]{1,0:T(8,128)}, f32[80,1024]{1,0:T(8,128)S(1)}, u32[]{:S(2)}, u32[]{:S(2)}) collective-permute-start(f32[80,1024]{1,0:T(8,128)} %get-tuple-element.33), channel_id=1, source_target_pairs={{0,1},{1,0},{2,3},{3,2},{4,5},{5,4},{6,7},{7,6},{8,9},{9,8},{10,11... | collective-permute-start | bytes 983048 | tf_op jit(solution)/shard_map/ppermute | solution.py:22
  44.6 17.2 %collective-permute-start.7 = (f32[160,512]{1,0:T(8,128)S(1)}, f32[160,512]{1,0:T(8,128)S(1)}, u32[]{:S(2)}, u32[]{:S(2)}) collective-permute-start(f32[160,512]{1,0:T(8,128)S(1)} %pad_maximum_fusion), channel_id=1, source_target_pairs={{0,6},{2,0},{4,2},{6,4},{1,7},{3,1},{5,3},{7,5},{8,14},{10,8},{12,... | collective-permute-start | bytes 983048 | tf_op jit(solution)/shard_map/ppermute | solution.py:22
  47.4 14.3 %collective-permute-start.6 = (f32[160,512]{1,0:T(8,128)S(1)}, f32[160,512]{1,0:T(8,128)S(1)}, u32[]{:S(2)}, u32[]{:S(2)}) collective-permute-start(f32[160,512]{1,0:T(8,128)S(1)} %pad_maximum_fusion), channel_id=1, source_target_pairs={{0,4},{2,6},{4,0},{6,2},{1,5},{3,7},{5,1},{7,3},{8,12},{10,14},{12... | collective-permute-start | bytes 983048 | tf_op jit(solution)/shard_map/ppermute | solution.py:22
  48.2 17.2 %collective-permute-start.5 = (f32[160,512]{1,0:T(8,128)S(1)}, f32[160,512]{1,0:T(8,128)S(1)}, u32[]{:S(2)}, u32[]{:S(2)}) collective-permute-start(f32[160,512]{1,0:T(8,128)S(1)} %pad_maximum_fusion), channel_id=1, source_target_pairs={{0,2},{2,4},{4,6},{6,0},{1,3},{3,5},{5,7},{7,1},{8,10},{10,12},{12... | collective-permute-start | bytes 983048 | tf_op jit(solution)/shard_map/ppermute | solution.py:22
  49.1 18.5 %copy-start.8 = (bf16[1536,1024]{1,0:T(8,128)(2,1)S(1)}, bf16[1536,1024]{1,0:T(8,128)(2,1)}, u32[]{:S(2)}) copy-start(bf16[1536,1024]{1,0:T(8,128)(2,1)} %get-tuple-element.39.e_ref) | copy-start | bytes 9437188
  56.9 15.1 %copy-start.7 = (bf16[1280,1536]{1,0:T(8,128)(2,1)}, bf16[1280,1536]{1,0:T(8,128)(2,1)S(1)}, u32[]{:S(2)}) copy-start(bf16[1280,1536]{1,0:T(8,128)(2,1)S(1)} %convolution_convert_fusion.t_ref) | copy-start | bytes 11796484
  65.6 12.7 %collective-permute-start.11 = (f32[80,512]{1,0:T(8,128)S(1)}, f32[80,512]{1,0:T(8,128)S(1)}, u32[]{:S(2)}, u32[]{:S(2)}) collective-permute-start(f32[80,512]{1,0:T(8,128)S(1)} %fusion.17), channel_id=1, source_target_pairs={{0,24},{8,0},{16,8},{24,16},{1,25},{9,1},{17,9},{25,17},{2,26},{10... | collective-permute-start | bytes 491528 | tf_op jit(solution)/shard_map/ppermute | solution.py:22
  65.7 12.6 %collective-permute-start.10 = (f32[80,512]{1,0:T(8,128)S(1)}, f32[80,512]{1,0:T(8,128)S(1)}, u32[]{:S(2)}, u32[]{:S(2)}) collective-permute-start(f32[80,512]{1,0:T(8,128)S(1)} %fusion.17), channel_id=1, source_target_pairs={{0,16},{8,24},{16,0},{24,8},{1,17},{9,25},{17,1},{25,9},{2,18},{10... | collective-permute-start | bytes 491528 | tf_op jit(solution)/shard_map/ppermute | solution.py:22
  67.2 11.1 %collective-permute-start.9 = (f32[80,512]{1,0:T(8,128)S(1)}, f32[80,512]{1,0:T(8,128)S(1)}, u32[]{:S(2)}, u32[]{:S(2)}) collective-permute-start(f32[80,512]{1,0:T(8,128)S(1)} %fusion.17), channel_id=1, source_target_pairs={{0,8},{8,16},{16,24},{24,0},{1,9},{9,17},{17,25},{25,1},{2,10},{10... | collective-permute-start | bytes 491528 | tf_op jit(solution)/shard_map/ppermute | solution.py:22
  71.4 23.7 %collective-permute-start.20 = (f32[640,1024]{1,0:T(8,128)}, f32[640,1024]{1,0:T(8,128)S(1)}, u32[]{:S(2)}, u32[]{:S(2)}) collective-permute-start(f32[640,1024]{1,0:T(8,128)} %fusion.4), channel_id=1, source_target_pairs={{0,1},{1,0},{2,3},{3,2},{4,5},{5,4},{6,7},{7,6},{8,9},{9,8},{10,11... | collective-permute-start | bytes 7864328 | tf_op jit(solution)/shard_map/ppermute | solution.py:22
  71.5 4.7 %collective-permute-start.8 = (f32[72,512]{1,0:T(8,128)S(1)}, f32[72,512]{1,0:T(8,128)S(1)}, u32[]{:S(2)}, u32[]{:S(2)}) collective-permute-start(f32[72,512]{1,0:T(8,128)S(1)} %slice_add_fusion.1), channel_id=1, source_target_pairs={{0,1},{1,0},{2,3},{3,2},{4,5},{5,4},{6,7},{7,6},{8,9},{9,8},{10,11... | collective-permute-start | bytes 442376 | tf_op jit(solution)/shard_map/ppermute | solution.py:22
  78.4 1.5 collective-permute-start.12
  93.9 6.3 %collective-permute-start.13 = (f32[640,1024]{1,0:T(8,128)}, f32[640,1024]{1,0:T(8,128)}, u32[]{:S(2)}, u32[]{:S(2)}) collective-permute-start(f32[640,1024]{1,0:T(8,128)} %get-tuple-element.44), channel_id=1, source_target_pairs={{0,1},{1,0},{2,3},{3,2},{4,5},{5,4},{6,7},{7,6},{8,9},{9,8},{10,11... | collective-permute-start | bytes 7864328 | tf_op jit(solution)/shard_map/ppermute | solution.py:22
  97.9 10.8 %copy-start.2 = (bf16[1152,1024]{1,0:T(8,128)(2,1)S(1)}, bf16[1152,1024]{1,0:T(8,128)(2,1)}, u32[]{:S(2)}) copy-start(bf16[1152,1024]{1,0:T(8,128)(2,1)} %fusion.1.sq_ref) | copy-start | bytes 7077892
  97.9 21.6 %collective-permute-start.23 = (f32[4,40,1024]{2,1,0:T(8,128)S(1)}, f32[4,40,1024]{2,1,0:T(8,128)}, u32[]{:S(2)}, u32[]{:S(2)}) collective-permute-start(f32[4,40,1024]{2,1,0:T(8,128)S(1)} %bitcast.102), channel_id=1, source_target_pairs={{0,6},{2,0},{4,2},{6,4},{1,7},{3,1},{5,3},{7,5},{8,14},{10,8},{12,... | collective-permute-start | bytes 1966088 | tf_op jit(solution)/shard_map/ppermute | solution.py:22
  98.6 38.9 %collective-permute-start.22 = (f32[4,40,1024]{2,1,0:T(8,128)S(1)}, f32[4,40,1024]{2,1,0:T(8,128)}, u32[]{:S(2)}, u32[]{:S(2)}) collective-permute-start(f32[4,40,1024]{2,1,0:T(8,128)S(1)} %bitcast.101), channel_id=1, source_target_pairs={{0,4},{2,6},{4,0},{6,2},{1,5},{3,7},{5,1},{7,3},{8,12},{10,14},{12... | collective-permute-start | bytes 1966088 | tf_op jit(solution)/shard_map/ppermute | solution.py:22
  99.4 38.1 %collective-permute-start.21 = (f32[4,40,1024]{2,1,0:T(8,128)S(1)}, f32[4,40,1024]{2,1,0:T(8,128)}, u32[]{:S(2)}, u32[]{:S(2)}) collective-permute-start(f32[4,40,1024]{2,1,0:T(8,128)S(1)} %bitcast.100), channel_id=1, source_target_pairs={{0,2},{2,4},{4,6},{6,0},{1,3},{3,5},{5,7},{7,1},{8,10},{10,12},{12... | collective-permute-start | bytes 1966088 | tf_op jit(solution)/shard_map/ppermute | solution.py:22
  104.2 38.4 %collective-permute-start.14 = (f32[160,1024]{1,0:T(8,128)}, f32[160,1024]{1,0:T(8,128)S(1)}, u32[]{:S(2)}, u32[]{:S(2)}) collective-permute-start(f32[160,1024]{1,0:T(8,128)} %get-tuple-element.50), channel_id=1, source_target_pairs={{0,8},{8,16},{16,24},{24,0},{1,9},{9,17},{17,25},{25,1},{2,10},{10... | collective-permute-start | bytes 1966088 | tf_op jit(solution)/shard_map/ppermute | solution.py:22
  105.8 9.2 %copy-start.3 = (bf16[1152,1024]{1,0:T(8,128)(2,1)S(1)}, bf16[1152,1024]{1,0:T(8,128)(2,1)}, u32[]{:S(2)}) copy-start(bf16[1152,1024]{1,0:T(8,128)(2,1)} %fusion.sl_ref) | copy-start | bytes 7077892
  105.8 9.2 %copy-start.6 = (bf16[1152,1152]{1,0:T(8,128)(2,1)S(1)}, bf16[1152,1152]{1,0:T(8,128)(2,1)}, u32[]{:S(2)}) copy-start(bf16[1152,1152]{1,0:T(8,128)(2,1)} %wv_ref.1) | copy-start | bytes 7962628
  105.8 36.9 %collective-permute-start.15 = (f32[160,1024]{1,0:T(8,128)}, f32[160,1024]{1,0:T(8,128)}, u32[]{:S(2)}, u32[]{:S(2)}) collective-permute-start(f32[160,1024]{1,0:T(8,128)} %get-tuple-element.51), channel_id=1, source_target_pairs={{0,16},{8,24},{16,0},{24,8},{1,17},{9,25},{17,1},{25,9},{2,18},{10... | collective-permute-start | bytes 1966088 | tf_op jit(solution)/shard_map/ppermute | solution.py:22
  119.5 23.2 %collective-permute-start.16 = (f32[160,1024]{1,0:T(8,128)}, f32[160,1024]{1,0:T(8,128)}, u32[]{:S(2)}, u32[]{:S(2)}) collective-permute-start(f32[160,1024]{1,0:T(8,128)} %get-tuple-element.52), channel_id=1, source_target_pairs={{0,24},{8,0},{16,8},{24,16},{1,25},{9,1},{17,9},{25,17},{2,26},{10... | collective-permute-start | bytes 1966088 | tf_op jit(solution)/shard_map/ppermute | solution.py:22
  137.5 5.2 %copy-start.4 = (f32[160,1024]{1,0:T(8,128)S(1)}, f32[160,1024]{1,0:T(8,128)}, u32[]{:S(2)}) copy-start(f32[160,1024]{1,0:T(8,128)} %get-tuple-element.49) | copy-start | bytes 1966084
  139.4 8.4 %collective-permute-start.24 = (f32[40,1024]{1,0:T(8,128)S(1)}, f32[40,1024]{1,0:T(8,128)S(1)}, u32[]{:S(2)}, u32[]{:S(2)}) collective-permute-start(f32[40,1024]{1,0:T(8,128)S(1)} %get-tuple-element.72), channel_id=1, source_target_pairs={{0,8},{8,16},{16,24},{24,0},{1,9},{9,17},{17,25},{25,1},{2,10},{10... | collective-permute-start | bytes 491528 | tf_op jit(solution)/shard_map/ppermute | solution.py:22
  139.4 12.2 %collective-permute-start.26 = (f32[40,1024]{1,0:T(8,128)S(1)}, f32[40,1024]{1,0:T(8,128)S(1)}, u32[]{:S(2)}, u32[]{:S(2)}) collective-permute-start(f32[40,1024]{1,0:T(8,128)S(1)} %get-tuple-element.73), channel_id=1, source_target_pairs={{0,24},{8,0},{16,8},{24,16},{1,25},{9,1},{17,9},{25,17},{2,26},{10... | collective-permute-start | bytes 491528 | tf_op jit(solution)/shard_map/ppermute | solution.py:22
  142.7 9.0 %collective-permute-start.25 = (f32[40,1024]{1,0:T(8,128)S(1)}, f32[40,1024]{1,0:T(8,128)S(1)}, u32[]{:S(2)}, u32[]{:S(2)}) collective-permute-start(f32[40,1024]{1,0:T(8,128)S(1)} %get-tuple-element.74), channel_id=1, source_target_pairs={{0,16},{8,24},{16,0},{24,8},{1,17},{9,25},{17,1},{25,9},{2,18},{10... | collective-permute-start | bytes 491528 | tf_op jit(solution)/shard_map/ppermute | solution.py:22
  144.3 8.4 %collective-permute-start.17 = (f32[40,1024]{1,0:T(8,128)S(1)}, f32[40,1024]{1,0:T(8,128)S(1)}, u32[]{:S(2)}, u32[]{:S(2)}) collective-permute-start(f32[40,1024]{1,0:T(8,128)S(1)} %get-tuple-element.69), channel_id=1, source_target_pairs={{0,2},{2,4},{4,6},{6,0},{1,3},{3,5},{5,7},{7,1},{8,10},{10,12},{12... | collective-permute-start | bytes 491528 | tf_op jit(solution)/shard_map/ppermute | solution.py:22
  146.2 6.4 %collective-permute-start.19 = (f32[40,1024]{1,0:T(8,128)S(1)}, f32[40,1024]{1,0:T(8,128)S(1)}, u32[]{:S(2)}, u32[]{:S(2)}) collective-permute-start(f32[40,1024]{1,0:T(8,128)S(1)} %get-tuple-element.70), channel_id=1, source_target_pairs={{0,6},{2,0},{4,2},{6,4},{1,7},{3,1},{5,3},{7,5},{8,14},{10,8},{12,... | collective-permute-start | bytes 491528 | tf_op jit(solution)/shard_map/ppermute | solution.py:22
  147.7 7.2 %collective-permute-start.18 = (f32[40,1024]{1,0:T(8,128)S(1)}, f32[40,1024]{1,0:T(8,128)S(1)}, u32[]{:S(2)}, u32[]{:S(2)}) collective-permute-start(f32[40,1024]{1,0:T(8,128)S(1)} %get-tuple-element.71), channel_id=1, source_target_pairs={{0,4},{2,6},{4,0},{6,2},{1,5},{3,7},{5,1},{7,3},{8,12},{10,14},{12... | collective-permute-start | bytes 491528 | tf_op jit(solution)/shard_map/ppermute | solution.py:22
  151.7 15.7 %copy-start.1 = (bf16[1152,1152]{1,0:T(8,128)(2,1)S(1)}, bf16[1152,1152]{1,0:T(8,128)(2,1)}, u32[]{:S(2)}) copy-start(bf16[1152,1152]{1,0:T(8,128)(2,1)} %param.11) | copy-start | bytes 7962628
  152.5 9.3 %copy-start.5 = (bf16[1152,36]{0,1:T(8,128)(2,1)S(1)}, bf16[1152,36]{0,1:T(8,128)(2,1)}, u32[]{:S(2)}) copy-start(bf16[1152,36]{0,1:T(8,128)(2,1)} %param.14) | copy-start | bytes 248836
  155.8 8.0 %collective-permute-start.27 = (f32[9,2304]{1,0:T(8,128)S(1)}, f32[9,2304]{1,0:T(8,128)S(1)}, u32[]{:S(2)}, u32[]{:S(2)}) collective-permute-start(f32[9,2304]{1,0:T(8,128)S(1)} %get-tuple-element.75), channel_id=1, source_target_pairs={{0,32},{32,64},{64,96},{96,0},{1,33},{33,65},{65,97},{97,1},{2,34}... | collective-permute-start | bytes 248840 | tf_op jit(solution)/shard_map/ppermute | solution.py:22
  157.8 6.0 %collective-permute-start.29 = (f32[9,2304]{1,0:T(8,128)S(1)}, f32[9,2304]{1,0:T(8,128)S(1)}, u32[]{:S(2)}, u32[]{:S(2)}) collective-permute-start(f32[9,2304]{1,0:T(8,128)S(1)} %get-tuple-element.76), channel_id=1, source_target_pairs={{0,96},{32,0},{64,32},{96,64},{1,97},{33,1},{65,33},{97,65},{2,98}... | collective-permute-start | bytes 248840 | tf_op jit(solution)/shard_map/ppermute | solution.py:22
  160.0 6.6 %collective-permute-start.28 = (f32[9,2304]{1,0:T(8,128)S(1)}, f32[9,2304]{1,0:T(8,128)S(1)}, u32[]{:S(2)}, u32[]{:S(2)}) collective-permute-start(f32[9,2304]{1,0:T(8,128)S(1)} %get-tuple-element.77), channel_id=1, source_target_pairs={{0,64},{32,96},{64,0},{96,32},{1,65},{33,97},{65,1},{97,33},{2,66}... | collective-permute-start | bytes 248840 | tf_op jit(solution)/shard_map/ppermute | solution.py:22
where the time goes:
time: 168 us; the launch traced here: 167 us
  Pallas kernels  55.8 us (33%)
  starting transfers between devices  40.4 us (24%)
  matrix products  31 us (18%)
  waiting for transfers between devices  18.2 us (11%)
  other arithmetic  14.9 us (9%)
  local copies, waits for them, and re-layouts  6.02 us (4%)
    pallas_call x3, Pallas kernels, call(): pl.pallas_call(body, grid=(steps,), in_specs=specs, out_specs=[pl.BlockSp...  51.7 us
    ppermute x30, starting transfers between devices, shift(): return lax.ppermute(value, axis, [(i, (i + step) % n) for i in range(n)])  40.4 us
    dot_general x10, matrix products, dot(): lax.dot_general(a, b, (((ca,), (cb,)), ((), ())), preferred_element_type=...  31 us
    ppermute x30, waiting for transfers between devices, shift(): return lax.ppermute(value, axis, [(i, (i + step) % n) for i in range(n)])  18.2 us
    pallas_call x1, Pallas kernels, per_device(): pl.pallas_call(split_kernel, out_shape=[cut] * 4, compiler_params=pltpu.C...  4.06 us
    convert_element_type x2, other arithmetic, spread(): return jnp.where(row == col, jnp.tile(part, (HEADS, 1)), 0.0).astype(BF16)  3.98 us
  transfers between devices with their start and end apart: 30, of which 10 were waited for; matrix products, arithmetic and copies ran while one was open for 27% of the time, Pallas kernels for 33%

commit v1 on v0

--- a/solution.py
+++ b/solution.py
@@ -61,6 +61,7 @@
 
 
 STEP = 256
+LONG = 512
 GROUP = 4
 WINDOW = 384
 
@@ -108,13 +109,15 @@
     gain_ref,
     wk_ref,
     wv_ref,
-    sq_ref,
+    wq_ref,
+    lat_ref,
     n_ref,
     v_ref,
     e_ref,
     pack_ref,
+    sq_ref,
     s_all,
-    v_all,
+    n_all,
     acc_ref,
     state_ref,
 ):
@@ -130,19 +133,25 @@
         acc_ref[...] = jnp.zeros_like(acc_ref)
         row = lax.broadcasted_iota(jnp.int32, state_ref.shape, 0)
         state_ref[...] = jnp.where(row == 0, -jnp.inf, 0.0)
+        twice = jnp.concatenate([lat_ref[...], lat_ref[...]], axis=0)
+        query = dot(twice, wq_ref[...]).astype(BF16).astype(F32).T
+        sq_ref[...] = jnp.zeros_like(sq_ref)
+        head_row = lax.broadcasted_iota(jnp.int32, (2 * width, 2 * nlat), 0) // width
+        head_col = lax.broadcasted_iota(jnp.int32, (2 * width, 2 * nlat), 1) // nlat
+        for t in range(HEADS // 2):
+            feat, cols = slice(2 * width * t, 2 * width * (t + 1)), slice(2 * nlat * t, 2 * nlat * (t + 1))
+            sq_ref[feat, cols] = jnp.where(head_row == head_col, query[feat, :], 0.0).astype(BF16)
 
     @pl.when(step < steps)
     def _():
         x = x_ref[...].astype(F32)
         centred = x - jnp.mean(x, axis=-1, keepdims=True)
         rstd = lax.rsqrt(jnp.mean(centred * centred, axis=-1, keepdims=True) + 1e-06)
-        normed = centred * rstd * gain_ref[...].astype(F32)
+        normed = centred * rstd * gain_ref[...].astype(F32)[None, :]
         normed = jnp.where(valid(x.shape[1]), normed, 0.0).astype(BF16)
         n_ref[...] = normed
         keys = dot(normed, wk_ref[...]).astype(BF16)
-        values = dot(normed, wv_ref[...]).astype(BF16)
-        v_ref[...] = values
-        v_all[here, :] = values
+        n_all[here, :] = normed
         for j in range(HEADS // GROUP):
             feat, cols = group(j, width, nlat)
             s = dot(keys[:, feat], sq_ref[feat, cols]) * (1.0 / width**0.5)
@@ -154,13 +163,15 @@
 
     @pl.when(step >= steps)
     def _():
+        values = dot(n_all[here, :], wv_ref[...]).astype(BF16)
+        v_ref[...] = values
         for j in range(HEADS // GROUP):
             feat, cols = group(j, width, nlat)
             e = jnp.exp(s_all[here, cols] - state_ref[0:1, cols])
             state_ref[1:2, cols] += jnp.sum(e, axis=0, keepdims=True)
             e = e.astype(BF16)
             e_ref[:, cols] = e
-            acc_ref[j] += dot(v_all[here, feat], e, 0, 0)
+            acc_ref[j] += dot(values[:, feat], e, 0, 0)
 
     @pl.when(step == 2 * steps - 1)
     def _():
@@ -201,7 +212,7 @@
     centred = x - jnp.mean(x, axis=-1, keepdims=True)
     rstd = lax.rsqrt(jnp.mean(centred * centred, axis=-1, keepdims=True) + 1e-06)
     xhat = centred * rstd
-    dxhat = normed_cot * gain_ref[...].astype(F32)
+    dxhat = normed_cot * gain_ref[...].astype(F32)[None, :]
     mean = jnp.mean(dxhat, axis=-1, keepdims=True)
     slope = jnp.mean(dxhat * xhat, axis=-1, keepdims=True)
     out_ref[...] = ((dxhat - mean - xhat * slope) * rstd).astype(BF16)
@@ -225,7 +236,6 @@
     steps = -(-rows // STEP)
     padded = steps * STEP
     half_rows = 16 * CHUNK
-    gain_row = gain.reshape(1, d)
 
     def own_half(value):
         return lax.dynamic_slice_in_dim(value, core * (cols // 2), cols // 2, 1)
@@ -238,9 +248,7 @@
     lc = by_head(dot(w_out, cotangent[0], 1, 1), width)
     lc = own_half(lc + shift(lc, "c", 1))
 
-    query = dot(w_query, latent_rows, 0, 1).astype(BF16)
-    spread_q = spread(by_head(query, width).astype(F32), width)
-    frames_1, spread_1 = lax.optimization_barrier((frames, spread_q, lc))[:2]
+    frames_1 = after(frames, lc)
     lc_y = [shift(lc, "y", k) for k in (1, 2, 3)]
 
     def first(i):
@@ -249,21 +257,23 @@
     def second(i):
         return (jnp.maximum(i - steps, 0), 0)
 
-    normed, values, expo, pack = call(
+    normed, values, expo, pack, spread_q = call(
         functools.partial(softmax_kernel, rows, width, nlat),
         2 * steps,
         [
             (frames_1, (STEP, d), first),
-            (gain_row, (1, d), whole_block),
+            (gain, (d,), lambda i: (0,)),
             (w_key, (d, d), whole_block),
             (w_value, (d, d), whole_block),
-            (spread_1, (d, cols), whole_block),
+            (w_query, (d, d), whole_block),
+            (latent_rows, (nlat, d), whole_block),
         ],
         [
             ((padded, d), BF16, (STEP, d), first),
-            ((padded, d), BF16, (STEP, d), first),
+            ((padded, d), BF16, (STEP, d), second),
             ((padded, cols), BF16, (STEP, cols), second),
             ((width + 8, cols), F32, (width + 8, cols), whole_block),
+            ((d, cols), BF16, (d, cols), whole_block),
         ],
         [
             pltpu.VMEM((padded, cols), F32),
@@ -287,7 +297,8 @@
     halves = [half] + [shift(half, "x", k) for k in (1, 2, 3)]
     tops = [h[width + 8 : width + 10].reshape(1, cols) for h in halves]
     top3 = jnp.maximum(jnp.maximum(tops[0], tops[1]), jnp.maximum(tops[2], tops[3]))
-    halves[0] = after(halves[0], turned)
+    q_key = dot(after(w_key, turned), spread_q).astype(BF16)
+    halves[0] = after(halves[0], q_key)
     half = merge([h[: width + 8] for h in halves], width)
     lc = sum(h[width + 16 :] for h in halves)
     lc = whole(lc, shift(lc, "c", 1))
@@ -307,16 +318,16 @@
 
     dscore, w, w_send = call(
         functools.partial(grad_kernel, width, nlat),
-        steps,
-        [
-            (values, (STEP, d), row_block),
+        padded // LONG,
+        [
+            (values, (LONG, d), row_block),
             (spread_lc, (d, cols), whole_block),
-            (expo, (STEP, cols), row_block),
+            (expo, (LONG, cols), row_block),
             (state, (8, cols), whole_block),
-            (turned, (2 * half_rows, STEP), col_block),
-        ],
-        [
-            ((padded, cols), BF16, (STEP, cols), row_block),
+            (turned, (2 * half_rows, LONG), col_block),
+        ],
+        [
+            ((padded, cols), BF16, (LONG, cols), row_block),
             ((half_rows, cols), F32, (half_rows, cols), whole_block),
             ((half_rows, cols), F32, (half_rows, cols), whole_block),
         ],
@@ -341,7 +352,6 @@
     )(w, w_got)
 
 
-    q_key = dot(after(w_key, parts[0]), spread_q).astype(BF16)
     q_value = dot(after(w_value, parts[0]), spread_lc).astype(BF16)
     patch_grad = call(
         back_kernel,
@@ -353,7 +363,7 @@
             (q_value, (d, cols), whole_block),
             (state, (8, cols), whole_block),
             (frames, (STEP, d), row_block),
-            (gain_row, (1, d), whole_block),
+            (gain, (d,), lambda i: (0,)),
         ],
         [((rows, d), BF16, (STEP, d), row_block)],
         [pltpu.VMEM((d, cols), BF16)],

time: 168 us -> 159 us (0.946)
  other arithmetic: 14.9 us -> 11.3 us
  local copies, waits for them, and re-layouts: 6.02 us -> 3.5 us
  matrix products: 31 us -> 28.6 us
  waiting for transfers between devices: 18.2 us -> 16.5 us
    dot_general x10 -> x9, matrix products: 31 us -> 28.6 us  [dot(): lax.dot_general(a, b, (((ca,), (cb,)), ((), ())), preferred_element_type=...]
    convert_element_type x2 -> x1, other arithmetic: 3.98 us -> 1.95 us  [spread(): return jnp.where(row == col, jnp.tile(part, (HEADS, 1)), 0.0).astype(BF16)]
  transfers between devices with their start and end apart: 30 -> 30, of which waited for: 10 -> 11; matrix products, arithmetic and copies ran while one was open for 27% -> 23% of each run, Pallas kernels for 33% -> 36%
where the time goes in v1:
time: 159 us; the launch traced here: 158 us
  Pallas kernels  56.1 us (35%)
  starting transfers between devices  40.6 us (26%)
  matrix products  28.6 us (18%)
  waiting for transfers between devices  16.5 us (10%)
  other arithmetic  11.3 us (7%)
  local copies, waits for them, and re-layouts  3.5 us (2%)
    pallas_call x3, Pallas kernels, call(): pl.pallas_call(body, grid=(steps,), in_specs=specs, out_specs=[pl.BlockSp...  51.8 us
    ppermute x30, starting transfers between devices, shift(): return lax.ppermute(value, axis, [(i, (i + step) % n) for i in range(n)])  40.6 us
    dot_general x9, matrix products, dot(): lax.dot_general(a, b, (((ca,), (cb,)), ((), ())), preferred_element_type=...  28.6 us
    ppermute x30, waiting for transfers between devices, shift(): return lax.ppermute(value, axis, [(i, (i + step) % n) for i in range(n)])  16.5 us
    pallas_call x1, Pallas kernels, per_device(): pl.pallas_call(split_kernel, out_shape=[cut] * 4, compiler_params=pltpu.C...  4.26 us
  transfers between devices with their start and end apart: 30, of which 11 were waited for; matrix products, arithmetic and copies ran while one was open for 23% of the time, Pallas kernels for 36%

profile of v1, /device:TPU:0, one launch (start us, length us, event | category | flops | bytes accessed | tf_op | source)
XLA Modules:
  0.0 157.6 jit_solution(1134394605682609082)
XLA Ops:
  0.6 1.2 dot_general.29
  1.8 0.3 fusion.20
  2.5 1.4 collective-permute-done
  4.0 3.4 %collective-permute-start.2 = (f32[72,512]{1,0:T(8,128)S(1)}, f32[72,512]{1,0:T(8,128)S(1)}, u32[]{:S(2)}, u32[]{:S(2)}) collective-permute-start(f32[72,512]{1,0:T(8,128)S(1)} %dynamic-slice_add_fusion), channel_id=1, source_target_pairs={{0,16},{8,24},{16,0},{24,8},{1,17},{9,25},{17,1},{25,9},{2,18},{10... | collective-permute-start | bytes 442376 | tf_op jit(solution)/shard_map/ppermute | solution.py:22
  7.3 0.7 collective-permute-start.1
  8.0 2.6 %collective-permute-start.3 = (f32[72,512]{1,0:T(8,128)S(1)}, f32[72,512]{1,0:T(8,128)S(1)}, u32[]{:S(2)}, u32[]{:S(2)}) collective-permute-start(f32[72,512]{1,0:T(8,128)S(1)} %dynamic-slice_add_fusion), channel_id=1, source_target_pairs={{0,24},{8,0},{16,8},{24,16},{1,25},{9,1},{17,9},{25,17},{2,26},{10... | collective-permute-start | bytes 442376 | tf_op jit(solution)/shard_map/ppermute | solution.py:22
  10.6 24.4 %softmax.1 = (bf16[1536,1152]{1,0:T(8,128)(2,1)}, bf16[1536,1152]{1,0:T(8,128)(2,1)}, bf16[1536,1024]{1,0:T(8,128)(2,1)}, f32[80,1024]{1,0:T(8,128)}, bf16[1152,1024]{1,0:T(8,128)(2,1)}) custom-call(bf16[1458,1152]{1,0:T(8,128)(2,1)} %bitcast.119, bf16[1152]{0:T(1024)(128)(2,1)} %gain_ref.3, bf16[1152,1152]{1,0:T(8,128)(2,1)} %wk_ref.1, ...), custom_call_target="tpu_custom_call" | custom-call | flops 10569646080 | bytes 21430272 | tf_op jit(solution)/shard_map/softmax/pallas_call | solution.py:79
  35.3 1.7 %collective-permute-done.4 = f32[80,1024]{1,0:T(8,128)S(1)} collective-permute-done((f32[80,1024]{1,0:T(8,128)}, f32[80,1024]{1,0:T(8,128)S(1)}, u32[]{:S(2)}, u32[]{:S(2)}) %collective-permute-start.4) | collective-permute-done | bytes 327712 | tf_op jit(solution)/shard_map/ppermute | solution.py:22
  37.0 0.8 subtract_exponential_fusion.5
  38.0 0.5 broadcast.417
  38.5 0.7 subtract_exponential_fusion.4
  39.3 1.0 fusion.19
  40.3 2.8 %collective-permute-start.7 = (f32[160,512]{1,0:T(8,128)S(1)}, f32[160,512]{1,0:T(8,128)S(1)}, u32[]{:S(2)}, u32[]{:S(2)}) collective-permute-start(f32[160,512]{1,0:T(8,128)S(1)} %pad_maximum_fusion), channel_id=1, source_target_pairs={{0,6},{2,0},{4,2},{6,4},{1,7},{3,1},{5,3},{7,5},{8,14},{10,8},{12,... | collective-permute-start | bytes 983048 | tf_op jit(solution)/shard_map/ppermute | solution.py:22
  43.1 0.8 collective-permute-start.6
  43.9 0.9 collective-permute-start.5
  44.8 7.8 %convolution_convert_fusion.t_ref = bf16[1280,1536]{1,0:T(8,128)(2,1)S(1)} fusion(bf16[1536,1152]{1,0:T(8,128)(2,1)} %get-tuple-element.34, s32[1280]{0:T(1024)S(1)} %fusion.44), kind=kOutput, calls=%fused_computation | convolution fusion | flops 4533288960 | bytes 7476224 | tf_op jit(solution)/shard_map/dot_general | solution.py:17
  52.7 4.4 %convolution_convert_fusion.2.qk_ref = bf16[1152,1024]{1,0:T(8,128)(2,1)} fusion(bf16[1152,1152]{1,0:T(8,128)(2,1)S(1)} %copy-done.7, bf16[1152,1024]{1,0:T(8,128)(2,1)S(1)} %copy-done.3), kind=kOutput, calls=%fused_computation.6 | convolution fusion | flops 2719088640 | bytes 7372800 | tf_op jit(solution)/shard_map/dot_general | solution.py:17
  57.1 0.4 collective-permute-done.7
  57.4 3.7 %collective-permute-done.5 = f32[160,512]{1,0:T(8,128)S(1)} collective-permute-done((f32[160,512]{1,0:T(8,128)S(1)}, f32[160,512]{1,0:T(8,128)S(1)}, u32[]{:S(2)}, u32[]{:S(2)}) %collective-permute-start.5) | collective-permute-done | bytes 327712 | tf_op jit(solution)/shard_map/ppermute | solution.py:22
  61.4 1.5 collective-permute-start.10
  62.9 0.5 collective-permute-start.9
  63.3 3.7 %fusion.2 = f32[640,1024]{1,0:T(8,128)} fusion(bf16[1536,1024]{1,0:T(8,128)(2,1)S(1)} %copy-done.9, bf16[1280,1536]{1,0:T(8,128)(2,1)S(1)} %convolution_convert_fusion.t_ref), kind=kOutput, calls=%fused_computation.9 | convolution fusion | flops 2013265920 | bytes 7733248 | tf_op jit(solution)/shard_map/dot_general | solution.py:17
  67.1 0.6 collective-permute-start.8
  67.7 3.7 %fusion.4 = f32[640,1024]{1,0:T(8,128)} fusion(bf16[1536,1024]{1,0:T(8,128)(2,1)S(1)} %copy-done.9, bf16[1280,1536]{1,0:T(8,128)(2,1)S(1)} %convolution_convert_fusion.t_ref), kind=kOutput, calls=%fused_computation.11 | convolution fusion | flops 2013265920 | bytes 7733248 | tf_op jit(solution)/shard_map/dot_general | solution.py:17
  71.4 0.4 collective-permute-done.8
  71.8 1.9 %fusion.sl_ref = bf16[1152,1024]{1,0:T(8,128)(2,1)} fusion(f32[72,1024]{1,0:T(8,128)S(1)} %maximum_select_fusion.1, s32[1024]{0:T(1024)S(1)} %get-tuple-element.100, s32[1024]{0:T(1024)S(1)} %get-tuple-element.101, s32[1152]{0:T(1024)S(1)} %get-tuple-element.98, s32[1152]{0:T(1024)S(1)} %get-tuple-element.99, pred[1152]{0:T(1024)(128)(4,1)S(1)} %fusion.66, ...), kind=kLoop, calls=%fused_computation.3 | loop fusion | flops 4718592 | bytes 2673792 | tf_op jit(solution)/shard_map/convert_element_type | solution.py:30
  73.9 0.5 collective-permute-start.12
  74.4 1.0 collective-permute-done.12
  75.4 0.8 broadcast_multiply_fusion
  76.3 0.7 maximum_maximum_fusion.state_ref
  77.0 11.7 %gradient.1 = (bf16[1536,1024]{1,0:T(8,128)(2,1)}, f32[640,1024]{1,0:T(8,128)}, f32[640,1024]{1,0:T(8,128)}) custom-call(bf16[1536,1152]{1,0:T(8,128)(2,1)} %get-tuple-element.42.v_ref, bf16[1152,1024]{1,0:T(8,128)(2,1)} %fusion.sl_ref, bf16[1536,1024]{1,0:T(8,128)(2,1)} %get-tuple-element.40.e_ref, f32[8,1024]{1,0:T(8,128)} %maximum_maximum_fusion.state_ref, ...), custom_call_target="tpu_custom_call" | custom-call | flops 5234491392 | bytes 21233664 | tf_op jit(solution)/shard_map/gradient/pallas_call | solution.py:79
  88.7 0.4 collective-permute-start.13
  89.3 0.4 copy.15
  89.7 0.3 convert_element_type.40
  90.0 2.4 %multiply_add_fusion = f32[640,1024]{1,0:T(8,128)S(1)} fusion(f32[640,1024]{1,0:T(8,128)S(1)} %collective-permute-done.20, f32[640,1024]{1,0:T(8,128)} %fusion.4, f32[1024]{0:T(1024)S(1)} %bitcast.103, f32[1024]{0:T(1024)S(1)} %bitcast.101), kind=kLoop, calls=%fused_computation.8 | loop fusion | flops 1966080 | bytes 7872512 | tf_op jit(solution)/shard_map/add | solution.py:340
  92.4 0.3 fusion.72
  92.7 0.7 collective-permute-start.23
  93.4 0.8 collective-permute-start.22
  94.2 0.8 collective-permute-start.21
  95.0 4.3 %split.1 = (f32[160,1024]{1,0:T(8,128)}, f32[160,1024]{1,0:T(8,128)}, f32[160,1024]{1,0:T(8,128)}, f32[160,1024]{1,0:T(8,128)}) custom-call(f32[640,1024]{1,0:T(8,128)} %get-tuple-element.44.keep_ref, f32[640,1024]{1,0:T(8,128)} %collective-permute-done.13.got_ref), custom_call_target="tpu_custom_call" | custom-call | flops 655360 | bytes 7864320 | tf_op jit(solution)/shard_map/split/pallas_call | solution.py:344
  99.3 1.6 collective-permute-start.14
  100.8 2.6 %collective-permute-start.15 = (f32[160,1024]{1,0:T(8,128)}, f32[160,1024]{1,0:T(8,128)S(1)}, u32[]{:S(2)}, u32[]{:S(2)}) collective-permute-start(f32[160,1024]{1,0:T(8,128)} %get-tuple-element.51), channel_id=1, source_target_pairs={{0,16},{8,24},{16,0},{24,8},{1,17},{9,25},{17,1},{25,9},{2,18},{10... | collective-permute-start | bytes 1966088 | tf_op jit(solution)/shard_map/ppermute | solution.py:22
  103.5 6.3 %convolution_convert_fusion.1.qv_ref = bf16[1152,1024]{1,0:T(8,128)(2,1)} fusion(bf16[1152,1152]{1,0:T(8,128)(2,1)} %wv_ref.1, bf16[1152,1024]{1,0:T(8,128)(2,1)S(1)} %copy-done.2), kind=kOutput, calls=%fused_computation.5 | convolution fusion | flops 2719088640 | bytes 7372800 | tf_op jit(solution)/shard_map/dot_general | solution.py:17
  109.8 0.6 collective-permute-done.23
  110.3 2.7 %collective-permute-start.16 = (f32[160,1024]{1,0:T(8,128)}, f32[160,1024]{1,0:T(8,128)S(1)}, u32[]{:S(2)}, u32[]{:S(2)}) collective-permute-start(f32[160,1024]{1,0:T(8,128)} %get-tuple-element.52), channel_id=1, source_target_pairs={{0,24},{8,0},{16,8},{24,16},{1,25},{9,1},{17,9},{25,17},{2,26},{10... | collective-permute-start | bytes 1966088 | tf_op jit(solution)/shard_map/ppermute | solution.py:22
  113.1 15.7 %back.1 = bf16[1458,1152]{1,0:T(8,128)(2,1)} custom-call(bf16[1536,1024]{1,0:T(8,128)(2,1)} %get-tuple-element.47.d_ref, bf16[1536,1024]{1,0:T(8,128)(2,1)} %get-tuple-element.40.e_ref, bf16[1152,1024]{1,0:T(8,128)(2,1)} %convolution_convert_fusion.2.qk_ref, bf16[1152,1024]{1,0:T(8,128)(2,1)} %convolution_convert_fusion.1.qv_ref, ...), custom_call_target="tpu_custom_call" | custom-call | flops 7247757312 | bytes 18087936 | tf_op jit(solution)/shard_map/back/pallas_call | solution.py:79
  128.8 1.5 add_multiply_fusion
  130.3 3.2 %collective-permute-start.26 = (f32[40,1024]{1,0:T(8,128)S(1)}, f32[40,1024]{1,0:T(8,128)S(1)}, u32[]{:S(2)}, u32[]{:S(2)}) collective-permute-start(f32[40,1024]{1,0:T(8,128)S(1)} %get-tuple-element.73), channel_id=1, source_target_pairs={{0,24},{8,0},{16,8},{24,16},{1,25},{9,1},{17,9},{25,17},{2,26},{10... | collective-permute-start | bytes 491528 | tf_op jit(solution)/shard_map/ppermute | solution.py:22
  133.6 0.2 collective-permute-start.25
  133.8 0.2 add_add_fusion
  134.1 2.6 %collective-permute-start.17 = (f32[40,1024]{1,0:T(8,128)S(1)}, f32[40,1024]{1,0:T(8,128)S(1)}, u32[]{:S(2)}, u32[]{:S(2)}) collective-permute-start(f32[40,1024]{1,0:T(8,128)S(1)} %get-tuple-element.69), channel_id=1, source_target_pairs={{0,2},{2,4},{4,6},{6,0},{1,3},{3,5},{5,7},{7,1},{8,10},{10,12},{12... | collective-permute-start | bytes 491528 | tf_op jit(solution)/shard_map/ppermute | solution.py:22
  136.7 1.0 collective-permute-start.19
  137.7 0.7 collective-permute-done.24
  138.4 3.4 %collective-permute-start.18 = (f32[40,1024]{1,0:T(8,128)S(1)}, f32[40,1024]{1,0:T(8,128)S(1)}, u32[]{:S(2)}, u32[]{:S(2)}) collective-permute-start(f32[40,1024]{1,0:T(8,128)S(1)} %get-tuple-element.71), channel_id=1, source_target_pairs={{0,4},{2,6},{4,0},{6,2},{1,5},{3,7},{5,1},{7,3},{8,12},{10,14},{12... | collective-permute-start | bytes 491528 | tf_op jit(solution)/shard_map/ppermute | solution.py:22
  141.8 0.8 fusion.31
  142.7 2.5 %collective-permute-done.18 = f32[40,1024]{1,0:T(8,128)S(1)} collective-permute-done((f32[40,1024]{1,0:T(8,128)S(1)}, f32[40,1024]{1,0:T(8,128)S(1)}, u32[]{:S(2)}, u32[]{:S(2)}) %collective-permute-start.18) | collective-permute-done | bytes 163872 | tf_op jit(solution)/shard_map/ppermute | solution.py:22
  145.2 0.8 fusion.29
  146.0 2.0 %collective-permute-start.27 = (f32[9,2304]{1,0:T(8,128)S(1)}, f32[9,2304]{1,0:T(8,128)S(1)}, u32[]{:S(2)}, u32[]{:S(2)}) collective-permute-start(f32[9,2304]{1,0:T(8,128)S(1)} %get-tuple-element.75), channel_id=1, source_target_pairs={{0,32},{32,64},{64,96},{96,0},{1,33},{33,65},{65,97},{97,1},{2,34}... | collective-permute-start | bytes 248840 | tf_op jit(solution)/shard_map/ppermute | solution.py:22
  148.0 2.2 %collective-permute-start.29 = (f32[9,2304]{1,0:T(8,128)S(1)}, f32[9,2304]{1,0:T(8,128)S(1)}, u32[]{:S(2)}, u32[]{:S(2)}) collective-permute-start(f32[9,2304]{1,0:T(8,128)S(1)} %get-tuple-element.76), channel_id=1, source_target_pairs={{0,96},{32,0},{64,32},{96,64},{1,97},{33,1},{65,33},{97,65},{2,98}... | collective-permute-start | bytes 248840 | tf_op jit(solution)/shard_map/ppermute | solution.py:22
  150.2 1.8 %collective-permute-start.28 = (f32[9,2304]{1,0:T(8,128)S(1)}, f32[9,2304]{1,0:T(8,128)S(1)}, u32[]{:S(2)}, u32[]{:S(2)}) collective-permute-start(f32[9,2304]{1,0:T(8,128)S(1)} %get-tuple-element.77), channel_id=1, source_target_pairs={{0,64},{32,96},{64,0},{96,32},{1,65},{33,97},{65,1},{97,33},{2,66}... | collective-permute-start | bytes 248840 | tf_op jit(solution)/shard_map/ppermute | solution.py:22
  152.0 0.8 fusion.6
  152.8 1.0 collective-permute-done.27
  153.8 3.0 %collective-permute-done.28 = f32[9,2304]{1,0:T(8,128)S(1)} collective-permute-done((f32[9,2304]{1,0:T(8,128)S(1)}, f32[9,2304]{1,0:T(8,128)S(1)}, u32[]{:S(2)}, u32[]{:S(2)}) %collective-permute-start.28) | collective-permute-done | bytes 82976 | tf_op jit(solution)/shard_map/ppermute | solution.py:22
  156.9 0.7 fusion.26
  (85 shorter events, 2.0 us)
Async XLA Ops:
  0.6 1.2 copy-start
  2.3 1.7 %collective-permute-start = (f32[72,1024]{1,0:T(8,128)S(1)}, f32[72,1024]{1,0:T(8,128)S(1)}, u32[]{:S(2)}, u32[]{:S(2)}) collective-permute-start(f32[72,1024]{1,0:T(8,128)S(1)} %copy.16), channel_id=1, source_target_pairs={{0,1},{1,0},{2,3},{3,2},{4,5},{5,4},{6,7},{7,6},{8,9},{9,8},{10,11... | collective-permute-start | bytes 884744 | tf_op jit(solution)/shard_map/ppermute | solution.py:22
  4.0 31.0 %collective-permute-start.2 = (f32[72,512]{1,0:T(8,128)S(1)}, f32[72,512]{1,0:T(8,128)S(1)}, u32[]{:S(2)}, u32[]{:S(2)}) collective-permute-start(f32[72,512]{1,0:T(8,128)S(1)} %dynamic-slice_add_fusion), channel_id=1, source_target_pairs={{0,16},{8,24},{16,0},{24,8},{1,17},{9,25},{17,1},{25,9},{2,18},{10... | collective-permute-start | bytes 442376 | tf_op jit(solution)/shard_map/ppermute | solution.py:22
  7.3 27.7 %collective-permute-start.1 = (f32[72,512]{1,0:T(8,128)S(1)}, f32[72,512]{1,0:T(8,128)S(1)}, u32[]{:S(2)}, u32[]{:S(2)}) collective-permute-start(f32[72,512]{1,0:T(8,128)S(1)} %dynamic-slice_add_fusion), channel_id=1, source_target_pairs={{0,8},{8,16},{16,24},{24,0},{1,9},{9,17},{17,25},{25,1},{2,10},{10... | collective-permute-start | bytes 442376 | tf_op jit(solution)/shard_map/ppermute | solution.py:22
  8.0 27.0 %collective-permute-start.3 = (f32[72,512]{1,0:T(8,128)S(1)}, f32[72,512]{1,0:T(8,128)S(1)}, u32[]{:S(2)}, u32[]{:S(2)}) collective-permute-start(f32[72,512]{1,0:T(8,128)S(1)} %dynamic-slice_add_fusion), channel_id=1, source_target_pairs={{0,24},{8,0},{16,8},{24,16},{1,25},{9,1},{17,9},{25,17},{2,26},{10... | collective-permute-start | bytes 442376 | tf_op jit(solution)/shard_map/ppermute | solution.py:22
  35.1 1.9 %collective-permute-start.4 = (f32[80,1024]{1,0:T(8,128)}, f32[80,1024]{1,0:T(8,128)S(1)}, u32[]{:S(2)}, u32[]{:S(2)}) collective-permute-start(f32[80,1024]{1,0:T(8,128)} %get-tuple-element.32), channel_id=1, source_target_pairs={{0,1},{1,0},{2,3},{3,2},{4,5},{5,4},{6,7},{7,6},{8,9},{9,8},{10,11... | collective-permute-start | bytes 983048 | tf_op jit(solution)/shard_map/ppermute | solution.py:22
  40.3 17.1 %collective-permute-start.7 = (f32[160,512]{1,0:T(8,128)S(1)}, f32[160,512]{1,0:T(8,128)S(1)}, u32[]{:S(2)}, u32[]{:S(2)}) collective-permute-start(f32[160,512]{1,0:T(8,128)S(1)} %pad_maximum_fusion), channel_id=1, source_target_pairs={{0,6},{2,0},{4,2},{6,4},{1,7},{3,1},{5,3},{7,5},{8,14},{10,8},{12,... | collective-permute-start | bytes 983048 | tf_op jit(solution)/shard_map/ppermute | solution.py:22
  43.1 14.3 %collective-permute-start.6 = (f32[160,512]{1,0:T(8,128)S(1)}, f32[160,512]{1,0:T(8,128)S(1)}, u32[]{:S(2)}, u32[]{:S(2)}) collective-permute-start(f32[160,512]{1,0:T(8,128)S(1)} %pad_maximum_fusion), channel_id=1, source_target_pairs={{0,4},{2,6},{4,0},{6,2},{1,5},{3,7},{5,1},{7,3},{8,12},{10,14},{12... | collective-permute-start | bytes 983048 | tf_op jit(solution)/shard_map/ppermute | solution.py:22
  43.9 17.2 %collective-permute-start.5 = (f32[160,512]{1,0:T(8,128)S(1)}, f32[160,512]{1,0:T(8,128)S(1)}, u32[]{:S(2)}, u32[]{:S(2)}) collective-permute-start(f32[160,512]{1,0:T(8,128)S(1)} %pad_maximum_fusion), channel_id=1, source_target_pairs={{0,2},{2,4},{4,6},{6,0},{1,3},{3,5},{5,7},{7,1},{8,10},{10,12},{12... | collective-permute-start | bytes 983048 | tf_op jit(solution)/shard_map/ppermute | solution.py:22
  44.8 7.8 %copy-start.3 = (bf16[1152,1024]{1,0:T(8,128)(2,1)S(1)}, bf16[1152,1024]{1,0:T(8,128)(2,1)}, u32[]{:S(2)}) copy-start(bf16[1152,1024]{1,0:T(8,128)(2,1)} %get-tuple-element.36) | copy-start | bytes 7077892
  44.8 7.8 %copy-start.7 = (bf16[1152,1152]{1,0:T(8,128)(2,1)S(1)}, bf16[1152,1152]{1,0:T(8,128)(2,1)}, u32[]{:S(2)}) copy-start(bf16[1152,1152]{1,0:T(8,128)(2,1)} %wk_ref.1) | copy-start | bytes 7962628
  52.6 15.1 %copy-start.8 = (bf16[1280,1536]{1,0:T(8,128)(2,1)}, bf16[1280,1536]{1,0:T(8,128)(2,1)S(1)}, u32[]{:S(2)}) copy-start(bf16[1280,1536]{1,0:T(8,128)(2,1)S(1)} %convolution_convert_fusion.t_ref) | copy-start | bytes 11796484
  52.7 10.7 %copy-start.9 = (bf16[1536,1024]{1,0:T(8,128)(2,1)S(1)}, bf16[1536,1024]{1,0:T(8,128)(2,1)}, u32[]{:S(2)}) copy-start(bf16[1536,1024]{1,0:T(8,128)(2,1)} %get-tuple-element.40.e_ref) | copy-start | bytes 9437188
  61.2 12.5 %collective-permute-start.11 = (f32[80,512]{1,0:T(8,128)S(1)}, f32[80,512]{1,0:T(8,128)S(1)}, u32[]{:S(2)}, u32[]{:S(2)}) collective-permute-start(f32[80,512]{1,0:T(8,128)S(1)} %fusion.15), channel_id=1, source_target_pairs={{0,24},{8,0},{16,8},{24,16},{1,25},{9,1},{17,9},{25,17},{2,26},{10... | collective-permute-start | bytes 491528 | tf_op jit(solution)/shard_map/ppermute | solution.py:22
  61.4 12.4 %collective-permute-start.10 = (f32[80,512]{1,0:T(8,128)S(1)}, f32[80,512]{1,0:T(8,128)S(1)}, u32[]{:S(2)}, u32[]{:S(2)}) collective-permute-start(f32[80,512]{1,0:T(8,128)S(1)} %fusion.15), channel_id=1, source_target_pairs={{0,16},{8,24},{16,0},{24,8},{1,17},{9,25},{17,1},{25,9},{2,18},{10... | collective-permute-start | bytes 491528 | tf_op jit(solution)/shard_map/ppermute | solution.py:22
  62.9 10.9 %collective-permute-start.9 = (f32[80,512]{1,0:T(8,128)S(1)}, f32[80,512]{1,0:T(8,128)S(1)}, u32[]{:S(2)}, u32[]{:S(2)}) collective-permute-start(f32[80,512]{1,0:T(8,128)S(1)} %fusion.15), channel_id=1, source_target_pairs={{0,8},{8,16},{16,24},{24,0},{1,9},{9,17},{17,25},{25,1},{2,10},{10... | collective-permute-start | bytes 491528 | tf_op jit(solution)/shard_map/ppermute | solution.py:22
  67.1 23.0 %collective-permute-start.20 = (f32[640,1024]{1,0:T(8,128)}, f32[640,1024]{1,0:T(8,128)S(1)}, u32[]{:S(2)}, u32[]{:S(2)}) collective-permute-start(f32[640,1024]{1,0:T(8,128)} %fusion.2), channel_id=1, source_target_pairs={{0,1},{1,0},{2,3},{3,2},{4,5},{5,4},{6,7},{7,6},{8,9},{9,8},{10,11... | collective-permute-start | bytes 7864328 | tf_op jit(solution)/shard_map/ppermute | solution.py:22
  67.1 4.7 %collective-permute-start.8 = (f32[72,512]{1,0:T(8,128)S(1)}, f32[72,512]{1,0:T(8,128)S(1)}, u32[]{:S(2)}, u32[]{:S(2)}) collective-permute-start(f32[72,512]{1,0:T(8,128)S(1)} %slice_add_fusion.1), channel_id=1, source_target_pairs={{0,1},{1,0},{2,3},{3,2},{4,5},{5,4},{6,7},{7,6},{8,9},{9,8},{10,11... | collective-permute-start | bytes 442376 | tf_op jit(solution)/shard_map/ppermute | solution.py:22
  73.9 1.5 collective-permute-start.12
  88.7 6.3 %collective-permute-start.13 = (f32[640,1024]{1,0:T(8,128)}, f32[640,1024]{1,0:T(8,128)}, u32[]{:S(2)}, u32[]{:S(2)}) collective-permute-start(f32[640,1024]{1,0:T(8,128)} %get-tuple-element.45), channel_id=1, source_target_pairs={{0,1},{1,0},{2,3},{3,2},{4,5},{5,4},{6,7},{7,6},{8,9},{9,8},{10,11... | collective-permute-start | bytes 7864328 | tf_op jit(solution)/shard_map/ppermute | solution.py:22
  92.7 17.6 %collective-permute-start.23 = (f32[4,40,1024]{2,1,0:T(8,128)S(1)}, f32[4,40,1024]{2,1,0:T(8,128)S(1)}, u32[]{:S(2)}, u32[]{:S(2)}) collective-permute-start(f32[4,40,1024]{2,1,0:T(8,128)S(1)} %bitcast.91), channel_id=1, source_target_pairs={{0,6},{2,0},{4,2},{6,4},{1,7},{3,1},{5,3},{7,5},{8,14},{10,8},{12,... | collective-permute-start | bytes 1966088 | tf_op jit(solution)/shard_map/ppermute | solution.py:22
  93.4 35.4 %collective-permute-start.22 = (f32[4,40,1024]{2,1,0:T(8,128)S(1)}, f32[4,40,1024]{2,1,0:T(8,128)S(1)}, u32[]{:S(2)}, u32[]{:S(2)}) collective-permute-start(f32[4,40,1024]{2,1,0:T(8,128)S(1)} %bitcast.90), channel_id=1, source_target_pairs={{0,4},{2,6},{4,0},{6,2},{1,5},{3,7},{5,1},{7,3},{8,12},{10,14},{12... | collective-permute-start | bytes 1966088 | tf_op jit(solution)/shard_map/ppermute | solution.py:22
  94.2 34.6 %collective-permute-start.21 = (f32[4,40,1024]{2,1,0:T(8,128)S(1)}, f32[4,40,1024]{2,1,0:T(8,128)}, u32[]{:S(2)}, u32[]{:S(2)}) collective-permute-start(f32[4,40,1024]{2,1,0:T(8,128)S(1)} %bitcast.89), channel_id=1, source_target_pairs={{0,2},{2,4},{4,6},{6,0},{1,3},{3,5},{5,7},{7,1},{8,10},{10,12},{12... | collective-permute-start | bytes 1966088 | tf_op jit(solution)/shard_map/ppermute | solution.py:22
  95.0 8.5 %copy-start.2 = (bf16[1152,1024]{1,0:T(8,128)(2,1)S(1)}, bf16[1152,1024]{1,0:T(8,128)(2,1)}, u32[]{:S(2)}) copy-start(bf16[1152,1024]{1,0:T(8,128)(2,1)} %fusion.sl_ref) | copy-start | bytes 7077892
  99.3 34.3 %collective-permute-start.14 = (f32[160,1024]{1,0:T(8,128)}, f32[160,1024]{1,0:T(8,128)S(1)}, u32[]{:S(2)}, u32[]{:S(2)}) collective-permute-start(f32[160,1024]{1,0:T(8,128)} %get-tuple-element.50), channel_id=1, source_target_pairs={{0,8},{8,16},{16,24},{24,0},{1,9},{9,17},{17,25},{25,1},{2,10},{10... | collective-permute-start | bytes 1966088 | tf_op jit(solution)/shard_map/ppermute | solution.py:22
  100.8 33.0 %collective-permute-start.15 = (f32[160,1024]{1,0:T(8,128)}, f32[160,1024]{1,0:T(8,128)S(1)}, u32[]{:S(2)}, u32[]{:S(2)}) collective-permute-start(f32[160,1024]{1,0:T(8,128)} %get-tuple-element.51), channel_id=1, source_target_pairs={{0,16},{8,24},{16,0},{24,8},{1,17},{9,25},{17,1},{25,9},{2,18},{10... | collective-permute-start | bytes 1966088 | tf_op jit(solution)/shard_map/ppermute | solution.py:22
  110.3 23.5 %collective-permute-start.16 = (f32[160,1024]{1,0:T(8,128)}, f32[160,1024]{1,0:T(8,128)S(1)}, u32[]{:S(2)}, u32[]{:S(2)}) collective-permute-start(f32[160,1024]{1,0:T(8,128)} %get-tuple-element.52), channel_id=1, source_target_pairs={{0,24},{8,0},{16,8},{24,16},{1,25},{9,1},{17,9},{25,17},{2,26},{10... | collective-permute-start | bytes 1966088 | tf_op jit(solution)/shard_map/ppermute | solution.py:22
  128.7 5.0 %copy-start.5 = (f32[160,1024]{1,0:T(8,128)S(1)}, f32[160,1024]{1,0:T(8,128)}, u32[]{:S(2)}) copy-start(f32[160,1024]{1,0:T(8,128)} %get-tuple-element.49) | copy-start | bytes 1966084
  130.3 8.1 %collective-permute-start.24 = (f32[40,1024]{1,0:T(8,128)S(1)}, f32[40,1024]{1,0:T(8,128)S(1)}, u32[]{:S(2)}, u32[]{:S(2)}) collective-permute-start(f32[40,1024]{1,0:T(8,128)S(1)} %get-tuple-element.72), channel_id=1, source_target_pairs={{0,8},{8,16},{16,24},{24,0},{1,9},{9,17},{17,25},{25,1},{2,10},{10... | collective-permute-start | bytes 491528 | tf_op jit(solution)/shard_map/ppermute | solution.py:22
  130.3 11.5 %collective-permute-start.26 = (f32[40,1024]{1,0:T(8,128)S(1)}, f32[40,1024]{1,0:T(8,128)S(1)}, u32[]{:S(2)}, u32[]{:S(2)}) collective-permute-start(f32[40,1024]{1,0:T(8,128)S(1)} %get-tuple-element.73), channel_id=1, source_target_pairs={{0,24},{8,0},{16,8},{24,16},{1,25},{9,1},{17,9},{25,17},{2,26},{10... | collective-permute-start | bytes 491528 | tf_op jit(solution)/shard_map/ppermute | solution.py:22
  133.6 8.2 %collective-permute-start.25 = (f32[40,1024]{1,0:T(8,128)S(1)}, f32[40,1024]{1,0:T(8,128)S(1)}, u32[]{:S(2)}, u32[]{:S(2)}) collective-permute-start(f32[40,1024]{1,0:T(8,128)S(1)} %get-tuple-element.74), channel_id=1, source_target_pairs={{0,16},{8,24},{16,0},{24,8},{1,17},{9,25},{17,1},{25,9},{2,18},{10... | collective-permute-start | bytes 491528 | tf_op jit(solution)/shard_map/ppermute | solution.py:22
  134.0 11.2 %copy-start.4 = (bf16[1152,1024]{1,0:T(8,128)(2,1)S(1)}, bf16[1152,1024]{1,0:T(8,128)(2,1)}, u32[]{:S(2)}) copy-start(bf16[1152,1024]{1,0:T(8,128)(2,1)} %get-tuple-element.36) | copy-start | bytes 7077892
  134.1 8.6 %collective-permute-start.17 = (f32[40,1024]{1,0:T(8,128)S(1)}, f32[40,1024]{1,0:T(8,128)S(1)}, u32[]{:S(2)}, u32[]{:S(2)}) collective-permute-start(f32[40,1024]{1,0:T(8,128)S(1)} %get-tuple-element.69), channel_id=1, source_target_pairs={{0,2},{2,4},{4,6},{6,0},{1,3},{3,5},{5,7},{7,1},{8,10},{10,12},{12... | collective-permute-start | bytes 491528 | tf_op jit(solution)/shard_map/ppermute | solution.py:22
  136.7 6.0 %collective-permute-start.19 = (f32[40,1024]{1,0:T(8,128)S(1)}, f32[40,1024]{1,0:T(8,128)S(1)}, u32[]{:S(2)}, u32[]{:S(2)}) collective-permute-start(f32[40,1024]{1,0:T(8,128)S(1)} %get-tuple-element.70), channel_id=1, source_target_pairs={{0,6},{2,0},{4,2},{6,4},{1,7},{3,1},{5,3},{7,5},{8,14},{10,8},{12,... | collective-permute-start | bytes 491528 | tf_op jit(solution)/shard_map/ppermute | solution.py:22
  138.4 6.8 %collective-permute-start.18 = (f32[40,1024]{1,0:T(8,128)S(1)}, f32[40,1024]{1,0:T(8,128)S(1)}, u32[]{:S(2)}, u32[]{:S(2)}) collective-permute-start(f32[40,1024]{1,0:T(8,128)S(1)} %get-tuple-element.71), channel_id=1, source_target_pairs={{0,4},{2,6},{4,0},{6,2},{1,5},{3,7},{5,1},{7,3},{8,12},{10,14},{12... | collective-permute-start | bytes 491528 | tf_op jit(solution)/shard_map/ppermute | solution.py:22
  141.8 15.8 %copy-start.1 = (bf16[1,64,36]{1,2,0:T(8,128)(2,1)S(1)}, bf16[1,64,36]{1,2,0:T(8,128)(2,1)}, u32[]{:S(2)}) copy-start(bf16[1,64,36]{1,2,0:T(8,128)(2,1)} %param.15) | copy-start | bytes 13828
  142.6 9.4 %copy-start.6 = (bf16[1152,36]{0,1:T(8,128)(2,1)S(1)}, bf16[1152,36]{0,1:T(8,128)(2,1)}, u32[]{:S(2)}) copy-start(bf16[1152,36]{0,1:T(8,128)(2,1)} %param.14) | copy-start | bytes 248836
  146.0 7.8 %collective-permute-start.27 = (f32[9,2304]{1,0:T(8,128)S(1)}, f32[9,2304]{1,0:T(8,128)S(1)}, u32[]{:S(2)}, u32[]{:S(2)}) collective-permute-start(f32[9,2304]{1,0:T(8,128)S(1)} %get-tuple-element.75), channel_id=1, source_target_pairs={{0,32},{32,64},{64,96},{96,0},{1,33},{33,65},{65,97},{97,1},{2,34}... | collective-permute-start | bytes 248840 | tf_op jit(solution)/shard_map/ppermute | solution.py:22
  148.0 5.8 %collective-permute-start.29 = (f32[9,2304]{1,0:T(8,128)S(1)}, f32[9,2304]{1,0:T(8,128)S(1)}, u32[]{:S(2)}, u32[]{:S(2)}) collective-permute-start(f32[9,2304]{1,0:T(8,128)S(1)} %get-tuple-element.76), channel_id=1, source_target_pairs={{0,96},{32,0},{64,32},{96,64},{1,97},{33,1},{65,33},{97,65},{2,98}... | collective-permute-start | bytes 248840 | tf_op jit(solution)/shard_map/ppermute | solution.py:22
  150.2 6.6 %collective-permute-start.28 = (f32[9,2304]{1,0:T(8,128)S(1)}, f32[9,2304]{1,0:T(8,128)S(1)}, u32[]{:S(2)}, u32[]{:S(2)}) collective-permute-start(f32[9,2304]{1,0:T(8,128)S(1)} %get-tuple-element.77), channel_id=1, source_target_pairs={{0,64},{32,96},{64,0},{96,32},{1,65},{33,97},{65,1},{97,33},{2,66}... | collective-permute-start | bytes 248840 | tf_op jit(solution)/shard_map/ppermute | solution.py:22

commit v2 on v1

--- a/solution.py
+++ b/solution.py
@@ -71,7 +71,7 @@
     return slice(start, start + WINDOW), slice(GROUP * nlat * j, GROUP * nlat * (j + 1))
 
 
-def call(body, steps, ins, outs, scratch, flops, moved, name):
+def call(body, steps, ins, outs, scratch, flops, moved, name, room):
     specs = [
         pl.BlockSpec(b, m, pipeline_mode=pl.Buffered(1)) if m is whole_block else pl.BlockSpec(b, m)
         for _, b, m in ins
@@ -83,7 +83,7 @@
         out_specs=[pl.BlockSpec(b, m) for _, _, b, m in outs],
         out_shape=[jax.ShapeDtypeStruct(s, t) for s, t, _, _ in outs],
         scratch_shapes=scratch,
-        compiler_params=pltpu.CompilerParams(vmem_limit_bytes=56 * 2**20),
+        compiler_params=pltpu.CompilerParams(vmem_limit_bytes=room * 2**20),
         cost_estimate=pl.CostEstimate(flops=flops, bytes_accessed=moved, transcendentals=0),
         name=name,
     )(*[a for a, _, _ in ins])
@@ -284,6 +284,7 @@
         4 * padded * (d * d + WINDOW * cols),
         6 * padded * d + 2 * padded * cols + 2 * d * (2 * d + cols),
         "softmax",
+        56,
     )
     lc = sum(lc_y, after(lc, pack))
     pack = after(pack, lc)
@@ -335,6 +336,7 @@
         2 * padded * cols * (WINDOW + 2 * half_rows),
         2 * padded * (2 * d + 2 * cols) + 12 * half_rows * cols,
         "gradient",
+        32,
     )
     w_got = shift(w_send, "c", 1)
     u = after(u, w_send) * jnp.exp(top - top2) + u_got * jnp.exp(top_pair - top2)
@@ -344,7 +346,7 @@
     parts = pl.pallas_call(
         split_kernel,
         out_shape=[cut] * 4,
-        compiler_params=pltpu.CompilerParams(vmem_limit_bytes=56 * 2**20),
+        compiler_params=pltpu.CompilerParams(vmem_limit_bytes=16 * 2**20),
         cost_estimate=pl.CostEstimate(
             flops=half_rows * cols, bytes_accessed=12 * half_rows * cols, transcendentals=0
         ),
@@ -370,6 +372,7 @@
         4 * padded * d * cols,
         4 * padded * (d + cols) + 4 * d * cols,
         "back",
+        28,
     )[0]
     attn_rows = attn.reshape(width, HEADS, nlat).transpose(1, 0, 2).reshape(d, nlat).astype(BF16)
     attended = dot(attn_rows, w_out, 0, 0).astype(BF16)

time: 159 us -> 156 us (0.981)
  Pallas kernels: 56.1 us -> 48.2 us
  waiting for transfers between devices: 16.5 us -> 22.9 us
  local copies, waits for them, and re-layouts: 3.5 us -> 6.72 us
  matrix products: 28.6 us -> 25.9 us
  other arithmetic: 11.3 us -> 9.12 us
    ppermute x30, waiting for transfers between devices: 16.5 us -> 22.9 us  [shift(): return lax.ppermute(value, axis, [(i, (i + step) % n) for i in range(n)])]
    pallas_call x3, Pallas kernels: 51.8 us -> 46.1 us  [call(): pl.pallas_call(body, grid=(steps,), in_specs=specs, out_specs=[pl.BlockSp...]
    unnamed x26 -> x40, local copies, waits for them, and re-layouts: 0.07 us -> 3.27 us
    dot_general x9, matrix products: 28.6 us -> 25.9 us  [dot(): lax.dot_general(a, b, (((ca,), (cb,)), ((), ())), preferred_element_type=...]
    pallas_call x1, Pallas kernels: 4.26 us -> 2.16 us  [per_device(): pl.pallas_call(split_kernel, out_shape=[cut] * 4, compiler_params=pltpu.C...]
  transfers between devices with their start and end apart: 30 -> 30, of which waited for: 11 -> 13; matrix products, arithmetic and copies ran while one was open for 23% -> 21% of each run, Pallas kernels for 36% -> 31%
where the time goes in v2:
time: 156 us
  Pallas kernels  48.2 us (31%)
  starting transfers between devices  41.7 us (27%)
  matrix products  25.9 us (17%)
  waiting for transfers between devices  22.9 us (15%)
  other arithmetic  9.12 us (6%)
  local copies, waits for them, and re-layouts  6.72 us (4%)
    pallas_call x3, Pallas kernels, call(): pl.pallas_call(body, grid=(steps,), in_specs=specs, out_specs=[pl.BlockSp...  46.1 us
    ppermute x30, starting transfers between devices, shift(): return lax.ppermute(value, axis, [(i, (i + step) % n) for i in range(n)])  41.7 us
    dot_general x9, matrix products, dot(): lax.dot_general(a, b, (((ca,), (cb,)), ((), ())), preferred_element_type=...  25.9 us
    ppermute x30, waiting for transfers between devices, shift(): return lax.ppermute(value, axis, [(i, (i + step) % n) for i in range(n)])  22.9 us
    add x1, other arithmetic, per_device(): after(u, w_send) * jnp.exp(top - top2) + u_got * jnp.exp(top_pair - top2)  3.4 us
    unnamed x40, local copies, waits for them, and re-layouts  3.27 us
  transfers between devices with their start and end apart: 30, of which 13 were waited for; matrix products, arithmetic and copies ran while one was open for 21% of the time, Pallas kernels for 31%

profile of v2, /device:TPU:0, one launch (start us, length us, event | category | flops | bytes accessed | tf_op | source)
XLA Modules:
  0.0 155.7 jit_solution(1279725643344994681)
XLA Ops:
  0.6 1.2 dot_general.29
  1.8 0.3 fusion.20
  2.5 1.4 collective-permute-done
  4.0 3.4 %collective-permute-start.2 = (f32[72,512]{1,0:T(8,128)S(1)}, f32[72,512]{1,0:T(8,128)S(1)}, u32[]{:S(2)}, u32[]{:S(2)}) collective-permute-start(f32[72,512]{1,0:T(8,128)S(1)} %dynamic-slice_add_fusion), channel_id=1, source_target_pairs={{0,16},{8,24},{16,0},{24,8},{1,17},{9,25},{17,1},{25,9},{2,18},{10... | collective-permute-start | bytes 442376 | tf_op jit(solution)/shard_map/ppermute | solution.py:22
  7.3 0.7 collective-permute-start.1
  8.0 2.6 %collective-permute-start.3 = (f32[72,512]{1,0:T(8,128)S(1)}, f32[72,512]{1,0:T(8,128)S(1)}, u32[]{:S(2)}, u32[]{:S(2)}) collective-permute-start(f32[72,512]{1,0:T(8,128)S(1)} %dynamic-slice_add_fusion), channel_id=1, source_target_pairs={{0,24},{8,0},{16,8},{24,16},{1,25},{9,1},{17,9},{25,17},{2,26},{10... | collective-permute-start | bytes 442376 | tf_op jit(solution)/shard_map/ppermute | solution.py:22
  10.6 24.5 %softmax.1 = (bf16[1536,1152]{1,0:T(8,128)(2,1)}, bf16[1536,1152]{1,0:T(8,128)(2,1)}, bf16[1536,1024]{1,0:T(8,128)(2,1)}, f32[80,1024]{1,0:T(8,128)}, bf16[1152,1024]{1,0:T(8,128)(2,1)}) custom-call(bf16[1458,1152]{1,0:T(8,128)(2,1)} %bitcast.86, bf16[1152]{0:T(1024)(128)(2,1)} %gain_ref.3, bf16[1152,1152]{1,0:T(8,128)(2,1)} %wk_ref.1, ...), custom_call_target="tpu_custom_call" | custom-call | flops 10569646080 | bytes 21430272 | tf_op jit(solution)/shard_map/softmax/pallas_call | solution.py:79
  35.3 1.7 %collective-permute-done.4 = f32[80,1024]{1,0:T(8,128)S(1)} collective-permute-done((f32[80,1024]{1,0:T(8,128)}, f32[80,1024]{1,0:T(8,128)S(1)}, u32[]{:S(2)}, u32[]{:S(2)}) %collective-permute-start.4) | collective-permute-done | bytes 327712 | tf_op jit(solution)/shard_map/ppermute | solution.py:22
  37.0 0.8 subtract_exponential_fusion.5
  38.0 0.5 broadcast.417
  38.5 0.7 subtract_exponential_fusion.4
  39.3 1.0 fusion.19
  40.3 2.8 %collective-permute-start.7 = (f32[160,512]{1,0:T(8,128)S(1)}, f32[160,512]{1,0:T(8,128)S(1)}, u32[]{:S(2)}, u32[]{:S(2)}) collective-permute-start(f32[160,512]{1,0:T(8,128)S(1)} %pad_maximum_fusion), channel_id=1, source_target_pairs={{0,6},{2,0},{4,2},{6,4},{1,7},{3,1},{5,3},{7,5},{8,14},{10,8},{12,... | collective-permute-start | bytes 983048 | tf_op jit(solution)/shard_map/ppermute | solution.py:22
  43.1 0.8 collective-permute-start.6
  43.9 0.9 collective-permute-start.5
  44.8 7.8 %convolution_convert_fusion.t_ref = bf16[1280,1536]{1,0:T(8,128)(2,1)S(1)} fusion(bf16[1536,1152]{1,0:T(8,128)(2,1)} %get-tuple-element.34, s32[1280]{0:T(1024)S(1)} %fusion.44), kind=kOutput, calls=%fused_computation | convolution fusion | flops 4533288960 | bytes 7476224 | tf_op jit(solution)/shard_map/dot_general | solution.py:17
  52.7 4.5 %convolution_convert_fusion.2.qk_ref = bf16[1152,1024]{1,0:T(8,128)(2,1)} fusion(bf16[1152,1152]{1,0:T(8,128)(2,1)S(1)} %copy-done.15, bf16[1152,1024]{1,0:T(8,128)(2,1)S(1)} %copy-done.12), kind=kOutput, calls=%fused_computation.6 | convolution fusion | flops 2719088640 | bytes 7372800 | tf_op jit(solution)/shard_map/dot_general | solution.py:17
  57.4 3.7 %collective-permute-done.5 = f32[160,512]{1,0:T(8,128)S(1)} collective-permute-done((f32[160,512]{1,0:T(8,128)S(1)}, f32[160,512]{1,0:T(8,128)S(1)}, u32[]{:S(2)}, u32[]{:S(2)}) %collective-permute-start.5) | collective-permute-done | bytes 327712 | tf_op jit(solution)/shard_map/ppermute | solution.py:22
  61.4 1.5 collective-permute-start.10
  62.9 0.5 collective-permute-start.9
  63.4 3.7 %fusion.2 = f32[640,1024]{1,0:T(8,128)} fusion(bf16[1536,1024]{1,0:T(8,128)(2,1)S(1)} %copy-done.6, bf16[1280,1536]{1,0:T(8,128)(2,1)S(1)} %convolution_convert_fusion.t_ref), kind=kOutput, calls=%fused_computation.9 | convolution fusion | flops 2013265920 | bytes 7733248 | tf_op jit(solution)/shard_map/dot_general | solution.py:17
  67.1 0.6 collective-permute-start.8
  67.7 3.8 %fusion.4 = f32[640,1024]{1,0:T(8,128)} fusion(bf16[1536,1024]{1,0:T(8,128)(2,1)S(1)} %copy-done.6, bf16[1280,1536]{1,0:T(8,128)(2,1)S(1)} %convolution_convert_fusion.t_ref), kind=kOutput, calls=%fused_computation.11 | convolution fusion | flops 2013265920 | bytes 7733248 | tf_op jit(solution)/shard_map/dot_general | solution.py:17
  71.5 0.3 collective-permute-done.8
  71.8 0.5 fusion.sl_ref
  72.7 0.3 collective-permute-start.12
  73.0 1.1 collective-permute-done.12
  74.2 0.8 broadcast_multiply_fusion
  75.1 8.5 %gradient.1 = (bf16[1536,1024]{1,0:T(8,128)(2,1)S(1)}, f32[640,1024]{1,0:T(8,128)S(1)}, f32[640,1024]{1,0:T(8,128)}) custom-call(bf16[1536,1152]{1,0:T(8,128)(2,1)S(1)} %copy-done.8, bf16[1152,1024]{1,0:T(8,128)(2,1)S(1)} %fusion.sl_ref, bf16[1536,1024]{1,0:T(8,128)(2,1)S(1)} %copy-done.6, f32[8,1024]{1,0:T(8,128)S(1)} %maximum_maximum_fusion.state_ref, ...), custom_call_target="tpu_custom_call" | custom-call | flops 5234491392 | bytes 21233664 | tf_op jit(solution)/shard_map/gradient/pallas_call | solution.py:79
  83.7 1.5 copy-done.2
  85.2 1.6 %copy-done.9 = bf16[1536,1024]{1,0:T(8,128)(2,1)} copy-done((bf16[1536,1024]{1,0:T(8,128)(2,1)}, bf16[1536,1024]{1,0:T(8,128)(2,1)S(1)}, u32[]{:S(2)}) %copy-start.9) | copy-done | bytes 3145752
  87.3 0.4 copy.15
  87.7 0.3 convert_element_type.40
  88.0 3.4 %multiply_add_fusion = f32[640,1024]{1,0:T(8,128)S(1)} fusion(f32[640,1024]{1,0:T(8,128)} %collective-permute-done.20, f32[640,1024]{1,0:T(8,128)} %fusion.4, f32[1024]{0:T(1024)S(1)} %bitcast.105, f32[1024]{0:T(1024)S(1)} %bitcast.103), kind=kLoop, calls=%fused_computation.8 | loop fusion | flops 1966080 | bytes 7872512 | tf_op jit(solution)/shard_map/add | solution.py:342
  91.5 0.3 fusion.72
  91.8 0.7 collective-permute-start.23
  92.4 0.8 collective-permute-start.22
  93.2 0.8 collective-permute-start.21
  94.1 2.2 %split.1 = (f32[160,1024]{1,0:T(8,128)S(1)}, f32[160,1024]{1,0:T(8,128)S(1)}, f32[160,1024]{1,0:T(8,128)S(1)}, f32[160,1024]{1,0:T(8,128)S(1)}) custom-call(f32[640,1024]{1,0:T(8,128)S(1)} %copy-done.3, f32[640,1024]{1,0:T(8,128)} %collective-permute-done.13.got_ref), custom_call_target="tpu_custom_call" | custom-call | flops 655360 | bytes 7864320 | tf_op jit(solution)/shard_map/split/pallas_call | solution.py:346
  96.2 1.6 %collective-permute-start.14 = (f32[160,1024]{1,0:T(8,128)S(1)}, f32[160,1024]{1,0:T(8,128)S(1)}, u32[]{:S(2)}, u32[]{:S(2)}) collective-permute-start(f32[160,1024]{1,0:T(8,128)S(1)} %get-tuple-element.50), channel_id=1, source_target_pairs={{0,8},{8,16},{16,24},{24,0},{1,9},{9,17},{17,25},{25,1},{2,10},{10... | collective-permute-start | bytes 1966088 | tf_op jit(solution)/shard_map/ppermute | solution.py:22
  97.9 2.7 %collective-permute-start.15 = (f32[160,1024]{1,0:T(8,128)S(1)}, f32[160,1024]{1,0:T(8,128)S(1)}, u32[]{:S(2)}, u32[]{:S(2)}) collective-permute-start(f32[160,1024]{1,0:T(8,128)S(1)} %get-tuple-element.51), channel_id=1, source_target_pairs={{0,16},{8,24},{16,0},{24,8},{1,17},{9,25},{17,1},{25,9},{2,18},{10... | collective-permute-start | bytes 1966088 | tf_op jit(solution)/shard_map/ppermute | solution.py:22
  100.6 3.5 %convolution_convert_fusion.1.qv_ref = bf16[1152,1024]{1,0:T(8,128)(2,1)S(1)} fusion(bf16[1152,1152]{1,0:T(8,128)(2,1)S(1)} %copy-done.16, bf16[1152,1024]{1,0:T(8,128)(2,1)S(1)} %fusion.sl_ref), kind=kOutput, calls=%fused_computation.5 | convolution fusion | flops 2719088640 | bytes 7372800 | tf_op jit(solution)/shard_map/dot_general | solution.py:17
  104.0 5.3 %collective-permute-done.23 = f32[4,40,1024]{2,1,0:T(8,128)S(1)} collective-permute-done((f32[4,40,1024]{2,1,0:T(8,128)S(1)}, f32[4,40,1024]{2,1,0:T(8,128)S(1)}, u32[]{:S(2)}, u32[]{:S(2)}) %collective-permute-start.23) | collective-permute-done | bytes 655392 | tf_op jit(solution)/shard_map/ppermute | solution.py:22
  109.4 2.8 %collective-permute-start.16 = (f32[160,1024]{1,0:T(8,128)S(1)}, f32[160,1024]{1,0:T(8,128)S(1)}, u32[]{:S(2)}, u32[]{:S(2)}) collective-permute-start(f32[160,1024]{1,0:T(8,128)S(1)} %get-tuple-element.52), channel_id=1, source_target_pairs={{0,24},{8,0},{16,8},{24,16},{1,25},{9,1},{17,9},{25,17},{2,26},{10... | collective-permute-start | bytes 1966088 | tf_op jit(solution)/shard_map/ppermute | solution.py:22
  112.2 13.1 %back.1 = bf16[1458,1152]{1,0:T(8,128)(2,1)} custom-call(bf16[1536,1024]{1,0:T(8,128)(2,1)S(1)} %copy-done.10, bf16[1536,1024]{1,0:T(8,128)(2,1)S(1)} %copy-done.7, bf16[1152,1024]{1,0:T(8,128)(2,1)S(1)} %copy-done.11, bf16[1152,1024]{1,0:T(8,128)(2,1)S(1)} %convolution_convert_fusion.1.qv_ref, f32[8,1024]{1,0:T(8,128)S(1)} %maximum_maximum_fusion.state_ref, ...), custom_call_target="tpu_custom_call" | custom-call | flops 7247757312 | bytes 18087936 | tf_op jit(solution)/shard_map/back/pallas_call | solution.py:79
  125.2 0.3 add_multiply_fusion
  125.6 0.8 collective-permute-start.24
  126.4 2.5 %collective-permute-start.26 = (f32[40,1024]{1,0:T(8,128)S(1)}, f32[40,1024]{1,0:T(8,128)S(1)}, u32[]{:S(2)}, u32[]{:S(2)}) collective-permute-start(f32[40,1024]{1,0:T(8,128)S(1)} %get-tuple-element.73), channel_id=1, source_target_pairs={{0,24},{8,0},{16,8},{24,16},{1,25},{9,1},{17,9},{25,17},{2,26},{10... | collective-permute-start | bytes 491528 | tf_op jit(solution)/shard_map/ppermute | solution.py:22
  128.9 2.1 %collective-permute-start.25 = (f32[40,1024]{1,0:T(8,128)S(1)}, f32[40,1024]{1,0:T(8,128)S(1)}, u32[]{:S(2)}, u32[]{:S(2)}) collective-permute-start(f32[40,1024]{1,0:T(8,128)S(1)} %get-tuple-element.74), channel_id=1, source_target_pairs={{0,16},{8,24},{16,0},{24,8},{1,17},{9,25},{17,1},{25,9},{2,18},{10... | collective-permute-start | bytes 491528 | tf_op jit(solution)/shard_map/ppermute | solution.py:22
  131.4 2.0 %collective-permute-start.17 = (f32[40,1024]{1,0:T(8,128)S(1)}, f32[40,1024]{1,0:T(8,128)S(1)}, u32[]{:S(2)}, u32[]{:S(2)}) collective-permute-start(f32[40,1024]{1,0:T(8,128)S(1)} %get-tuple-element.69), channel_id=1, source_target_pairs={{0,2},{2,4},{4,6},{6,0},{1,3},{3,5},{5,7},{7,1},{8,10},{10,12},{12... | collective-permute-start | bytes 491528 | tf_op jit(solution)/shard_map/ppermute | solution.py:22
  133.4 1.3 collective-permute-start.19
  134.7 3.0 %collective-permute-start.18 = (f32[40,1024]{1,0:T(8,128)S(1)}, f32[40,1024]{1,0:T(8,128)S(1)}, u32[]{:S(2)}, u32[]{:S(2)}) collective-permute-start(f32[40,1024]{1,0:T(8,128)S(1)} %get-tuple-element.71), channel_id=1, source_target_pairs={{0,4},{2,6},{4,0},{6,2},{1,5},{3,7},{5,1},{7,3},{8,12},{10,14},{12... | collective-permute-start | bytes 491528 | tf_op jit(solution)/shard_map/ppermute | solution.py:22
  137.6 0.8 fusion.31
  138.5 1.4 collective-permute-done.19
  139.8 2.4 %collective-permute-done.18 = f32[40,1024]{1,0:T(8,128)S(1)} collective-permute-done((f32[40,1024]{1,0:T(8,128)S(1)}, f32[40,1024]{1,0:T(8,128)S(1)}, u32[]{:S(2)}, u32[]{:S(2)}) %collective-permute-start.18) | collective-permute-done | bytes 163872 | tf_op jit(solution)/shard_map/ppermute | solution.py:22
  142.2 0.8 fusion.29
  143.1 2.0 %collective-permute-start.27 = (f32[9,2304]{1,0:T(8,128)S(1)}, f32[9,2304]{1,0:T(8,128)S(1)}, u32[]{:S(2)}, u32[]{:S(2)}) collective-permute-start(f32[9,2304]{1,0:T(8,128)S(1)} %get-tuple-element.75), channel_id=1, source_target_pairs={{0,32},{32,64},{64,96},{96,0},{1,33},{33,65},{65,97},{97,1},{2,34}... | collective-permute-start | bytes 248840 | tf_op jit(solution)/shard_map/ppermute | solution.py:22
  145.1 2.2 %collective-permute-start.29 = (f32[9,2304]{1,0:T(8,128)S(1)}, f32[9,2304]{1,0:T(8,128)S(1)}, u32[]{:S(2)}, u32[]{:S(2)}) collective-permute-start(f32[9,2304]{1,0:T(8,128)S(1)} %get-tuple-element.76), channel_id=1, source_target_pairs={{0,96},{32,0},{64,32},{96,64},{1,97},{33,1},{65,33},{97,65},{2,98}... | collective-permute-start | bytes 248840 | tf_op jit(solution)/shard_map/ppermute | solution.py:22
  147.3 1.8 %collective-permute-start.28 = (f32[9,2304]{1,0:T(8,128)S(1)}, f32[9,2304]{1,0:T(8,128)S(1)}, u32[]{:S(2)}, u32[]{:S(2)}) collective-permute-start(f32[9,2304]{1,0:T(8,128)S(1)} %get-tuple-element.77), channel_id=1, source_target_pairs={{0,64},{32,96},{64,0},{96,32},{1,65},{33,97},{65,1},{97,33},{2,66}... | collective-permute-start | bytes 248840 | tf_op jit(solution)/shard_map/ppermute | solution.py:22
  149.1 0.8 fusion.6
  149.9 0.6 collective-permute-done.27
  150.5 2.5 %collective-permute-done.29 = f32[9,2304]{1,0:T(8,128)S(1)} collective-permute-done((f32[9,2304]{1,0:T(8,128)S(1)}, f32[9,2304]{1,0:T(8,128)S(1)}, u32[]{:S(2)}, u32[]{:S(2)}) %collective-permute-start.29) | collective-permute-done | bytes 82976 | tf_op jit(solution)/shard_map/ppermute | solution.py:22
  153.0 1.9 %collective-permute-done.28 = f32[9,2304]{1,0:T(8,128)S(1)} collective-permute-done((f32[9,2304]{1,0:T(8,128)S(1)}, f32[9,2304]{1,0:T(8,128)S(1)}, u32[]{:S(2)}, u32[]{:S(2)}) %collective-permute-start.28) | collective-permute-done | bytes 82976 | tf_op jit(solution)/shard_map/ppermute | solution.py:22
  154.9 0.7 fusion.26
  (99 shorter events, 2.8 us)
Async XLA Ops:
  0.6 1.2 copy-start
  2.3 1.7 %collective-permute-start = (f32[72,1024]{1,0:T(8,128)S(1)}, f32[72,1024]{1,0:T(8,128)S(1)}, u32[]{:S(2)}, u32[]{:S(2)}) collective-permute-start(f32[72,1024]{1,0:T(8,128)S(1)} %copy.16), channel_id=1, source_target_pairs={{0,1},{1,0},{2,3},{3,2},{4,5},{5,4},{6,7},{7,6},{8,9},{9,8},{10,11... | collective-permute-start | bytes 884744 | tf_op jit(solution)/shard_map/ppermute | solution.py:22
  4.0 31.1 %collective-permute-start.2 = (f32[72,512]{1,0:T(8,128)S(1)}, f32[72,512]{1,0:T(8,128)S(1)}, u32[]{:S(2)}, u32[]{:S(2)}) collective-permute-start(f32[72,512]{1,0:T(8,128)S(1)} %dynamic-slice_add_fusion), channel_id=1, source_target_pairs={{0,16},{8,24},{16,0},{24,8},{1,17},{9,25},{17,1},{25,9},{2,18},{10... | collective-permute-start | bytes 442376 | tf_op jit(solution)/shard_map/ppermute | solution.py:22
  7.3 27.7 %collective-permute-start.1 = (f32[72,512]{1,0:T(8,128)S(1)}, f32[72,512]{1,0:T(8,128)S(1)}, u32[]{:S(2)}, u32[]{:S(2)}) collective-permute-start(f32[72,512]{1,0:T(8,128)S(1)} %dynamic-slice_add_fusion), channel_id=1, source_target_pairs={{0,8},{8,16},{16,24},{24,0},{1,9},{9,17},{17,25},{25,1},{2,10},{10... | collective-permute-start | bytes 442376 | tf_op jit(solution)/shard_map/ppermute | solution.py:22
  8.0 27.0 %collective-permute-start.3 = (f32[72,512]{1,0:T(8,128)S(1)}, f32[72,512]{1,0:T(8,128)S(1)}, u32[]{:S(2)}, u32[]{:S(2)}) collective-permute-start(f32[72,512]{1,0:T(8,128)S(1)} %dynamic-slice_add_fusion), channel_id=1, source_target_pairs={{0,24},{8,0},{16,8},{24,16},{1,25},{9,1},{17,9},{25,17},{2,26},{10... | collective-permute-start | bytes 442376 | tf_op jit(solution)/shard_map/ppermute | solution.py:22
  35.1 1.9 %collective-permute-start.4 = (f32[80,1024]{1,0:T(8,128)}, f32[80,1024]{1,0:T(8,128)S(1)}, u32[]{:S(2)}, u32[]{:S(2)}) collective-permute-start(f32[80,1024]{1,0:T(8,128)} %get-tuple-element.32), channel_id=1, source_target_pairs={{0,1},{1,0},{2,3},{3,2},{4,5},{5,4},{6,7},{7,6},{8,9},{9,8},{10,11... | collective-permute-start | bytes 983048 | tf_op jit(solution)/shard_map/ppermute | solution.py:22
  40.3 17.1 %collective-permute-start.7 = (f32[160,512]{1,0:T(8,128)S(1)}, f32[160,512]{1,0:T(8,128)S(1)}, u32[]{:S(2)}, u32[]{:S(2)}) collective-permute-start(f32[160,512]{1,0:T(8,128)S(1)} %pad_maximum_fusion), channel_id=1, source_target_pairs={{0,6},{2,0},{4,2},{6,4},{1,7},{3,1},{5,3},{7,5},{8,14},{10,8},{12,... | collective-permute-start | bytes 983048 | tf_op jit(solution)/shard_map/ppermute | solution.py:22
  43.1 14.3 %collective-permute-start.6 = (f32[160,512]{1,0:T(8,128)S(1)}, f32[160,512]{1,0:T(8,128)S(1)}, u32[]{:S(2)}, u32[]{:S(2)}) collective-permute-start(f32[160,512]{1,0:T(8,128)S(1)} %pad_maximum_fusion), channel_id=1, source_target_pairs={{0,4},{2,6},{4,0},{6,2},{1,5},{3,7},{5,1},{7,3},{8,12},{10,14},{12... | collective-permute-start | bytes 983048 | tf_op jit(solution)/shard_map/ppermute | solution.py:22
  43.9 17.2 %collective-permute-start.5 = (f32[160,512]{1,0:T(8,128)S(1)}, f32[160,512]{1,0:T(8,128)S(1)}, u32[]{:S(2)}, u32[]{:S(2)}) collective-permute-start(f32[160,512]{1,0:T(8,128)S(1)} %pad_maximum_fusion), channel_id=1, source_target_pairs={{0,2},{2,4},{4,6},{6,0},{1,3},{3,5},{5,7},{7,1},{8,10},{10,12},{12... | collective-permute-start | bytes 983048 | tf_op jit(solution)/shard_map/ppermute | solution.py:22
  44.8 7.8 %copy-start.12 = (bf16[1152,1024]{1,0:T(8,128)(2,1)S(1)}, bf16[1152,1024]{1,0:T(8,128)(2,1)}, u32[]{:S(2)}) copy-start(bf16[1152,1024]{1,0:T(8,128)(2,1)} %get-tuple-element.36) | copy-start | bytes 7077892
  44.8 7.8 %copy-start.15 = (bf16[1152,1152]{1,0:T(8,128)(2,1)S(1)}, bf16[1152,1152]{1,0:T(8,128)(2,1)}, u32[]{:S(2)}) copy-start(bf16[1152,1152]{1,0:T(8,128)(2,1)} %wk_ref.1) | copy-start | bytes 7962628
  52.7 10.7 %copy-start.6 = (bf16[1536,1024]{1,0:T(8,128)(2,1)S(1)}, bf16[1536,1024]{1,0:T(8,128)(2,1)}, u32[]{:S(2)}) copy-start(bf16[1536,1024]{1,0:T(8,128)(2,1)} %get-tuple-element.40.e_ref) | copy-start | bytes 9437188
  61.2 11.1 %collective-permute-start.11 = (f32[80,512]{1,0:T(8,128)S(1)}, f32[80,512]{1,0:T(8,128)S(1)}, u32[]{:S(2)}, u32[]{:S(2)}) collective-permute-start(f32[80,512]{1,0:T(8,128)S(1)} %fusion.15), channel_id=1, source_target_pairs={{0,24},{8,0},{16,8},{24,16},{1,25},{9,1},{17,9},{25,17},{2,26},{10... | collective-permute-start | bytes 491528 | tf_op jit(solution)/shard_map/ppermute | solution.py:22
  61.4 11.0 %collective-permute-start.10 = (f32[80,512]{1,0:T(8,128)S(1)}, f32[80,512]{1,0:T(8,128)S(1)}, u32[]{:S(2)}, u32[]{:S(2)}) collective-permute-start(f32[80,512]{1,0:T(8,128)S(1)} %fusion.15), channel_id=1, source_target_pairs={{0,16},{8,24},{16,0},{24,8},{1,17},{9,25},{17,1},{25,9},{2,18},{10... | collective-permute-start | bytes 491528 | tf_op jit(solution)/shard_map/ppermute | solution.py:22
  62.9 9.7 %collective-permute-start.9 = (f32[80,512]{1,0:T(8,128)S(1)}, f32[80,512]{1,0:T(8,128)S(1)}, u32[]{:S(2)}, u32[]{:S(2)}) collective-permute-start(f32[80,512]{1,0:T(8,128)S(1)} %fusion.15), channel_id=1, source_target_pairs={{0,8},{8,16},{16,24},{24,0},{1,9},{9,17},{17,25},{25,1},{2,10},{10... | collective-permute-start | bytes 491528 | tf_op jit(solution)/shard_map/ppermute | solution.py:22
  67.0 21.0 %collective-permute-start.20 = (f32[640,1024]{1,0:T(8,128)}, f32[640,1024]{1,0:T(8,128)}, u32[]{:S(2)}, u32[]{:S(2)}) collective-permute-start(f32[640,1024]{1,0:T(8,128)} %fusion.2), channel_id=1, source_target_pairs={{0,1},{1,0},{2,3},{3,2},{4,5},{5,4},{6,7},{7,6},{8,9},{9,8},{10,11... | collective-permute-start | bytes 7864328 | tf_op jit(solution)/shard_map/ppermute | solution.py:22
  67.1 4.7 %collective-permute-start.8 = (f32[72,512]{1,0:T(8,128)S(1)}, f32[72,512]{1,0:T(8,128)S(1)}, u32[]{:S(2)}, u32[]{:S(2)}) collective-permute-start(f32[72,512]{1,0:T(8,128)S(1)} %slice_add_fusion.1), channel_id=1, source_target_pairs={{0,1},{1,0},{2,3},{3,2},{4,5},{5,4},{6,7},{7,6},{8,9},{9,8},{10,11... | collective-permute-start | bytes 442376 | tf_op jit(solution)/shard_map/ppermute | solution.py:22
  71.8 3.3 %copy-start.8 = (bf16[1536,1152]{1,0:T(8,128)(2,1)S(1)}, bf16[1536,1152]{1,0:T(8,128)(2,1)}, u32[]{:S(2)}) copy-start(bf16[1536,1152]{1,0:T(8,128)(2,1)} %get-tuple-element.42.v_ref) | copy-start | bytes 10616836
  72.7 1.5 collective-permute-start.12
  83.7 1.5 copy-start.2
  85.2 1.6 %copy-start.9 = (bf16[1536,1024]{1,0:T(8,128)(2,1)}, bf16[1536,1024]{1,0:T(8,128)(2,1)S(1)}, u32[]{:S(2)}) copy-start(bf16[1536,1024]{1,0:T(8,128)(2,1)S(1)} %get-tuple-element.47.d_ref) | copy-start | bytes 9437188
  86.8 7.2 %collective-permute-start.13 = (f32[640,1024]{1,0:T(8,128)}, f32[640,1024]{1,0:T(8,128)}, u32[]{:S(2)}, u32[]{:S(2)}) collective-permute-start(f32[640,1024]{1,0:T(8,128)} %get-tuple-element.45), channel_id=1, source_target_pairs={{0,1},{1,0},{2,3},{3,2},{4,5},{5,4},{6,7},{7,6},{8,9},{9,8},{10,11... | collective-permute-start | bytes 7864328 | tf_op jit(solution)/shard_map/ppermute | solution.py:22
  91.5 2.6 %copy-start.3 = (f32[640,1024]{1,0:T(8,128)S(1)}, f32[640,1024]{1,0:T(8,128)}, u32[]{:S(2)}) copy-start(f32[640,1024]{1,0:T(8,128)} %copy-done.2) | copy-start | bytes 7864324
  91.8 17.6 %collective-permute-start.23 = (f32[4,40,1024]{2,1,0:T(8,128)S(1)}, f32[4,40,1024]{2,1,0:T(8,128)S(1)}, u32[]{:S(2)}, u32[]{:S(2)}) collective-permute-start(f32[4,40,1024]{2,1,0:T(8,128)S(1)} %bitcast.93), channel_id=1, source_target_pairs={{0,6},{2,0},{4,2},{6,4},{1,7},{3,1},{5,3},{7,5},{8,14},{10,8},{12,... | collective-permute-start | bytes 1966088 | tf_op jit(solution)/shard_map/ppermute | solution.py:22
  92.4 32.8 %collective-permute-start.22 = (f32[4,40,1024]{2,1,0:T(8,128)S(1)}, f32[4,40,1024]{2,1,0:T(8,128)S(1)}, u32[]{:S(2)}, u32[]{:S(2)}) collective-permute-start(f32[4,40,1024]{2,1,0:T(8,128)S(1)} %bitcast.92), channel_id=1, source_target_pairs={{0,4},{2,6},{4,0},{6,2},{1,5},{3,7},{5,1},{7,3},{8,12},{10,14},{12... | collective-permute-start | bytes 1966088 | tf_op jit(solution)/shard_map/ppermute | solution.py:22
  93.2 32.0 %collective-permute-start.21 = (f32[4,40,1024]{2,1,0:T(8,128)S(1)}, f32[4,40,1024]{2,1,0:T(8,128)S(1)}, u32[]{:S(2)}, u32[]{:S(2)}) collective-permute-start(f32[4,40,1024]{2,1,0:T(8,128)S(1)} %bitcast.91), channel_id=1, source_target_pairs={{0,2},{2,4},{4,6},{6,0},{1,3},{3,5},{5,7},{7,1},{8,10},{10,12},{12... | collective-permute-start | bytes 1966088 | tf_op jit(solution)/shard_map/ppermute | solution.py:22
  94.1 6.5 %copy-start.16 = (bf16[1152,1152]{1,0:T(8,128)(2,1)S(1)}, bf16[1152,1152]{1,0:T(8,128)(2,1)}, u32[]{:S(2)}) copy-start(bf16[1152,1152]{1,0:T(8,128)(2,1)} %wv_ref.1) | copy-start | bytes 7962628
  96.2 32.7 %collective-permute-start.14 = (f32[160,1024]{1,0:T(8,128)S(1)}, f32[160,1024]{1,0:T(8,128)S(1)}, u32[]{:S(2)}, u32[]{:S(2)}) collective-permute-start(f32[160,1024]{1,0:T(8,128)S(1)} %get-tuple-element.50), channel_id=1, source_target_pairs={{0,8},{8,16},{16,24},{24,0},{1,9},{9,17},{17,25},{25,1},{2,10},{10... | collective-permute-start | bytes 1966088 | tf_op jit(solution)/shard_map/ppermute | solution.py:22
  97.8 14.3 %copy-start.4 = (bf16[1,1458,1152]{2,1,0:T(8,128)(2,1)S(1)}, bf16[1,1458,1152]{2,1,0:T(8,128)(2,1)}, u32[]{:S(2)}) copy-start(bf16[1,1458,1152]{2,1,0:T(8,128)(2,1)} %param.8) | copy-start | bytes 10077700
  97.8 14.3 %copy-start.5 = (bf16[1152]{0:T(1024)(128)(2,1)S(1)}, bf16[1152]{0:T(1024)(128)(2,1)}, u32[]{:S(2)}) copy-start(bf16[1152]{0:T(1024)(128)(2,1)} %gain_ref.3) | copy-start | bytes 6916
  97.8 14.3 %copy-start.7 = (bf16[1536,1024]{1,0:T(8,128)(2,1)S(1)}, bf16[1536,1024]{1,0:T(8,128)(2,1)}, u32[]{:S(2)}) copy-start(bf16[1536,1024]{1,0:T(8,128)(2,1)} %get-tuple-element.40.e_ref) | copy-start | bytes 9437188
  97.8 14.3 %copy-start.10 = (bf16[1536,1024]{1,0:T(8,128)(2,1)S(1)}, bf16[1536,1024]{1,0:T(8,128)(2,1)}, u32[]{:S(2)}) copy-start(bf16[1536,1024]{1,0:T(8,128)(2,1)} %copy-done.9) | copy-start | bytes 9437188
  97.8 14.3 %copy-start.11 = (bf16[1152,1024]{1,0:T(8,128)(2,1)S(1)}, bf16[1152,1024]{1,0:T(8,128)(2,1)}, u32[]{:S(2)}) copy-start(bf16[1152,1024]{1,0:T(8,128)(2,1)} %convolution_convert_fusion.2.qk_ref) | copy-start | bytes 7077892
  97.9 33.2 %collective-permute-start.15 = (f32[160,1024]{1,0:T(8,128)S(1)}, f32[160,1024]{1,0:T(8,128)S(1)}, u32[]{:S(2)}, u32[]{:S(2)}) collective-permute-start(f32[160,1024]{1,0:T(8,128)S(1)} %get-tuple-element.51), channel_id=1, source_target_pairs={{0,16},{8,24},{16,0},{24,8},{1,17},{9,25},{17,1},{25,9},{2,18},{10... | collective-permute-start | bytes 1966088 | tf_op jit(solution)/shard_map/ppermute | solution.py:22
  109.4 21.7 %collective-permute-start.16 = (f32[160,1024]{1,0:T(8,128)S(1)}, f32[160,1024]{1,0:T(8,128)S(1)}, u32[]{:S(2)}, u32[]{:S(2)}) collective-permute-start(f32[160,1024]{1,0:T(8,128)S(1)} %get-tuple-element.52), channel_id=1, source_target_pairs={{0,24},{8,0},{16,8},{24,16},{1,25},{9,1},{17,9},{25,17},{2,26},{10... | collective-permute-start | bytes 1966088 | tf_op jit(solution)/shard_map/ppermute | solution.py:22
  125.6 9.1 %collective-permute-start.24 = (f32[40,1024]{1,0:T(8,128)S(1)}, f32[40,1024]{1,0:T(8,128)S(1)}, u32[]{:S(2)}, u32[]{:S(2)}) collective-permute-start(f32[40,1024]{1,0:T(8,128)S(1)} %get-tuple-element.72), channel_id=1, source_target_pairs={{0,8},{8,16},{16,24},{24,0},{1,9},{9,17},{17,25},{25,1},{2,10},{10... | collective-permute-start | bytes 491528 | tf_op jit(solution)/shard_map/ppermute | solution.py:22
  126.4 11.2 %collective-permute-start.26 = (f32[40,1024]{1,0:T(8,128)S(1)}, f32[40,1024]{1,0:T(8,128)S(1)}, u32[]{:S(2)}, u32[]{:S(2)}) collective-permute-start(f32[40,1024]{1,0:T(8,128)S(1)} %get-tuple-element.73), channel_id=1, source_target_pairs={{0,24},{8,0},{16,8},{24,16},{1,25},{9,1},{17,9},{25,17},{2,26},{10... | collective-permute-start | bytes 491528 | tf_op jit(solution)/shard_map/ppermute | solution.py:22
  128.9 8.7 %collective-permute-start.25 = (f32[40,1024]{1,0:T(8,128)S(1)}, f32[40,1024]{1,0:T(8,128)S(1)}, u32[]{:S(2)}, u32[]{:S(2)}) collective-permute-start(f32[40,1024]{1,0:T(8,128)S(1)} %get-tuple-element.74), channel_id=1, source_target_pairs={{0,16},{8,24},{16,0},{24,8},{1,17},{9,25},{17,1},{25,9},{2,18},{10... | collective-permute-start | bytes 491528 | tf_op jit(solution)/shard_map/ppermute | solution.py:22
  131.3 10.9 %copy-start.13 = (bf16[1152,1024]{1,0:T(8,128)(2,1)S(1)}, bf16[1152,1024]{1,0:T(8,128)(2,1)}, u32[]{:S(2)}) copy-start(bf16[1152,1024]{1,0:T(8,128)(2,1)} %get-tuple-element.36) | copy-start | bytes 7077892
  131.4 7.1 %collective-permute-start.17 = (f32[40,1024]{1,0:T(8,128)S(1)}, f32[40,1024]{1,0:T(8,128)S(1)}, u32[]{:S(2)}, u32[]{:S(2)}) collective-permute-start(f32[40,1024]{1,0:T(8,128)S(1)} %get-tuple-element.69), channel_id=1, source_target_pairs={{0,2},{2,4},{4,6},{6,0},{1,3},{3,5},{5,7},{7,1},{8,10},{10,12},{12... | collective-permute-start | bytes 491528 | tf_op jit(solution)/shard_map/ppermute | solution.py:22
  133.4 6.5 %collective-permute-start.19 = (f32[40,1024]{1,0:T(8,128)S(1)}, f32[40,1024]{1,0:T(8,128)S(1)}, u32[]{:S(2)}, u32[]{:S(2)}) collective-permute-start(f32[40,1024]{1,0:T(8,128)S(1)} %get-tuple-element.70), channel_id=1, source_target_pairs={{0,6},{2,0},{4,2},{6,4},{1,7},{3,1},{5,3},{7,5},{8,14},{10,8},{12,... | collective-permute-start | bytes 491528 | tf_op jit(solution)/shard_map/ppermute | solution.py:22
  134.7 7.6 %collective-permute-start.18 = (f32[40,1024]{1,0:T(8,128)S(1)}, f32[40,1024]{1,0:T(8,128)S(1)}, u32[]{:S(2)}, u32[]{:S(2)}) collective-permute-start(f32[40,1024]{1,0:T(8,128)S(1)} %get-tuple-element.71), channel_id=1, source_target_pairs={{0,4},{2,6},{4,0},{6,2},{1,5},{3,7},{5,1},{7,3},{8,12},{10,14},{12... | collective-permute-start | bytes 491528 | tf_op jit(solution)/shard_map/ppermute | solution.py:22
  137.6 18.0 %copy-start.1 = (bf16[1,64,36]{1,2,0:T(8,128)(2,1)S(1)}, bf16[1,64,36]{1,2,0:T(8,128)(2,1)}, u32[]{:S(2)}) copy-start(bf16[1,64,36]{1,2,0:T(8,128)(2,1)} %param.15) | copy-start | bytes 13828
  138.4 10.7 %copy-start.14 = (bf16[1152,36]{0,1:T(8,128)(2,1)S(1)}, bf16[1152,36]{0,1:T(8,128)(2,1)}, u32[]{:S(2)}) copy-start(bf16[1152,36]{0,1:T(8,128)(2,1)} %param.14) | copy-start | bytes 248836
  143.1 7.4 %collective-permute-start.27 = (f32[9,2304]{1,0:T(8,128)S(1)}, f32[9,2304]{1,0:T(8,128)S(1)}, u32[]{:S(2)}, u32[]{:S(2)}) collective-permute-start(f32[9,2304]{1,0:T(8,128)S(1)} %get-tuple-element.75), channel_id=1, source_target_pairs={{0,32},{32,64},{64,96},{96,0},{1,33},{33,65},{65,97},{97,1},{2,34}... | collective-permute-start | bytes 248840 | tf_op jit(solution)/shard_map/ppermute | solution.py:22
  145.1 7.9 %collective-permute-start.29 = (f32[9,2304]{1,0:T(8,128)S(1)}, f32[9,2304]{1,0:T(8,128)S(1)}, u32[]{:S(2)}, u32[]{:S(2)}) collective-permute-start(f32[9,2304]{1,0:T(8,128)S(1)} %get-tuple-element.76), channel_id=1, source_target_pairs={{0,96},{32,0},{64,32},{96,64},{1,97},{33,1},{65,33},{97,65},{2,98}... | collective-permute-start | bytes 248840 | tf_op jit(solution)/shard_map/ppermute | solution.py:22
  147.3 7.6 %collective-permute-start.28 = (f32[9,2304]{1,0:T(8,128)S(1)}, f32[9,2304]{1,0:T(8,128)S(1)}, u32[]{:S(2)}, u32[]{:S(2)}) collective-permute-start(f32[9,2304]{1,0:T(8,128)S(1)} %get-tuple-element.77), channel_id=1, source_target_pairs={{0,64},{32,96},{64,0},{96,32},{1,65},{33,97},{65,1},{97,33},{2,66}... | collective-permute-start | bytes 248840 | tf_op jit(solution)/shard_map/ppermute | solution.py:22

commit v3 on v2

--- a/solution.py
+++ b/solution.py
@@ -72,15 +72,18 @@
 
 
 def call(body, steps, ins, outs, scratch, flops, moved, name, room):
-    specs = [
-        pl.BlockSpec(b, m, pipeline_mode=pl.Buffered(1)) if m is whole_block else pl.BlockSpec(b, m)
-        for _, b, m in ins
-    ]
+    def spec(block, where, buffers):
+        if block is None:
+            return pl.BlockSpec(memory_space=pl.ANY)
+        if where is whole_block and buffers:
+            return pl.BlockSpec(block, where, pipeline_mode=pl.Buffered(buffers))
+        return pl.BlockSpec(block, where)
+
     return pl.pallas_call(
         body,
         grid=(steps,),
-        in_specs=specs,
-        out_specs=[pl.BlockSpec(b, m) for _, _, b, m in outs],
+        in_specs=[spec(b, m, 1) for _, b, m in ins],
+        out_specs=[spec(b, m, 0) for _, _, b, m in outs],
         out_shape=[jax.ShapeDtypeStruct(s, t) for s, t, _, _ in outs],
         scratch_shapes=scratch,
         compiler_params=pltpu.CompilerParams(vmem_limit_bytes=room * 2**20),
@@ -107,19 +110,27 @@
     nlat,
     x_ref,
     gain_ref,
-    wk_ref,
-    wv_ref,
-    wq_ref,
+    wk_far,
+    wv_far,
+    wq_far,
     lat_ref,
     n_ref,
     v_ref,
     e_ref,
     pack_ref,
-    sq_ref,
+    sq_far,
     s_all,
     n_all,
     acc_ref,
     state_ref,
+    wk_ref,
+    wv_ref,
+    wq_ref,
+    sq_ref,
+    wk_sem,
+    wv_sem,
+    wq_sem,
+    sq_sem,
 ):
     step, steps = pl.program_id(0), pl.num_programs(0) // 2
     at = pl.multiple_of((step % steps) * STEP, STEP)
@@ -128,11 +139,20 @@
     def valid(columns):
         return lax.broadcasted_iota(jnp.int32, (STEP, columns), 0) + at < rows
 
+    wk_copy = pltpu.make_async_copy(wk_far, wk_ref, wk_sem)
+    wv_copy = pltpu.make_async_copy(wv_far, wv_ref, wv_sem)
+    wq_copy = pltpu.make_async_copy(wq_far, wq_ref, wq_sem)
+    sq_copy = pltpu.make_async_copy(sq_ref, sq_far, sq_sem)
+
     @pl.when(step == 0)
     def _():
+        wq_copy.start()
+        wk_copy.start()
+        wv_copy.start()
         acc_ref[...] = jnp.zeros_like(acc_ref)
         row = lax.broadcasted_iota(jnp.int32, state_ref.shape, 0)
         state_ref[...] = jnp.where(row == 0, -jnp.inf, 0.0)
+        wq_copy.wait()
         twice = jnp.concatenate([lat_ref[...], lat_ref[...]], axis=0)
         query = dot(twice, wq_ref[...]).astype(BF16).astype(F32).T
         sq_ref[...] = jnp.zeros_like(sq_ref)
@@ -141,6 +161,8 @@
         for t in range(HEADS // 2):
             feat, cols = slice(2 * width * t, 2 * width * (t + 1)), slice(2 * nlat * t, 2 * nlat * (t + 1))
             sq_ref[feat, cols] = jnp.where(head_row == head_col, query[feat, :], 0.0).astype(BF16)
+        sq_copy.start()
+        wk_copy.wait()
 
     @pl.when(step < steps)
     def _():
@@ -161,6 +183,10 @@
                 state_ref[0:1, cols], jnp.max(s, axis=0, keepdims=True)
             )
 
+    @pl.when(step == steps)
+    def _():
+        wv_copy.wait()
+
     @pl.when(step >= steps)
     def _():
         values = dot(n_all[here, :], wv_ref[...]).astype(BF16)
@@ -184,6 +210,7 @@
                 out = out + jnp.where(lane == g, acc_ref[j, start : start + width, :], 0.0)
             pack_ref[:width, cols] = out
         pack_ref[width:, :] = state_ref[...]
+        sq_copy.wait()
 
 
 def grad_kernel(width, nlat, v_ref, sl_ref, e_ref, state_ref, t_ref, d_ref, keep_ref, send_ref):
@@ -263,9 +290,9 @@
         [
             (frames_1, (STEP, d), first),
             (gain, (d,), lambda i: (0,)),
-            (w_key, (d, d), whole_block),
-            (w_value, (d, d), whole_block),
-            (w_query, (d, d), whole_block),
+            (w_key, None, None),
+            (w_value, None, None),
+            (w_query, None, None),
             (latent_rows, (nlat, d), whole_block),
         ],
         [
@@ -273,13 +300,21 @@
             ((padded, d), BF16, (STEP, d), second),
             ((padded, cols), BF16, (STEP, cols), second),
             ((width + 8, cols), F32, (width + 8, cols), whole_block),
-            ((d, cols), BF16, (d, cols), whole_block),
+            ((d, cols), BF16, None, None),
         ],
         [
             pltpu.VMEM((padded, cols), F32),
             pltpu.VMEM((padded, d), BF16),
             pltpu.VMEM((HEADS // GROUP, WINDOW, GROUP * nlat), F32),
             pltpu.VMEM((8, cols), F32),
+            pltpu.VMEM((d, d), BF16),
+            pltpu.VMEM((d, d), BF16),
+            pltpu.VMEM((d, d), BF16),
+            pltpu.VMEM((d, cols), BF16),
+            pltpu.SemaphoreType.DMA,
+            pltpu.SemaphoreType.DMA,
+            pltpu.SemaphoreType.DMA,
+            pltpu.SemaphoreType.DMA,
         ],
         4 * padded * (d * d + WINDOW * cols),
         6 * padded * d + 2 * padded * cols + 2 * d * (2 * d + cols),

time: 156 us -> 154 us (0.987)
  transfers between devices with their start and end apart: 30 -> 30, of which waited for: 13 -> 13; matrix products, arithmetic and copies ran while one was open for 21% -> 21% of each run, Pallas kernels for 31% -> 30%
where the time goes in v3:
time: 154 us
  Pallas kernels  46.7 us (30%)
  starting transfers between devices  41.6 us (27%)
  matrix products  25.9 us (17%)
  waiting for transfers between devices  22.9 us (15%)
  other arithmetic  9.12 us (6%)
  local copies, waits for them, and re-layouts  6.72 us (4%)
    pallas_call x3, Pallas kernels, call(): pl.pallas_call(body, grid=(steps,), in_specs=[spec(b, m, 1) for _, b, m i...  44.5 us
    ppermute x30, starting transfers between devices, shift(): return lax.ppermute(value, axis, [(i, (i + step) % n) for i in range(n)])  41.6 us
    dot_general x9, matrix products, dot(): lax.dot_general(a, b, (((ca,), (cb,)), ((), ())), preferred_element_type=...  25.9 us
    ppermute x30, waiting for transfers between devices, shift(): return lax.ppermute(value, axis, [(i, (i + step) % n) for i in range(n)])  22.9 us
    add x1, other arithmetic, per_device(): after(u, w_send) * jnp.exp(top - top2) + u_got * jnp.exp(top_pair - top2)  3.4 us
    unnamed x40, local copies, waits for them, and re-layouts  3.27 us
  transfers between devices with their start and end apart: 30, of which 13 were waited for; matrix products, arithmetic and copies ran while one was open for 21% of the time, Pallas kernels for 30%

profile of v3, /device:TPU:0, one launch (start us, length us, event | category | flops | bytes accessed | tf_op | source)
XLA Modules:
  0.0 154.1 jit_solution(13057665022593035150)
XLA Ops:
  0.6 1.2 dot_general.29
  1.8 0.3 fusion.20
  2.5 1.4 collective-permute-done
  4.0 3.4 %collective-permute-start.2 = (f32[72,512]{1,0:T(8,128)S(1)}, f32[72,512]{1,0:T(8,128)S(1)}, u32[]{:S(2)}, u32[]{:S(2)}) collective-permute-start(f32[72,512]{1,0:T(8,128)S(1)} %dynamic-slice_add_fusion), channel_id=1, source_target_pairs={{0,16},{8,24},{16,0},{24,8},{1,17},{9,25},{17,1},{25,9},{2,18},{10... | collective-permute-start | bytes 442376 | tf_op jit(solution)/shard_map/ppermute | solution.py:22
  7.3 0.7 collective-permute-start.1
  8.0 2.6 %collective-permute-start.3 = (f32[72,512]{1,0:T(8,128)S(1)}, f32[72,512]{1,0:T(8,128)S(1)}, u32[]{:S(2)}, u32[]{:S(2)}) collective-permute-start(f32[72,512]{1,0:T(8,128)S(1)} %dynamic-slice_add_fusion), channel_id=1, source_target_pairs={{0,24},{8,0},{16,8},{24,16},{1,25},{9,1},{17,9},{25,17},{2,26},{10... | collective-permute-start | bytes 442376 | tf_op jit(solution)/shard_map/ppermute | solution.py:22
  10.6 22.9 %softmax.1 = (bf16[1536,1152]{1,0:T(8,128)(2,1)}, bf16[1536,1152]{1,0:T(8,128)(2,1)}, bf16[1536,1024]{1,0:T(8,128)(2,1)}, f32[80,1024]{1,0:T(8,128)}, bf16[1152,1024]{1,0:T(8,128)(2,1)}) custom-call(bf16[1458,1152]{1,0:T(8,128)(2,1)} %bitcast.86, bf16[1152]{0:T(1024)(128)(2,1)} %gain_ref.3, bf16[1152,1152]{1,0:T(8,128)(2,1)} %wk_far.1, ...), custom_call_target="tpu_custom_call" | custom-call | flops 10569646080 | bytes 21430272 | tf_op jit(solution)/shard_map/softmax/pallas_call | solution.py:82
  33.8 1.7 %collective-permute-done.4 = f32[80,1024]{1,0:T(8,128)S(1)} collective-permute-done((f32[80,1024]{1,0:T(8,128)}, f32[80,1024]{1,0:T(8,128)S(1)}, u32[]{:S(2)}, u32[]{:S(2)}) %collective-permute-start.4) | collective-permute-done | bytes 327712 | tf_op jit(solution)/shard_map/ppermute | solution.py:22
  35.5 0.8 subtract_exponential_fusion.5
  36.4 0.5 broadcast.417
  36.9 0.7 subtract_exponential_fusion.4
  37.7 1.0 fusion.19
  38.8 2.8 %collective-permute-start.7 = (f32[160,512]{1,0:T(8,128)S(1)}, f32[160,512]{1,0:T(8,128)S(1)}, u32[]{:S(2)}, u32[]{:S(2)}) collective-permute-start(f32[160,512]{1,0:T(8,128)S(1)} %pad_maximum_fusion), channel_id=1, source_target_pairs={{0,6},{2,0},{4,2},{6,4},{1,7},{3,1},{5,3},{7,5},{8,14},{10,8},{12,... | collective-permute-start | bytes 983048 | tf_op jit(solution)/shard_map/ppermute | solution.py:22
  41.6 0.8 collective-permute-start.6
  42.4 0.9 collective-permute-start.5
  43.3 7.8 %convolution_convert_fusion.t_ref = bf16[1280,1536]{1,0:T(8,128)(2,1)S(1)} fusion(bf16[1536,1152]{1,0:T(8,128)(2,1)} %get-tuple-element.34, s32[1280]{0:T(1024)S(1)} %fusion.44), kind=kOutput, calls=%fused_computation | convolution fusion | flops 4533288960 | bytes 7476224 | tf_op jit(solution)/shard_map/dot_general | solution.py:17
  51.2 4.5 %convolution_convert_fusion.2.qk_ref = bf16[1152,1024]{1,0:T(8,128)(2,1)} fusion(bf16[1152,1152]{1,0:T(8,128)(2,1)S(1)} %copy-done.15, bf16[1152,1024]{1,0:T(8,128)(2,1)S(1)} %copy-done.12), kind=kOutput, calls=%fused_computation.6 | convolution fusion | flops 2719088640 | bytes 7372800 | tf_op jit(solution)/shard_map/dot_general | solution.py:17
  55.9 3.7 %collective-permute-done.5 = f32[160,512]{1,0:T(8,128)S(1)} collective-permute-done((f32[160,512]{1,0:T(8,128)S(1)}, f32[160,512]{1,0:T(8,128)S(1)}, u32[]{:S(2)}, u32[]{:S(2)}) %collective-permute-start.5) | collective-permute-done | bytes 327712 | tf_op jit(solution)/shard_map/ppermute | solution.py:22
  59.8 1.5 collective-permute-start.10
  61.3 0.5 collective-permute-start.9
  61.8 3.7 %fusion.2 = f32[640,1024]{1,0:T(8,128)} fusion(bf16[1536,1024]{1,0:T(8,128)(2,1)S(1)} %copy-done.6, bf16[1280,1536]{1,0:T(8,128)(2,1)S(1)} %convolution_convert_fusion.t_ref), kind=kOutput, calls=%fused_computation.9 | convolution fusion | flops 2013265920 | bytes 7733248 | tf_op jit(solution)/shard_map/dot_general | solution.py:17
  65.6 0.6 collective-permute-start.8
  66.2 3.8 %fusion.4 = f32[640,1024]{1,0:T(8,128)} fusion(bf16[1536,1024]{1,0:T(8,128)(2,1)S(1)} %copy-done.6, bf16[1280,1536]{1,0:T(8,128)(2,1)S(1)} %convolution_convert_fusion.t_ref), kind=kOutput, calls=%fused_computation.11 | convolution fusion | flops 2013265920 | bytes 7733248 | tf_op jit(solution)/shard_map/dot_general | solution.py:17
  70.0 0.3 collective-permute-done.8
  70.3 0.5 fusion.sl_ref
  71.2 0.3 collective-permute-start.12
  71.5 1.1 collective-permute-done.12
  72.7 0.8 broadcast_multiply_fusion
  73.6 8.5 %gradient.1 = (bf16[1536,1024]{1,0:T(8,128)(2,1)S(1)}, f32[640,1024]{1,0:T(8,128)S(1)}, f32[640,1024]{1,0:T(8,128)}) custom-call(bf16[1536,1152]{1,0:T(8,128)(2,1)S(1)} %copy-done.8, bf16[1152,1024]{1,0:T(8,128)(2,1)S(1)} %fusion.sl_ref, bf16[1536,1024]{1,0:T(8,128)(2,1)S(1)} %copy-done.6, f32[8,1024]{1,0:T(8,128)S(1)} %maximum_maximum_fusion.state_ref, ...), custom_call_target="tpu_custom_call" | custom-call | flops 5234491392 | bytes 21233664 | tf_op jit(solution)/shard_map/gradient/pallas_call | solution.py:82
  82.1 1.5 copy-done.2
  83.7 1.6 %copy-done.9 = bf16[1536,1024]{1,0:T(8,128)(2,1)} copy-done((bf16[1536,1024]{1,0:T(8,128)(2,1)}, bf16[1536,1024]{1,0:T(8,128)(2,1)S(1)}, u32[]{:S(2)}) %copy-start.9) | copy-done | bytes 3145752
  85.8 0.4 copy.15
  86.2 0.3 convert_element_type.40
  86.5 3.4 %multiply_add_fusion = f32[640,1024]{1,0:T(8,128)S(1)} fusion(f32[640,1024]{1,0:T(8,128)} %collective-permute-done.20, f32[640,1024]{1,0:T(8,128)} %fusion.4, f32[1024]{0:T(1024)S(1)} %bitcast.105, f32[1024]{0:T(1024)S(1)} %bitcast.103), kind=kLoop, calls=%fused_computation.8 | loop fusion | flops 1966080 | bytes 7872512 | tf_op jit(solution)/shard_map/add | solution.py:377
  89.9 0.3 fusion.72
  90.2 0.7 collective-permute-start.23
  90.9 0.8 collective-permute-start.22
  91.7 0.8 collective-permute-start.21
  92.5 2.2 %split.1 = (f32[160,1024]{1,0:T(8,128)S(1)}, f32[160,1024]{1,0:T(8,128)S(1)}, f32[160,1024]{1,0:T(8,128)S(1)}, f32[160,1024]{1,0:T(8,128)S(1)}) custom-call(f32[640,1024]{1,0:T(8,128)S(1)} %copy-done.3, f32[640,1024]{1,0:T(8,128)} %collective-permute-done.13.got_ref), custom_call_target="tpu_custom_call" | custom-call | flops 655360 | bytes 7864320 | tf_op jit(solution)/shard_map/split/pallas_call | solution.py:381
  94.7 1.6 %collective-permute-start.14 = (f32[160,1024]{1,0:T(8,128)S(1)}, f32[160,1024]{1,0:T(8,128)S(1)}, u32[]{:S(2)}, u32[]{:S(2)}) collective-permute-start(f32[160,1024]{1,0:T(8,128)S(1)} %get-tuple-element.50), channel_id=1, source_target_pairs={{0,8},{8,16},{16,24},{24,0},{1,9},{9,17},{17,25},{25,1},{2,10},{10... | collective-permute-start | bytes 1966088 | tf_op jit(solution)/shard_map/ppermute | solution.py:22
  96.3 2.7 %collective-permute-start.15 = (f32[160,1024]{1,0:T(8,128)S(1)}, f32[160,1024]{1,0:T(8,128)S(1)}, u32[]{:S(2)}, u32[]{:S(2)}) collective-permute-start(f32[160,1024]{1,0:T(8,128)S(1)} %get-tuple-element.51), channel_id=1, source_target_pairs={{0,16},{8,24},{16,0},{24,8},{1,17},{9,25},{17,1},{25,9},{2,18},{10... | collective-permute-start | bytes 1966088 | tf_op jit(solution)/shard_map/ppermute | solution.py:22
  99.1 3.5 %convolution_convert_fusion.1.qv_ref = bf16[1152,1024]{1,0:T(8,128)(2,1)S(1)} fusion(bf16[1152,1152]{1,0:T(8,128)(2,1)S(1)} %copy-done.16, bf16[1152,1024]{1,0:T(8,128)(2,1)S(1)} %fusion.sl_ref), kind=kOutput, calls=%fused_computation.5 | convolution fusion | flops 2719088640 | bytes 7372800 | tf_op jit(solution)/shard_map/dot_general | solution.py:17
  102.5 5.3 %collective-permute-done.23 = f32[4,40,1024]{2,1,0:T(8,128)S(1)} collective-permute-done((f32[4,40,1024]{2,1,0:T(8,128)S(1)}, f32[4,40,1024]{2,1,0:T(8,128)S(1)}, u32[]{:S(2)}, u32[]{:S(2)}) %collective-permute-start.23) | collective-permute-done | bytes 655392 | tf_op jit(solution)/shard_map/ppermute | solution.py:22
  107.9 2.8 %collective-permute-start.16 = (f32[160,1024]{1,0:T(8,128)S(1)}, f32[160,1024]{1,0:T(8,128)S(1)}, u32[]{:S(2)}, u32[]{:S(2)}) collective-permute-start(f32[160,1024]{1,0:T(8,128)S(1)} %get-tuple-element.52), channel_id=1, source_target_pairs={{0,24},{8,0},{16,8},{24,16},{1,25},{9,1},{17,9},{25,17},{2,26},{10... | collective-permute-start | bytes 1966088 | tf_op jit(solution)/shard_map/ppermute | solution.py:22
  110.6 13.1 %back.1 = bf16[1458,1152]{1,0:T(8,128)(2,1)} custom-call(bf16[1536,1024]{1,0:T(8,128)(2,1)S(1)} %copy-done.10, bf16[1536,1024]{1,0:T(8,128)(2,1)S(1)} %copy-done.7, bf16[1152,1024]{1,0:T(8,128)(2,1)S(1)} %copy-done.11, bf16[1152,1024]{1,0:T(8,128)(2,1)S(1)} %convolution_convert_fusion.1.qv_ref, f32[8,1024]{1,0:T(8,128)S(1)} %maximum_maximum_fusion.state_ref, ...), custom_call_target="tpu_custom_call" | custom-call | flops 7247757312 | bytes 18087936 | tf_op jit(solution)/shard_map/back/pallas_call | solution.py:82
  123.7 0.3 add_multiply_fusion
  124.1 0.9 collective-permute-start.24
  124.9 2.5 %collective-permute-start.26 = (f32[40,1024]{1,0:T(8,128)S(1)}, f32[40,1024]{1,0:T(8,128)S(1)}, u32[]{:S(2)}, u32[]{:S(2)}) collective-permute-start(f32[40,1024]{1,0:T(8,128)S(1)} %get-tuple-element.73), channel_id=1, source_target_pairs={{0,24},{8,0},{16,8},{24,16},{1,25},{9,1},{17,9},{25,17},{2,26},{10... | collective-permute-start | bytes 491528 | tf_op jit(solution)/shard_map/ppermute | solution.py:22
  127.4 2.2 %collective-permute-start.25 = (f32[40,1024]{1,0:T(8,128)S(1)}, f32[40,1024]{1,0:T(8,128)S(1)}, u32[]{:S(2)}, u32[]{:S(2)}) collective-permute-start(f32[40,1024]{1,0:T(8,128)S(1)} %get-tuple-element.74), channel_id=1, source_target_pairs={{0,16},{8,24},{16,0},{24,8},{1,17},{9,25},{17,1},{25,9},{2,18},{10... | collective-permute-start | bytes 491528 | tf_op jit(solution)/shard_map/ppermute | solution.py:22
  129.8 2.0 %collective-permute-start.17 = (f32[40,1024]{1,0:T(8,128)S(1)}, f32[40,1024]{1,0:T(8,128)S(1)}, u32[]{:S(2)}, u32[]{:S(2)}) collective-permute-start(f32[40,1024]{1,0:T(8,128)S(1)} %get-tuple-element.69), channel_id=1, source_target_pairs={{0,2},{2,4},{4,6},{6,0},{1,3},{3,5},{5,7},{7,1},{8,10},{10,12},{12... | collective-permute-start | bytes 491528 | tf_op jit(solution)/shard_map/ppermute | solution.py:22
  131.9 1.3 collective-permute-start.19
  133.1 2.9 %collective-permute-start.18 = (f32[40,1024]{1,0:T(8,128)S(1)}, f32[40,1024]{1,0:T(8,128)S(1)}, u32[]{:S(2)}, u32[]{:S(2)}) collective-permute-start(f32[40,1024]{1,0:T(8,128)S(1)} %get-tuple-element.71), channel_id=1, source_target_pairs={{0,4},{2,6},{4,0},{6,2},{1,5},{3,7},{5,1},{7,3},{8,12},{10,14},{12... | collective-permute-start | bytes 491528 | tf_op jit(solution)/shard_map/ppermute | solution.py:22
  136.1 0.8 fusion.31
  136.9 1.4 collective-permute-done.19
  138.3 2.4 %collective-permute-done.18 = f32[40,1024]{1,0:T(8,128)S(1)} collective-permute-done((f32[40,1024]{1,0:T(8,128)S(1)}, f32[40,1024]{1,0:T(8,128)S(1)}, u32[]{:S(2)}, u32[]{:S(2)}) %collective-permute-start.18) | collective-permute-done | bytes 163872 | tf_op jit(solution)/shard_map/ppermute | solution.py:22
  140.8 0.8 fusion.29
  141.6 2.0 %collective-permute-start.27 = (f32[9,2304]{1,0:T(8,128)S(1)}, f32[9,2304]{1,0:T(8,128)S(1)}, u32[]{:S(2)}, u32[]{:S(2)}) collective-permute-start(f32[9,2304]{1,0:T(8,128)S(1)} %get-tuple-element.75), channel_id=1, source_target_pairs={{0,32},{32,64},{64,96},{96,0},{1,33},{33,65},{65,97},{97,1},{2,34}... | collective-permute-start | bytes 248840 | tf_op jit(solution)/shard_map/ppermute | solution.py:22
  143.6 2.2 %collective-permute-start.29 = (f32[9,2304]{1,0:T(8,128)S(1)}, f32[9,2304]{1,0:T(8,128)S(1)}, u32[]{:S(2)}, u32[]{:S(2)}) collective-permute-start(f32[9,2304]{1,0:T(8,128)S(1)} %get-tuple-element.76), channel_id=1, source_target_pairs={{0,96},{32,0},{64,32},{96,64},{1,97},{33,1},{65,33},{97,65},{2,98}... | collective-permute-start | bytes 248840 | tf_op jit(solution)/shard_map/ppermute | solution.py:22
  145.8 1.8 %collective-permute-start.28 = (f32[9,2304]{1,0:T(8,128)S(1)}, f32[9,2304]{1,0:T(8,128)S(1)}, u32[]{:S(2)}, u32[]{:S(2)}) collective-permute-start(f32[9,2304]{1,0:T(8,128)S(1)} %get-tuple-element.77), channel_id=1, source_target_pairs={{0,64},{32,96},{64,0},{96,32},{1,65},{33,97},{65,1},{97,33},{2,66}... | collective-permute-start | bytes 248840 | tf_op jit(solution)/shard_map/ppermute | solution.py:22
  147.6 0.8 fusion.6
  148.4 0.6 collective-permute-done.27
  149.0 2.5 %collective-permute-done.29 = f32[9,2304]{1,0:T(8,128)S(1)} collective-permute-done((f32[9,2304]{1,0:T(8,128)S(1)}, f32[9,2304]{1,0:T(8,128)S(1)}, u32[]{:S(2)}, u32[]{:S(2)}) %collective-permute-start.29) | collective-permute-done | bytes 82976 | tf_op jit(solution)/shard_map/ppermute | solution.py:22
  151.5 1.9 %collective-permute-done.28 = f32[9,2304]{1,0:T(8,128)S(1)} collective-permute-done((f32[9,2304]{1,0:T(8,128)S(1)}, f32[9,2304]{1,0:T(8,128)S(1)}, u32[]{:S(2)}, u32[]{:S(2)}) %collective-permute-start.28) | collective-permute-done | bytes 82976 | tf_op jit(solution)/shard_map/ppermute | solution.py:22
  153.4 0.7 fusion.26
  (99 shorter events, 2.8 us)
Async XLA Ops:
  0.6 1.2 copy-start
  2.3 1.7 %collective-permute-start = (f32[72,1024]{1,0:T(8,128)S(1)}, f32[72,1024]{1,0:T(8,128)S(1)}, u32[]{:S(2)}, u32[]{:S(2)}) collective-permute-start(f32[72,1024]{1,0:T(8,128)S(1)} %copy.16), channel_id=1, source_target_pairs={{0,1},{1,0},{2,3},{3,2},{4,5},{5,4},{6,7},{7,6},{8,9},{9,8},{10,11... | collective-permute-start | bytes 884744 | tf_op jit(solution)/shard_map/ppermute | solution.py:22
  4.0 29.5 %collective-permute-start.2 = (f32[72,512]{1,0:T(8,128)S(1)}, f32[72,512]{1,0:T(8,128)S(1)}, u32[]{:S(2)}, u32[]{:S(2)}) collective-permute-start(f32[72,512]{1,0:T(8,128)S(1)} %dynamic-slice_add_fusion), channel_id=1, source_target_pairs={{0,16},{8,24},{16,0},{24,8},{1,17},{9,25},{17,1},{25,9},{2,18},{10... | collective-permute-start | bytes 442376 | tf_op jit(solution)/shard_map/ppermute | solution.py:22
  7.3 26.2 %collective-permute-start.1 = (f32[72,512]{1,0:T(8,128)S(1)}, f32[72,512]{1,0:T(8,128)S(1)}, u32[]{:S(2)}, u32[]{:S(2)}) collective-permute-start(f32[72,512]{1,0:T(8,128)S(1)} %dynamic-slice_add_fusion), channel_id=1, source_target_pairs={{0,8},{8,16},{16,24},{24,0},{1,9},{9,17},{17,25},{25,1},{2,10},{10... | collective-permute-start | bytes 442376 | tf_op jit(solution)/shard_map/ppermute | solution.py:22
  8.0 25.5 %collective-permute-start.3 = (f32[72,512]{1,0:T(8,128)S(1)}, f32[72,512]{1,0:T(8,128)S(1)}, u32[]{:S(2)}, u32[]{:S(2)}) collective-permute-start(f32[72,512]{1,0:T(8,128)S(1)} %dynamic-slice_add_fusion), channel_id=1, source_target_pairs={{0,24},{8,0},{16,8},{24,16},{1,25},{9,1},{17,9},{25,17},{2,26},{10... | collective-permute-start | bytes 442376 | tf_op jit(solution)/shard_map/ppermute | solution.py:22
  33.6 1.9 %collective-permute-start.4 = (f32[80,1024]{1,0:T(8,128)}, f32[80,1024]{1,0:T(8,128)S(1)}, u32[]{:S(2)}, u32[]{:S(2)}) collective-permute-start(f32[80,1024]{1,0:T(8,128)} %get-tuple-element.32), channel_id=1, source_target_pairs={{0,1},{1,0},{2,3},{3,2},{4,5},{5,4},{6,7},{7,6},{8,9},{9,8},{10,11... | collective-permute-start | bytes 983048 | tf_op jit(solution)/shard_map/ppermute | solution.py:22
  38.8 17.1 %collective-permute-start.7 = (f32[160,512]{1,0:T(8,128)S(1)}, f32[160,512]{1,0:T(8,128)S(1)}, u32[]{:S(2)}, u32[]{:S(2)}) collective-permute-start(f32[160,512]{1,0:T(8,128)S(1)} %pad_maximum_fusion), channel_id=1, source_target_pairs={{0,6},{2,0},{4,2},{6,4},{1,7},{3,1},{5,3},{7,5},{8,14},{10,8},{12,... | collective-permute-start | bytes 983048 | tf_op jit(solution)/shard_map/ppermute | solution.py:22
  41.6 14.3 %collective-permute-start.6 = (f32[160,512]{1,0:T(8,128)S(1)}, f32[160,512]{1,0:T(8,128)S(1)}, u32[]{:S(2)}, u32[]{:S(2)}) collective-permute-start(f32[160,512]{1,0:T(8,128)S(1)} %pad_maximum_fusion), channel_id=1, source_target_pairs={{0,4},{2,6},{4,0},{6,2},{1,5},{3,7},{5,1},{7,3},{8,12},{10,14},{12... | collective-permute-start | bytes 983048 | tf_op jit(solution)/shard_map/ppermute | solution.py:22
  42.4 17.2 %collective-permute-start.5 = (f32[160,512]{1,0:T(8,128)S(1)}, f32[160,512]{1,0:T(8,128)S(1)}, u32[]{:S(2)}, u32[]{:S(2)}) collective-permute-start(f32[160,512]{1,0:T(8,128)S(1)} %pad_maximum_fusion), channel_id=1, source_target_pairs={{0,2},{2,4},{4,6},{6,0},{1,3},{3,5},{5,7},{7,1},{8,10},{10,12},{12... | collective-permute-start | bytes 983048 | tf_op jit(solution)/shard_map/ppermute | solution.py:22
  43.3 7.8 %copy-start.12 = (bf16[1152,1024]{1,0:T(8,128)(2,1)S(1)}, bf16[1152,1024]{1,0:T(8,128)(2,1)}, u32[]{:S(2)}) copy-start(bf16[1152,1024]{1,0:T(8,128)(2,1)} %get-tuple-element.36) | copy-start | bytes 7077892
  43.3 7.8 %copy-start.15 = (bf16[1152,1152]{1,0:T(8,128)(2,1)S(1)}, bf16[1152,1152]{1,0:T(8,128)(2,1)}, u32[]{:S(2)}) copy-start(bf16[1152,1152]{1,0:T(8,128)(2,1)} %wk_far.1) | copy-start | bytes 7962628
  51.1 10.7 %copy-start.6 = (bf16[1536,1024]{1,0:T(8,128)(2,1)S(1)}, bf16[1536,1024]{1,0:T(8,128)(2,1)}, u32[]{:S(2)}) copy-start(bf16[1536,1024]{1,0:T(8,128)(2,1)} %get-tuple-element.40.e_ref) | copy-start | bytes 9437188
  59.7 11.1 %collective-permute-start.11 = (f32[80,512]{1,0:T(8,128)S(1)}, f32[80,512]{1,0:T(8,128)S(1)}, u32[]{:S(2)}, u32[]{:S(2)}) collective-permute-start(f32[80,512]{1,0:T(8,128)S(1)} %fusion.15), channel_id=1, source_target_pairs={{0,24},{8,0},{16,8},{24,16},{1,25},{9,1},{17,9},{25,17},{2,26},{10... | collective-permute-start | bytes 491528 | tf_op jit(solution)/shard_map/ppermute | solution.py:22
  59.8 11.0 %collective-permute-start.10 = (f32[80,512]{1,0:T(8,128)S(1)}, f32[80,512]{1,0:T(8,128)S(1)}, u32[]{:S(2)}, u32[]{:S(2)}) collective-permute-start(f32[80,512]{1,0:T(8,128)S(1)} %fusion.15), channel_id=1, source_target_pairs={{0,16},{8,24},{16,0},{24,8},{1,17},{9,25},{17,1},{25,9},{2,18},{10... | collective-permute-start | bytes 491528 | tf_op jit(solution)/shard_map/ppermute | solution.py:22
  61.3 9.7 %collective-permute-start.9 = (f32[80,512]{1,0:T(8,128)S(1)}, f32[80,512]{1,0:T(8,128)S(1)}, u32[]{:S(2)}, u32[]{:S(2)}) collective-permute-start(f32[80,512]{1,0:T(8,128)S(1)} %fusion.15), channel_id=1, source_target_pairs={{0,8},{8,16},{16,24},{24,0},{1,9},{9,17},{17,25},{25,1},{2,10},{10... | collective-permute-start | bytes 491528 | tf_op jit(solution)/shard_map/ppermute | solution.py:22
  65.5 21.0 %collective-permute-start.20 = (f32[640,1024]{1,0:T(8,128)}, f32[640,1024]{1,0:T(8,128)}, u32[]{:S(2)}, u32[]{:S(2)}) collective-permute-start(f32[640,1024]{1,0:T(8,128)} %fusion.2), channel_id=1, source_target_pairs={{0,1},{1,0},{2,3},{3,2},{4,5},{5,4},{6,7},{7,6},{8,9},{9,8},{10,11... | collective-permute-start | bytes 7864328 | tf_op jit(solution)/shard_map/ppermute | solution.py:22
  65.6 4.7 %collective-permute-start.8 = (f32[72,512]{1,0:T(8,128)S(1)}, f32[72,512]{1,0:T(8,128)S(1)}, u32[]{:S(2)}, u32[]{:S(2)}) collective-permute-start(f32[72,512]{1,0:T(8,128)S(1)} %slice_add_fusion.1), channel_id=1, source_target_pairs={{0,1},{1,0},{2,3},{3,2},{4,5},{5,4},{6,7},{7,6},{8,9},{9,8},{10,11... | collective-permute-start | bytes 442376 | tf_op jit(solution)/shard_map/ppermute | solution.py:22
  70.3 3.3 %copy-start.8 = (bf16[1536,1152]{1,0:T(8,128)(2,1)S(1)}, bf16[1536,1152]{1,0:T(8,128)(2,1)}, u32[]{:S(2)}) copy-start(bf16[1536,1152]{1,0:T(8,128)(2,1)} %get-tuple-element.42.v_ref) | copy-start | bytes 10616836
  71.2 1.5 collective-permute-start.12
  82.1 1.5 copy-start.2
  83.7 1.6 %copy-start.9 = (bf16[1536,1024]{1,0:T(8,128)(2,1)}, bf16[1536,1024]{1,0:T(8,128)(2,1)S(1)}, u32[]{:S(2)}) copy-start(bf16[1536,1024]{1,0:T(8,128)(2,1)S(1)} %get-tuple-element.47.d_ref) | copy-start | bytes 9437188
  85.3 7.2 %collective-permute-start.13 = (f32[640,1024]{1,0:T(8,128)}, f32[640,1024]{1,0:T(8,128)}, u32[]{:S(2)}, u32[]{:S(2)}) collective-permute-start(f32[640,1024]{1,0:T(8,128)} %get-tuple-element.45), channel_id=1, source_target_pairs={{0,1},{1,0},{2,3},{3,2},{4,5},{5,4},{6,7},{7,6},{8,9},{9,8},{10,11... | collective-permute-start | bytes 7864328 | tf_op jit(solution)/shard_map/ppermute | solution.py:22
  89.9 2.6 %copy-start.3 = (f32[640,1024]{1,0:T(8,128)S(1)}, f32[640,1024]{1,0:T(8,128)}, u32[]{:S(2)}) copy-start(f32[640,1024]{1,0:T(8,128)} %copy-done.2) | copy-start | bytes 7864324
  90.2 17.6 %collective-permute-start.23 = (f32[4,40,1024]{2,1,0:T(8,128)S(1)}, f32[4,40,1024]{2,1,0:T(8,128)S(1)}, u32[]{:S(2)}, u32[]{:S(2)}) collective-permute-start(f32[4,40,1024]{2,1,0:T(8,128)S(1)} %bitcast.93), channel_id=1, source_target_pairs={{0,6},{2,0},{4,2},{6,4},{1,7},{3,1},{5,3},{7,5},{8,14},{10,8},{12,... | collective-permute-start | bytes 1966088 | tf_op jit(solution)/shard_map/ppermute | solution.py:22
  90.9 32.8 %collective-permute-start.22 = (f32[4,40,1024]{2,1,0:T(8,128)S(1)}, f32[4,40,1024]{2,1,0:T(8,128)S(1)}, u32[]{:S(2)}, u32[]{:S(2)}) collective-permute-start(f32[4,40,1024]{2,1,0:T(8,128)S(1)} %bitcast.92), channel_id=1, source_target_pairs={{0,4},{2,6},{4,0},{6,2},{1,5},{3,7},{5,1},{7,3},{8,12},{10,14},{12... | collective-permute-start | bytes 1966088 | tf_op jit(solution)/shard_map/ppermute | solution.py:22
  91.7 32.0 %collective-permute-start.21 = (f32[4,40,1024]{2,1,0:T(8,128)S(1)}, f32[4,40,1024]{2,1,0:T(8,128)S(1)}, u32[]{:S(2)}, u32[]{:S(2)}) collective-permute-start(f32[4,40,1024]{2,1,0:T(8,128)S(1)} %bitcast.91), channel_id=1, source_target_pairs={{0,2},{2,4},{4,6},{6,0},{1,3},{3,5},{5,7},{7,1},{8,10},{10,12},{12... | collective-permute-start | bytes 1966088 | tf_op jit(solution)/shard_map/ppermute | solution.py:22
  92.5 6.5 %copy-start.16 = (bf16[1152,1152]{1,0:T(8,128)(2,1)S(1)}, bf16[1152,1152]{1,0:T(8,128)(2,1)}, u32[]{:S(2)}) copy-start(bf16[1152,1152]{1,0:T(8,128)(2,1)} %wv_far.1) | copy-start | bytes 7962628
  94.7 32.7 %collective-permute-start.14 = (f32[160,1024]{1,0:T(8,128)S(1)}, f32[160,1024]{1,0:T(8,128)S(1)}, u32[]{:S(2)}, u32[]{:S(2)}) collective-permute-start(f32[160,1024]{1,0:T(8,128)S(1)} %get-tuple-element.50), channel_id=1, source_target_pairs={{0,8},{8,16},{16,24},{24,0},{1,9},{9,17},{17,25},{25,1},{2,10},{10... | collective-permute-start | bytes 1966088 | tf_op jit(solution)/shard_map/ppermute | solution.py:22
  96.3 14.3 %copy-start.4 = (bf16[1,1458,1152]{2,1,0:T(8,128)(2,1)S(1)}, bf16[1,1458,1152]{2,1,0:T(8,128)(2,1)}, u32[]{:S(2)}) copy-start(bf16[1,1458,1152]{2,1,0:T(8,128)(2,1)} %param.8) | copy-start | bytes 10077700
  96.3 14.3 %copy-start.5 = (bf16[1152]{0:T(1024)(128)(2,1)S(1)}, bf16[1152]{0:T(1024)(128)(2,1)}, u32[]{:S(2)}) copy-start(bf16[1152]{0:T(1024)(128)(2,1)} %gain_ref.3) | copy-start | bytes 6916
  96.3 14.3 %copy-start.7 = (bf16[1536,1024]{1,0:T(8,128)(2,1)S(1)}, bf16[1536,1024]{1,0:T(8,128)(2,1)}, u32[]{:S(2)}) copy-start(bf16[1536,1024]{1,0:T(8,128)(2,1)} %get-tuple-element.40.e_ref) | copy-start | bytes 9437188
  96.3 14.3 %copy-start.10 = (bf16[1536,1024]{1,0:T(8,128)(2,1)S(1)}, bf16[1536,1024]{1,0:T(8,128)(2,1)}, u32[]{:S(2)}) copy-start(bf16[1536,1024]{1,0:T(8,128)(2,1)} %copy-done.9) | copy-start | bytes 9437188
  96.3 14.3 %copy-start.11 = (bf16[1152,1024]{1,0:T(8,128)(2,1)S(1)}, bf16[1152,1024]{1,0:T(8,128)(2,1)}, u32[]{:S(2)}) copy-start(bf16[1152,1024]{1,0:T(8,128)(2,1)} %convolution_convert_fusion.2.qk_ref) | copy-start | bytes 7077892
  96.3 33.2 %collective-permute-start.15 = (f32[160,1024]{1,0:T(8,128)S(1)}, f32[160,1024]{1,0:T(8,128)S(1)}, u32[]{:S(2)}, u32[]{:S(2)}) collective-permute-start(f32[160,1024]{1,0:T(8,128)S(1)} %get-tuple-element.51), channel_id=1, source_target_pairs={{0,16},{8,24},{16,0},{24,8},{1,17},{9,25},{17,1},{25,9},{2,18},{10... | collective-permute-start | bytes 1966088 | tf_op jit(solution)/shard_map/ppermute | solution.py:22
  107.9 21.7 %collective-permute-start.16 = (f32[160,1024]{1,0:T(8,128)S(1)}, f32[160,1024]{1,0:T(8,128)S(1)}, u32[]{:S(2)}, u32[]{:S(2)}) collective-permute-start(f32[160,1024]{1,0:T(8,128)S(1)} %get-tuple-element.52), channel_id=1, source_target_pairs={{0,24},{8,0},{16,8},{24,16},{1,25},{9,1},{17,9},{25,17},{2,26},{10... | collective-permute-start | bytes 1966088 | tf_op jit(solution)/shard_map/ppermute | solution.py:22
  124.1 9.1 %collective-permute-start.24 = (f32[40,1024]{1,0:T(8,128)S(1)}, f32[40,1024]{1,0:T(8,128)S(1)}, u32[]{:S(2)}, u32[]{:S(2)}) collective-permute-start(f32[40,1024]{1,0:T(8,128)S(1)} %get-tuple-element.72), channel_id=1, source_target_pairs={{0,8},{8,16},{16,24},{24,0},{1,9},{9,17},{17,25},{25,1},{2,10},{10... | collective-permute-start | bytes 491528 | tf_op jit(solution)/shard_map/ppermute | solution.py:22
  124.9 11.2 %collective-permute-start.26 = (f32[40,1024]{1,0:T(8,128)S(1)}, f32[40,1024]{1,0:T(8,128)S(1)}, u32[]{:S(2)}, u32[]{:S(2)}) collective-permute-start(f32[40,1024]{1,0:T(8,128)S(1)} %get-tuple-element.73), channel_id=1, source_target_pairs={{0,24},{8,0},{16,8},{24,16},{1,25},{9,1},{17,9},{25,17},{2,26},{10... | collective-permute-start | bytes 491528 | tf_op jit(solution)/shard_map/ppermute | solution.py:22
  127.4 8.7 %collective-permute-start.25 = (f32[40,1024]{1,0:T(8,128)S(1)}, f32[40,1024]{1,0:T(8,128)S(1)}, u32[]{:S(2)}, u32[]{:S(2)}) collective-permute-start(f32[40,1024]{1,0:T(8,128)S(1)} %get-tuple-element.74), channel_id=1, source_target_pairs={{0,16},{8,24},{16,0},{24,8},{1,17},{9,25},{17,1},{25,9},{2,18},{10... | collective-permute-start | bytes 491528 | tf_op jit(solution)/shard_map/ppermute | solution.py:22
  129.8 11.0 %copy-start.13 = (bf16[1152,1024]{1,0:T(8,128)(2,1)S(1)}, bf16[1152,1024]{1,0:T(8,128)(2,1)}, u32[]{:S(2)}) copy-start(bf16[1152,1024]{1,0:T(8,128)(2,1)} %get-tuple-element.36) | copy-start | bytes 7077892
  129.8 7.1 %collective-permute-start.17 = (f32[40,1024]{1,0:T(8,128)S(1)}, f32[40,1024]{1,0:T(8,128)S(1)}, u32[]{:S(2)}, u32[]{:S(2)}) collective-permute-start(f32[40,1024]{1,0:T(8,128)S(1)} %get-tuple-element.69), channel_id=1, source_target_pairs={{0,2},{2,4},{4,6},{6,0},{1,3},{3,5},{5,7},{7,1},{8,10},{10,12},{12... | collective-permute-start | bytes 491528 | tf_op jit(solution)/shard_map/ppermute | solution.py:22
  131.9 6.5 %collective-permute-start.19 = (f32[40,1024]{1,0:T(8,128)S(1)}, f32[40,1024]{1,0:T(8,128)S(1)}, u32[]{:S(2)}, u32[]{:S(2)}) collective-permute-start(f32[40,1024]{1,0:T(8,128)S(1)} %get-tuple-element.70), channel_id=1, source_target_pairs={{0,6},{2,0},{4,2},{6,4},{1,7},{3,1},{5,3},{7,5},{8,14},{10,8},{12,... | collective-permute-start | bytes 491528 | tf_op jit(solution)/shard_map/ppermute | solution.py:22
  133.1 7.6 %collective-permute-start.18 = (f32[40,1024]{1,0:T(8,128)S(1)}, f32[40,1024]{1,0:T(8,128)S(1)}, u32[]{:S(2)}, u32[]{:S(2)}) collective-permute-start(f32[40,1024]{1,0:T(8,128)S(1)} %get-tuple-element.71), channel_id=1, source_target_pairs={{0,4},{2,6},{4,0},{6,2},{1,5},{3,7},{5,1},{7,3},{8,12},{10,14},{12... | collective-permute-start | bytes 491528 | tf_op jit(solution)/shard_map/ppermute | solution.py:22
  136.1 18.0 %copy-start.1 = (bf16[1,64,36]{1,2,0:T(8,128)(2,1)S(1)}, bf16[1,64,36]{1,2,0:T(8,128)(2,1)}, u32[]{:S(2)}) copy-start(bf16[1,64,36]{1,2,0:T(8,128)(2,1)} %param.15) | copy-start | bytes 13828
  136.9 10.7 %copy-start.14 = (bf16[1152,36]{0,1:T(8,128)(2,1)S(1)}, bf16[1152,36]{0,1:T(8,128)(2,1)}, u32[]{:S(2)}) copy-start(bf16[1152,36]{0,1:T(8,128)(2,1)} %param.14) | copy-start | bytes 248836
  141.6 7.4 %collective-permute-start.27 = (f32[9,2304]{1,0:T(8,128)S(1)}, f32[9,2304]{1,0:T(8,128)S(1)}, u32[]{:S(2)}, u32[]{:S(2)}) collective-permute-start(f32[9,2304]{1,0:T(8,128)S(1)} %get-tuple-element.75), channel_id=1, source_target_pairs={{0,32},{32,64},{64,96},{96,0},{1,33},{33,65},{65,97},{97,1},{2,34}... | collective-permute-start | bytes 248840 | tf_op jit(solution)/shard_map/ppermute | solution.py:22
  143.6 7.9 %collective-permute-start.29 = (f32[9,2304]{1,0:T(8,128)S(1)}, f32[9,2304]{1,0:T(8,128)S(1)}, u32[]{:S(2)}, u32[]{:S(2)}) collective-permute-start(f32[9,2304]{1,0:T(8,128)S(1)} %get-tuple-element.76), channel_id=1, source_target_pairs={{0,96},{32,0},{64,32},{96,64},{1,97},{33,1},{65,33},{97,65},{2,98}... | collective-permute-start | bytes 248840 | tf_op jit(solution)/shard_map/ppermute | solution.py:22
  145.8 7.6 %collective-permute-start.28 = (f32[9,2304]{1,0:T(8,128)S(1)}, f32[9,2304]{1,0:T(8,128)S(1)}, u32[]{:S(2)}, u32[]{:S(2)}) collective-permute-start(f32[9,2304]{1,0:T(8,128)S(1)} %get-tuple-element.77), channel_id=1, source_target_pairs={{0,64},{32,96},{64,0},{96,32},{1,65},{33,97},{65,1},{97,33},{2,66}... | collective-permute-start | bytes 248840 | tf_op jit(solution)/shard_map/ppermute | solution.py:22

commit v4 on v3

--- a/solution.py
+++ b/solution.py
@@ -173,11 +173,11 @@
         normed = jnp.where(valid(x.shape[1]), normed, 0.0).astype(BF16)
         n_ref[...] = normed
         keys = dot(normed, wk_ref[...]).astype(BF16)
+        unused = jnp.where(valid(1), 0.0, -jnp.inf)
         n_all[here, :] = normed
         for j in range(HEADS // GROUP):
             feat, cols = group(j, width, nlat)
-            s = dot(keys[:, feat], sq_ref[feat, cols]) * (1.0 / width**0.5)
-            s = jnp.where(valid(s.shape[1]), s, -jnp.inf)
+            s = dot(keys[:, feat], sq_ref[feat, cols]) * (1.0 / width**0.5) + unused
             s_all[here, cols] = s
             state_ref[0:1, cols] = jnp.maximum(
                 state_ref[0:1, cols], jnp.max(s, axis=0, keepdims=True)
@@ -243,6 +243,21 @@
     mean = jnp.mean(dxhat, axis=-1, keepdims=True)
     slope = jnp.mean(dxhat * xhat, axis=-1, keepdims=True)
     out_ref[...] = ((dxhat - mean - xhat * slope) * rstd).astype(BF16)
+
+
+def pair_kernel(width, core_ref, own_ref, got_ref, lc_ref, out_ref):
+    cut = out_ref.shape[1]
+    top = jnp.maximum(own_ref[width : width + 1, :], got_ref[width : width + 1, :])
+    here = pl.ds(pl.multiple_of(core_ref[0] * cut, cut), cut)
+    own, got = own_ref[:, here], got_ref[:, here]
+    own_top, got_top = own[width : width + 1, :], got[width : width + 1, :]
+    best = jnp.maximum(own_top, got_top)
+    both = own * jnp.exp(own_top - best) + got * jnp.exp(got_top - best)
+    row = lax.broadcasted_iota(jnp.int32, both.shape, 0)
+    out_ref[: width + 8, :] = jnp.where(row == width, best, both)
+    row = lax.broadcasted_iota(jnp.int32, (8, cut), 0)
+    out_ref[width + 8 : width + 16, :] = jnp.where(row % 2 == 0, top[:, :cut], top[:, cut:])
+    out_ref[width + 16 :, :] = lc_ref[...]
 
 
 def split_kernel(keep_ref, got_ref, *outs):
@@ -326,10 +341,17 @@
     paired = shift(pack, "c", 1)
     top, top_pair = pack[width : width + 1], paired[width : width + 1]
     top2 = jnp.maximum(top, top_pair)
-    half = own_half(merge([pack, paired], width))
+    vmem = pl.BlockSpec(memory_space=pltpu.VMEM)
+    half = pl.pallas_call(
+        functools.partial(pair_kernel, width),
+        in_specs=[pl.BlockSpec(memory_space=pltpu.SMEM), vmem, vmem, vmem],
+        out_specs=vmem,
+        out_shape=jax.ShapeDtypeStruct((2 * width + 16, cols // 2), F32),
+        compiler_params=pltpu.CompilerParams(vmem_limit_bytes=16 * 2**20),
+        name="pair",
+    )(core.astype(jnp.int32).reshape(1), pack, paired, lc)
 
     turned = dot(chosen_rows(d), after(normed, half), 1, 1).astype(BF16)
-    half = jnp.concatenate([half, jnp.tile(top2.reshape(2, cols // 2), (4, 1)), lc], axis=0)
     halves = [half] + [shift(half, "x", k) for k in (1, 2, 3)]
     tops = [h[width + 8 : width + 10].reshape(1, cols) for h in halves]
     top3 = jnp.maximum(jnp.maximum(tops[0], tops[1]), jnp.maximum(tops[2], tops[3]))

time: 154 us -> 152 us (0.987)
  other arithmetic: 9.12 us -> 6.38 us
    unnamed x40 -> x41, local copies, waits for them, and re-layouts: 3.27 us -> 4.23 us
  transfers between devices with their start and end apart: 30 -> 30, of which waited for: 13 -> 13; matrix products, arithmetic and copies ran while one was open for 21% -> 21% of each run, Pallas kernels for 30% -> 31%
where the time goes in v4:
time: 152 us
  Pallas kernels  47.1 us (31%)
  starting transfers between devices  41.8 us (28%)
  matrix products  25.9 us (17%)
  waiting for transfers between devices  22.9 us (15%)
  local copies, waits for them, and re-layouts  6.92 us (5%)
  other arithmetic  6.38 us (4%)
    pallas_call x3, Pallas kernels, call(): pl.pallas_call(body, grid=(steps,), in_specs=[spec(b, m, 1) for _, b, m i...  44.9 us
    ppermute x30, starting transfers between devices, shift(): return lax.ppermute(value, axis, [(i, (i + step) % n) for i in range(n)])  41.8 us
    dot_general x9, matrix products, dot(): lax.dot_general(a, b, (((ca,), (cb,)), ((), ())), preferred_element_type=...  25.9 us
    ppermute x30, waiting for transfers between devices, shift(): return lax.ppermute(value, axis, [(i, (i + step) % n) for i in range(n)])  22.9 us
    unnamed x41, local copies, waits for them, and re-layouts  4.23 us
    add x1, other arithmetic, per_device(): after(u, w_send) * jnp.exp(top - top2) + u_got * jnp.exp(top_pair - top2)  3.16 us
  transfers between devices with their start and end apart: 30, of which 13 were waited for; matrix products, arithmetic and copies ran while one was open for 21% of the time, Pallas kernels for 31%

profile of v4, /device:TPU:0, one launch (start us, length us, event | category | flops | bytes accessed | tf_op | source)
XLA Modules:
  0.0 152.1 jit_solution(2195741406883814983)
XLA Ops:
  0.6 1.2 dot_general.29
  1.8 0.3 fusion.18
  2.5 1.4 collective-permute-done
  4.0 3.4 %collective-permute-start.2 = (f32[72,512]{1,0:T(8,128)S(1)}, f32[72,512]{1,0:T(8,128)S(1)}, u32[]{:S(2)}, u32[]{:S(2)}) collective-permute-start(f32[72,512]{1,0:T(8,128)S(1)} %dynamic-slice_add_fusion), channel_id=1, source_target_pairs={{0,16},{8,24},{16,0},{24,8},{1,17},{9,25},{17,1},{25,9},{2,18},{10... | collective-permute-start | bytes 442376 | tf_op jit(solution)/shard_map/ppermute | solution.py:22
  7.3 0.7 collective-permute-start.1
  8.0 2.6 %collective-permute-start.3 = (f32[72,512]{1,0:T(8,128)S(1)}, f32[72,512]{1,0:T(8,128)S(1)}, u32[]{:S(2)}, u32[]{:S(2)}) collective-permute-start(f32[72,512]{1,0:T(8,128)S(1)} %dynamic-slice_add_fusion), channel_id=1, source_target_pairs={{0,24},{8,0},{16,8},{24,16},{1,25},{9,1},{17,9},{25,17},{2,26},{10... | collective-permute-start | bytes 442376 | tf_op jit(solution)/shard_map/ppermute | solution.py:22
  10.6 23.2 %softmax.1 = (bf16[1536,1152]{1,0:T(8,128)(2,1)}, bf16[1536,1152]{1,0:T(8,128)(2,1)}, bf16[1536,1024]{1,0:T(8,128)(2,1)}, f32[80,1024]{1,0:T(8,128)}, bf16[1152,1024]{1,0:T(8,128)(2,1)}) custom-call(bf16[1458,1152]{1,0:T(8,128)(2,1)} %bitcast.85, bf16[1152]{0:T(1024)(128)(2,1)} %gain_ref.3, bf16[1152,1152]{1,0:T(8,128)(2,1)} %wk_far.1, ...), custom_call_target="tpu_custom_call" | custom-call | flops 10569646080 | bytes 21430272 | tf_op jit(solution)/shard_map/softmax/pallas_call | solution.py:82
  34.0 1.7 %collective-permute-done.4.got_ref = f32[80,1024]{1,0:T(8,128)S(1)} collective-permute-done((f32[80,1024]{1,0:T(8,128)}, f32[80,1024]{1,0:T(8,128)S(1)}, u32[]{:S(2)}, u32[]{:S(2)}) %collective-permute-start.4) | collective-permute-done | bytes 327712 | tf_op jit(solution)/shard_map/ppermute | solution.py:22
  35.8 1.0 copy-done.4
  36.8 2.8 %collective-permute-start.7 = (f32[160,512]{1,0:T(8,128)S(1)}, f32[160,512]{1,0:T(8,128)S(1)}, u32[]{:S(2)}, u32[]{:S(2)}) collective-permute-start(f32[160,512]{1,0:T(8,128)S(1)} %pair.1), channel_id=1, source_target_pairs={{0,6},{2,0},{4,2},{6,4},{1,7},{3,1},{5,3},{7,5},{8,14},{10,8},{12,... | collective-permute-start | bytes 983048 | tf_op jit(solution)/shard_map/ppermute | solution.py:22
  39.6 0.8 collective-permute-start.6
  40.4 0.9 collective-permute-start.5
  41.3 7.8 %convolution_convert_fusion.t_ref = bf16[1280,1536]{1,0:T(8,128)(2,1)S(1)} fusion(bf16[1536,1152]{1,0:T(8,128)(2,1)} %get-tuple-element.34, s32[1280]{0:T(1024)S(1)} %fusion.42), kind=kOutput, calls=%fused_computation | convolution fusion | flops 4533288960 | bytes 7476224 | tf_op jit(solution)/shard_map/dot_general | solution.py:17
  49.2 4.5 %convolution_convert_fusion.2.qk_ref = bf16[1152,1024]{1,0:T(8,128)(2,1)} fusion(bf16[1152,1152]{1,0:T(8,128)(2,1)S(1)} %copy-done.16, bf16[1152,1024]{1,0:T(8,128)(2,1)S(1)} %copy-done.13), kind=kOutput, calls=%fused_computation.6 | convolution fusion | flops 2719088640 | bytes 7372800 | tf_op jit(solution)/shard_map/dot_general | solution.py:17
  53.7 0.2 collective-permute-done.7
  53.9 3.7 %collective-permute-done.5 = f32[160,512]{1,0:T(8,128)S(1)} collective-permute-done((f32[160,512]{1,0:T(8,128)S(1)}, f32[160,512]{1,0:T(8,128)S(1)}, u32[]{:S(2)}, u32[]{:S(2)}) %collective-permute-start.5) | collective-permute-done | bytes 327712 | tf_op jit(solution)/shard_map/ppermute | solution.py:22
  57.9 1.5 collective-permute-start.10
  59.4 0.5 collective-permute-start.9
  59.9 3.7 %fusion.2 = f32[640,1024]{1,0:T(8,128)} fusion(bf16[1536,1024]{1,0:T(8,128)(2,1)S(1)} %copy-done.7, bf16[1280,1536]{1,0:T(8,128)(2,1)S(1)} %convolution_convert_fusion.t_ref), kind=kOutput, calls=%fused_computation.9 | convolution fusion | flops 2013265920 | bytes 7733248 | tf_op jit(solution)/shard_map/dot_general | solution.py:17
  63.6 0.6 collective-permute-start.8
  64.2 3.8 %fusion.4 = f32[640,1024]{1,0:T(8,128)} fusion(bf16[1536,1024]{1,0:T(8,128)(2,1)S(1)} %copy-done.7, bf16[1280,1536]{1,0:T(8,128)(2,1)S(1)} %convolution_convert_fusion.t_ref), kind=kOutput, calls=%fused_computation.11 | convolution fusion | flops 2013265920 | bytes 7733248 | tf_op jit(solution)/shard_map/dot_general | solution.py:17
  68.0 0.3 collective-permute-done.8
  68.3 0.5 fusion.sl_ref
  69.2 0.3 collective-permute-start.12
  69.5 1.1 collective-permute-done.12
  70.7 0.8 broadcast_multiply_fusion
  71.6 8.7 %gradient.1 = (bf16[1536,1024]{1,0:T(8,128)(2,1)S(1)}, f32[640,1024]{1,0:T(8,128)S(1)}, f32[640,1024]{1,0:T(8,128)}) custom-call(bf16[1536,1152]{1,0:T(8,128)(2,1)S(1)} %copy-done.9, bf16[1152,1024]{1,0:T(8,128)(2,1)S(1)} %fusion.sl_ref, bf16[1536,1024]{1,0:T(8,128)(2,1)S(1)} %copy-done.7, f32[8,1024]{1,0:T(8,128)S(1)} %maximum_maximum_fusion.state_ref, ...), custom_call_target="tpu_custom_call" | custom-call | flops 5234491392 | bytes 21233664 | tf_op jit(solution)/shard_map/gradient/pallas_call | solution.py:82
  80.3 1.5 %copy-done.2 = f32[640,1024]{1,0:T(8,128)} copy-done((f32[640,1024]{1,0:T(8,128)}, f32[640,1024]{1,0:T(8,128)S(1)}, u32[]{:S(2)}) %copy-start.2) | copy-done | bytes 2621464
  81.9 1.6 %copy-done.10 = bf16[1536,1024]{1,0:T(8,128)(2,1)} copy-done((bf16[1536,1024]{1,0:T(8,128)(2,1)}, bf16[1536,1024]{1,0:T(8,128)(2,1)S(1)}, u32[]{:S(2)}) %copy-start.10) | copy-done | bytes 3145752
  83.5 0.2 collective-permute-start.13
  84.0 0.4 copy.15
  84.4 0.3 convert_element_type.40
  84.7 3.2 %multiply_add_fusion = f32[640,1024]{1,0:T(8,128)S(1)} fusion(f32[640,1024]{1,0:T(8,128)} %collective-permute-done.20, f32[640,1024]{1,0:T(8,128)} %fusion.4, f32[1024]{0:T(1024)S(1)} %bitcast.103, f32[1024]{0:T(1024)S(1)} %bitcast.104), kind=kLoop, calls=%fused_computation.8 | loop fusion | flops 1966080 | bytes 7872512 | tf_op jit(solution)/shard_map/add | solution.py:399
  87.9 0.3 fusion.72
  88.2 0.7 collective-permute-start.23
  88.9 0.8 collective-permute-start.22
  89.7 0.8 collective-permute-start.21
  90.5 2.1 %split.1 = (f32[160,1024]{1,0:T(8,128)S(1)}, f32[160,1024]{1,0:T(8,128)S(1)}, f32[160,1024]{1,0:T(8,128)S(1)}, f32[160,1024]{1,0:T(8,128)S(1)}) custom-call(f32[640,1024]{1,0:T(8,128)S(1)} %copy-done.3, f32[640,1024]{1,0:T(8,128)} %collective-permute-done.13.got_ref), custom_call_target="tpu_custom_call" | custom-call | flops 655360 | bytes 7864320 | tf_op jit(solution)/shard_map/split/pallas_call | solution.py:403
  92.7 1.6 %collective-permute-start.14 = (f32[160,1024]{1,0:T(8,128)S(1)}, f32[160,1024]{1,0:T(8,128)S(1)}, u32[]{:S(2)}, u32[]{:S(2)}) collective-permute-start(f32[160,1024]{1,0:T(8,128)S(1)} %get-tuple-element.50), channel_id=1, source_target_pairs={{0,8},{8,16},{16,24},{24,0},{1,9},{9,17},{17,25},{25,1},{2,10},{10... | collective-permute-start | bytes 1966088 | tf_op jit(solution)/shard_map/ppermute | solution.py:22
  94.3 2.7 %collective-permute-start.15 = (f32[160,1024]{1,0:T(8,128)S(1)}, f32[160,1024]{1,0:T(8,128)S(1)}, u32[]{:S(2)}, u32[]{:S(2)}) collective-permute-start(f32[160,1024]{1,0:T(8,128)S(1)} %get-tuple-element.51), channel_id=1, source_target_pairs={{0,16},{8,24},{16,0},{24,8},{1,17},{9,25},{17,1},{25,9},{2,18},{10... | collective-permute-start | bytes 1966088 | tf_op jit(solution)/shard_map/ppermute | solution.py:22
  97.0 3.5 %convolution_convert_fusion.1.qv_ref = bf16[1152,1024]{1,0:T(8,128)(2,1)S(1)} fusion(bf16[1152,1152]{1,0:T(8,128)(2,1)S(1)} %copy-done.17, bf16[1152,1024]{1,0:T(8,128)(2,1)S(1)} %fusion.sl_ref), kind=kOutput, calls=%fused_computation.5 | convolution fusion | flops 2719088640 | bytes 7372800 | tf_op jit(solution)/shard_map/dot_general | solution.py:17
  100.5 5.3 %collective-permute-done.23 = f32[4,40,1024]{2,1,0:T(8,128)S(1)} collective-permute-done((f32[4,40,1024]{2,1,0:T(8,128)S(1)}, f32[4,40,1024]{2,1,0:T(8,128)S(1)}, u32[]{:S(2)}, u32[]{:S(2)}) %collective-permute-start.23) | collective-permute-done | bytes 655392 | tf_op jit(solution)/shard_map/ppermute | solution.py:22
  105.8 2.8 %collective-permute-start.16 = (f32[160,1024]{1,0:T(8,128)S(1)}, f32[160,1024]{1,0:T(8,128)S(1)}, u32[]{:S(2)}, u32[]{:S(2)}) collective-permute-start(f32[160,1024]{1,0:T(8,128)S(1)} %get-tuple-element.52), channel_id=1, source_target_pairs={{0,24},{8,0},{16,8},{24,16},{1,25},{9,1},{17,9},{25,17},{2,26},{10... | collective-permute-start | bytes 1966088 | tf_op jit(solution)/shard_map/ppermute | solution.py:22
  108.6 13.0 %back.1 = bf16[1458,1152]{1,0:T(8,128)(2,1)} custom-call(bf16[1536,1024]{1,0:T(8,128)(2,1)S(1)} %copy-done.11, bf16[1536,1024]{1,0:T(8,128)(2,1)S(1)} %copy-done.8, bf16[1152,1024]{1,0:T(8,128)(2,1)S(1)} %copy-done.12, bf16[1152,1024]{1,0:T(8,128)(2,1)S(1)} %convolution_convert_fusion.1.qv_ref, f32[8,1024]{1,0:T(8,128)S(1)} %maximum_maximum_fusion.state_ref, ...), custom_call_target="tpu_custom_call" | custom-call | flops 7247757312 | bytes 18087936 | tf_op jit(solution)/shard_map/back/pallas_call | solution.py:82
  121.6 0.3 add_multiply_fusion
  121.9 0.9 collective-permute-start.24
  122.9 2.4 %collective-permute-start.26 = (f32[40,1024]{1,0:T(8,128)S(1)}, f32[40,1024]{1,0:T(8,128)S(1)}, u32[]{:S(2)}, u32[]{:S(2)}) collective-permute-start(f32[40,1024]{1,0:T(8,128)S(1)} %get-tuple-element.71), channel_id=1, source_target_pairs={{0,24},{8,0},{16,8},{24,16},{1,25},{9,1},{17,9},{25,17},{2,26},{10... | collective-permute-start | bytes 491528 | tf_op jit(solution)/shard_map/ppermute | solution.py:22
  125.3 2.2 %collective-permute-start.25 = (f32[40,1024]{1,0:T(8,128)S(1)}, f32[40,1024]{1,0:T(8,128)S(1)}, u32[]{:S(2)}, u32[]{:S(2)}) collective-permute-start(f32[40,1024]{1,0:T(8,128)S(1)} %get-tuple-element.72), channel_id=1, source_target_pairs={{0,16},{8,24},{16,0},{24,8},{1,17},{9,25},{17,1},{25,9},{2,18},{10... | collective-permute-start | bytes 491528 | tf_op jit(solution)/shard_map/ppermute | solution.py:22
  127.5 0.2 add_add_fusion
  127.8 2.1 %collective-permute-start.17 = (f32[40,1024]{1,0:T(8,128)S(1)}, f32[40,1024]{1,0:T(8,128)S(1)}, u32[]{:S(2)}, u32[]{:S(2)}) collective-permute-start(f32[40,1024]{1,0:T(8,128)S(1)} %get-tuple-element.67), channel_id=1, source_target_pairs={{0,2},{2,4},{4,6},{6,0},{1,3},{3,5},{5,7},{7,1},{8,10},{10,12},{12... | collective-permute-start | bytes 491528 | tf_op jit(solution)/shard_map/ppermute | solution.py:22
  129.8 1.2 collective-permute-start.19
  131.1 3.0 %collective-permute-start.18 = (f32[40,1024]{1,0:T(8,128)S(1)}, f32[40,1024]{1,0:T(8,128)S(1)}, u32[]{:S(2)}, u32[]{:S(2)}) collective-permute-start(f32[40,1024]{1,0:T(8,128)S(1)} %get-tuple-element.69), channel_id=1, source_target_pairs={{0,4},{2,6},{4,0},{6,2},{1,5},{3,7},{5,1},{7,3},{8,12},{10,14},{12... | collective-permute-start | bytes 491528 | tf_op jit(solution)/shard_map/ppermute | solution.py:22
  134.1 0.8 fusion.29
  134.9 1.5 collective-permute-done.19
  136.4 2.3 %collective-permute-done.18 = f32[40,1024]{1,0:T(8,128)S(1)} collective-permute-done((f32[40,1024]{1,0:T(8,128)S(1)}, f32[40,1024]{1,0:T(8,128)S(1)}, u32[]{:S(2)}, u32[]{:S(2)}) %collective-permute-start.18) | collective-permute-done | bytes 163872 | tf_op jit(solution)/shard_map/ppermute | solution.py:22
  138.7 0.8 fusion.27
  139.5 2.0 %collective-permute-start.27 = (f32[9,2304]{1,0:T(8,128)S(1)}, f32[9,2304]{1,0:T(8,128)S(1)}, u32[]{:S(2)}, u32[]{:S(2)}) collective-permute-start(f32[9,2304]{1,0:T(8,128)S(1)} %get-tuple-element.75), channel_id=1, source_target_pairs={{0,32},{32,64},{64,96},{96,0},{1,33},{33,65},{65,97},{97,1},{2,34}... | collective-permute-start | bytes 248840 | tf_op jit(solution)/shard_map/ppermute | solution.py:22
  141.5 2.2 %collective-permute-start.29 = (f32[9,2304]{1,0:T(8,128)S(1)}, f32[9,2304]{1,0:T(8,128)S(1)}, u32[]{:S(2)}, u32[]{:S(2)}) collective-permute-start(f32[9,2304]{1,0:T(8,128)S(1)} %get-tuple-element.76), channel_id=1, source_target_pairs={{0,96},{32,0},{64,32},{96,64},{1,97},{33,1},{65,33},{97,65},{2,98}... | collective-permute-start | bytes 248840 | tf_op jit(solution)/shard_map/ppermute | solution.py:22
  143.7 1.8 %collective-permute-start.28 = (f32[9,2304]{1,0:T(8,128)S(1)}, f32[9,2304]{1,0:T(8,128)S(1)}, u32[]{:S(2)}, u32[]{:S(2)}) collective-permute-start(f32[9,2304]{1,0:T(8,128)S(1)} %get-tuple-element.77), channel_id=1, source_target_pairs={{0,64},{32,96},{64,0},{96,32},{1,65},{33,97},{65,1},{97,33},{2,66}... | collective-permute-start | bytes 248840 | tf_op jit(solution)/shard_map/ppermute | solution.py:22
  145.5 0.8 fusion.6
  146.3 0.6 collective-permute-done.27
  146.9 2.6 %collective-permute-done.29 = f32[9,2304]{1,0:T(8,128)S(1)} collective-permute-done((f32[9,2304]{1,0:T(8,128)S(1)}, f32[9,2304]{1,0:T(8,128)S(1)}, u32[]{:S(2)}, u32[]{:S(2)}) %collective-permute-start.29) | collective-permute-done | bytes 82976 | tf_op jit(solution)/shard_map/ppermute | solution.py:22
  149.4 1.9 %collective-permute-done.28 = f32[9,2304]{1,0:T(8,128)S(1)} collective-permute-done((f32[9,2304]{1,0:T(8,128)S(1)}, f32[9,2304]{1,0:T(8,128)S(1)}, u32[]{:S(2)}, u32[]{:S(2)}) %collective-permute-start.28) | collective-permute-done | bytes 82976 | tf_op jit(solution)/shard_map/ppermute | solution.py:22
  151.4 0.7 fusion.24
  (90 shorter events, 1.8 us)
Async XLA Ops:
  0.6 1.2 copy-start
  2.3 1.7 %collective-permute-start = (f32[72,1024]{1,0:T(8,128)S(1)}, f32[72,1024]{1,0:T(8,128)S(1)}, u32[]{:S(2)}, u32[]{:S(2)}) collective-permute-start(f32[72,1024]{1,0:T(8,128)S(1)} %copy.16), channel_id=1, source_target_pairs={{0,1},{1,0},{2,3},{3,2},{4,5},{5,4},{6,7},{7,6},{8,9},{9,8},{10,11... | collective-permute-start | bytes 884744 | tf_op jit(solution)/shard_map/ppermute | solution.py:22
  4.0 29.8 %collective-permute-start.2 = (f32[72,512]{1,0:T(8,128)S(1)}, f32[72,512]{1,0:T(8,128)S(1)}, u32[]{:S(2)}, u32[]{:S(2)}) collective-permute-start(f32[72,512]{1,0:T(8,128)S(1)} %dynamic-slice_add_fusion), channel_id=1, source_target_pairs={{0,16},{8,24},{16,0},{24,8},{1,17},{9,25},{17,1},{25,9},{2,18},{10... | collective-permute-start | bytes 442376 | tf_op jit(solution)/shard_map/ppermute | solution.py:22
  7.3 26.4 %collective-permute-start.1 = (f32[72,512]{1,0:T(8,128)S(1)}, f32[72,512]{1,0:T(8,128)S(1)}, u32[]{:S(2)}, u32[]{:S(2)}) collective-permute-start(f32[72,512]{1,0:T(8,128)S(1)} %dynamic-slice_add_fusion), channel_id=1, source_target_pairs={{0,8},{8,16},{16,24},{24,0},{1,9},{9,17},{17,25},{25,1},{2,10},{10... | collective-permute-start | bytes 442376 | tf_op jit(solution)/shard_map/ppermute | solution.py:22
  8.0 25.8 %collective-permute-start.3 = (f32[72,512]{1,0:T(8,128)S(1)}, f32[72,512]{1,0:T(8,128)S(1)}, u32[]{:S(2)}, u32[]{:S(2)}) collective-permute-start(f32[72,512]{1,0:T(8,128)S(1)} %dynamic-slice_add_fusion), channel_id=1, source_target_pairs={{0,24},{8,0},{16,8},{24,16},{1,25},{9,1},{17,9},{25,17},{2,26},{10... | collective-permute-start | bytes 442376 | tf_op jit(solution)/shard_map/ppermute | solution.py:22
  33.8 1.9 %collective-permute-start.4 = (f32[80,1024]{1,0:T(8,128)}, f32[80,1024]{1,0:T(8,128)S(1)}, u32[]{:S(2)}, u32[]{:S(2)}) collective-permute-start(f32[80,1024]{1,0:T(8,128)} %get-tuple-element.32.own_ref), channel_id=1, source_target_pairs={{0,1},{1,0},{2,3},{3,2},{4,5},{5,4},{6,7},{7,6},{8,9},{9,8},{10,11... | collective-permute-start | bytes 983048 | tf_op jit(solution)/shard_map/ppermute | solution.py:22
  35.8 1.0 copy-start.4
  36.8 17.1 %collective-permute-start.7 = (f32[160,512]{1,0:T(8,128)S(1)}, f32[160,512]{1,0:T(8,128)S(1)}, u32[]{:S(2)}, u32[]{:S(2)}) collective-permute-start(f32[160,512]{1,0:T(8,128)S(1)} %pair.1), channel_id=1, source_target_pairs={{0,6},{2,0},{4,2},{6,4},{1,7},{3,1},{5,3},{7,5},{8,14},{10,8},{12,... | collective-permute-start | bytes 983048 | tf_op jit(solution)/shard_map/ppermute | solution.py:22
  39.6 14.3 %collective-permute-start.6 = (f32[160,512]{1,0:T(8,128)S(1)}, f32[160,512]{1,0:T(8,128)S(1)}, u32[]{:S(2)}, u32[]{:S(2)}) collective-permute-start(f32[160,512]{1,0:T(8,128)S(1)} %pair.1), channel_id=1, source_target_pairs={{0,4},{2,6},{4,0},{6,2},{1,5},{3,7},{5,1},{7,3},{8,12},{10,14},{12... | collective-permute-start | bytes 983048 | tf_op jit(solution)/shard_map/ppermute | solution.py:22
  40.4 17.2 %collective-permute-start.5 = (f32[160,512]{1,0:T(8,128)S(1)}, f32[160,512]{1,0:T(8,128)S(1)}, u32[]{:S(2)}, u32[]{:S(2)}) collective-permute-start(f32[160,512]{1,0:T(8,128)S(1)} %pair.1), channel_id=1, source_target_pairs={{0,2},{2,4},{4,6},{6,0},{1,3},{3,5},{5,7},{7,1},{8,10},{10,12},{12... | collective-permute-start | bytes 983048 | tf_op jit(solution)/shard_map/ppermute | solution.py:22
  41.3 7.8 %copy-start.13 = (bf16[1152,1024]{1,0:T(8,128)(2,1)S(1)}, bf16[1152,1024]{1,0:T(8,128)(2,1)}, u32[]{:S(2)}) copy-start(bf16[1152,1024]{1,0:T(8,128)(2,1)} %get-tuple-element.36) | copy-start | bytes 7077892
  41.3 7.8 %copy-start.16 = (bf16[1152,1152]{1,0:T(8,128)(2,1)S(1)}, bf16[1152,1152]{1,0:T(8,128)(2,1)}, u32[]{:S(2)}) copy-start(bf16[1152,1152]{1,0:T(8,128)(2,1)} %wk_far.1) | copy-start | bytes 7962628
  49.2 10.7 %copy-start.7 = (bf16[1536,1024]{1,0:T(8,128)(2,1)S(1)}, bf16[1536,1024]{1,0:T(8,128)(2,1)}, u32[]{:S(2)}) copy-start(bf16[1536,1024]{1,0:T(8,128)(2,1)} %get-tuple-element.40.e_ref) | copy-start | bytes 9437188
  57.7 11.1 %collective-permute-start.11 = (f32[80,512]{1,0:T(8,128)S(1)}, f32[80,512]{1,0:T(8,128)S(1)}, u32[]{:S(2)}, u32[]{:S(2)}) collective-permute-start(f32[80,512]{1,0:T(8,128)S(1)} %fusion.15), channel_id=1, source_target_pairs={{0,24},{8,0},{16,8},{24,16},{1,25},{9,1},{17,9},{25,17},{2,26},{10... | collective-permute-start | bytes 491528 | tf_op jit(solution)/shard_map/ppermute | solution.py:22
  57.9 11.0 %collective-permute-start.10 = (f32[80,512]{1,0:T(8,128)S(1)}, f32[80,512]{1,0:T(8,128)S(1)}, u32[]{:S(2)}, u32[]{:S(2)}) collective-permute-start(f32[80,512]{1,0:T(8,128)S(1)} %fusion.15), channel_id=1, source_target_pairs={{0,16},{8,24},{16,0},{24,8},{1,17},{9,25},{17,1},{25,9},{2,18},{10... | collective-permute-start | bytes 491528 | tf_op jit(solution)/shard_map/ppermute | solution.py:22
  59.4 9.7 %collective-permute-start.9 = (f32[80,512]{1,0:T(8,128)S(1)}, f32[80,512]{1,0:T(8,128)S(1)}, u32[]{:S(2)}, u32[]{:S(2)}) collective-permute-start(f32[80,512]{1,0:T(8,128)S(1)} %fusion.15), channel_id=1, source_target_pairs={{0,8},{8,16},{16,24},{24,0},{1,9},{9,17},{17,25},{25,1},{2,10},{10... | collective-permute-start | bytes 491528 | tf_op jit(solution)/shard_map/ppermute | solution.py:22
  63.5 21.2 %collective-permute-start.20 = (f32[640,1024]{1,0:T(8,128)}, f32[640,1024]{1,0:T(8,128)}, u32[]{:S(2)}, u32[]{:S(2)}) collective-permute-start(f32[640,1024]{1,0:T(8,128)} %fusion.2), channel_id=1, source_target_pairs={{0,1},{1,0},{2,3},{3,2},{4,5},{5,4},{6,7},{7,6},{8,9},{9,8},{10,11... | collective-permute-start | bytes 7864328 | tf_op jit(solution)/shard_map/ppermute | solution.py:22
  63.6 4.7 %collective-permute-start.8 = (f32[72,512]{1,0:T(8,128)S(1)}, f32[72,512]{1,0:T(8,128)S(1)}, u32[]{:S(2)}, u32[]{:S(2)}) collective-permute-start(f32[72,512]{1,0:T(8,128)S(1)} %slice_add_fusion.1), channel_id=1, source_target_pairs={{0,1},{1,0},{2,3},{3,2},{4,5},{5,4},{6,7},{7,6},{8,9},{9,8},{10,11... | collective-permute-start | bytes 442376 | tf_op jit(solution)/shard_map/ppermute | solution.py:22
  68.3 3.3 %copy-start.9 = (bf16[1536,1152]{1,0:T(8,128)(2,1)S(1)}, bf16[1536,1152]{1,0:T(8,128)(2,1)}, u32[]{:S(2)}) copy-start(bf16[1536,1152]{1,0:T(8,128)(2,1)} %get-tuple-element.42.v_ref) | copy-start | bytes 10616836
  69.2 1.5 collective-permute-start.12
  80.3 1.5 %copy-start.2 = (f32[640,1024]{1,0:T(8,128)}, f32[640,1024]{1,0:T(8,128)S(1)}, u32[]{:S(2)}) copy-start(f32[640,1024]{1,0:T(8,128)S(1)} %get-tuple-element.44.keep_ref) | copy-start | bytes 7864324
  81.9 1.6 %copy-start.10 = (bf16[1536,1024]{1,0:T(8,128)(2,1)}, bf16[1536,1024]{1,0:T(8,128)(2,1)S(1)}, u32[]{:S(2)}) copy-start(bf16[1536,1024]{1,0:T(8,128)(2,1)S(1)} %get-tuple-element.47.d_ref) | copy-start | bytes 9437188
  83.5 7.0 %collective-permute-start.13 = (f32[640,1024]{1,0:T(8,128)}, f32[640,1024]{1,0:T(8,128)}, u32[]{:S(2)}, u32[]{:S(2)}) collective-permute-start(f32[640,1024]{1,0:T(8,128)} %get-tuple-element.45), channel_id=1, source_target_pairs={{0,1},{1,0},{2,3},{3,2},{4,5},{5,4},{6,7},{7,6},{8,9},{9,8},{10,11... | collective-permute-start | bytes 7864328 | tf_op jit(solution)/shard_map/ppermute | solution.py:22
  87.9 2.6 %copy-start.3 = (f32[640,1024]{1,0:T(8,128)S(1)}, f32[640,1024]{1,0:T(8,128)}, u32[]{:S(2)}) copy-start(f32[640,1024]{1,0:T(8,128)} %copy-done.2) | copy-start | bytes 7864324
  88.2 17.6 %collective-permute-start.23 = (f32[4,40,1024]{2,1,0:T(8,128)S(1)}, f32[4,40,1024]{2,1,0:T(8,128)S(1)}, u32[]{:S(2)}, u32[]{:S(2)}) collective-permute-start(f32[4,40,1024]{2,1,0:T(8,128)S(1)} %bitcast.92), channel_id=1, source_target_pairs={{0,6},{2,0},{4,2},{6,4},{1,7},{3,1},{5,3},{7,5},{8,14},{10,8},{12,... | collective-permute-start | bytes 1966088 | tf_op jit(solution)/shard_map/ppermute | solution.py:22
  88.9 32.7 %collective-permute-start.22 = (f32[4,40,1024]{2,1,0:T(8,128)S(1)}, f32[4,40,1024]{2,1,0:T(8,128)S(1)}, u32[]{:S(2)}, u32[]{:S(2)}) collective-permute-start(f32[4,40,1024]{2,1,0:T(8,128)S(1)} %bitcast.91), channel_id=1, source_target_pairs={{0,4},{2,6},{4,0},{6,2},{1,5},{3,7},{5,1},{7,3},{8,12},{10,14},{12... | collective-permute-start | bytes 1966088 | tf_op jit(solution)/shard_map/ppermute | solution.py:22
  89.7 31.9 %collective-permute-start.21 = (f32[4,40,1024]{2,1,0:T(8,128)S(1)}, f32[4,40,1024]{2,1,0:T(8,128)S(1)}, u32[]{:S(2)}, u32[]{:S(2)}) collective-permute-start(f32[4,40,1024]{2,1,0:T(8,128)S(1)} %bitcast.90), channel_id=1, source_target_pairs={{0,2},{2,4},{4,6},{6,0},{1,3},{3,5},{5,7},{7,1},{8,10},{10,12},{12... | collective-permute-start | bytes 1966088 | tf_op jit(solution)/shard_map/ppermute | solution.py:22
  90.5 6.5 %copy-start.17 = (bf16[1152,1152]{1,0:T(8,128)(2,1)S(1)}, bf16[1152,1152]{1,0:T(8,128)(2,1)}, u32[]{:S(2)}) copy-start(bf16[1152,1152]{1,0:T(8,128)(2,1)} %wv_far.1) | copy-start | bytes 7962628
  92.7 32.6 %collective-permute-start.14 = (f32[160,1024]{1,0:T(8,128)S(1)}, f32[160,1024]{1,0:T(8,128)S(1)}, u32[]{:S(2)}, u32[]{:S(2)}) collective-permute-start(f32[160,1024]{1,0:T(8,128)S(1)} %get-tuple-element.50), channel_id=1, source_target_pairs={{0,8},{8,16},{16,24},{24,0},{1,9},{9,17},{17,25},{25,1},{2,10},{10... | collective-permute-start | bytes 1966088 | tf_op jit(solution)/shard_map/ppermute | solution.py:22
  94.3 14.3 %copy-start.5 = (bf16[1,1458,1152]{2,1,0:T(8,128)(2,1)S(1)}, bf16[1,1458,1152]{2,1,0:T(8,128)(2,1)}, u32[]{:S(2)}) copy-start(bf16[1,1458,1152]{2,1,0:T(8,128)(2,1)} %param.8) | copy-start | bytes 10077700
  94.3 14.3 %copy-start.6 = (bf16[1152]{0:T(1024)(128)(2,1)S(1)}, bf16[1152]{0:T(1024)(128)(2,1)}, u32[]{:S(2)}) copy-start(bf16[1152]{0:T(1024)(128)(2,1)} %gain_ref.3) | copy-start | bytes 6916
  94.3 14.3 %copy-start.8 = (bf16[1536,1024]{1,0:T(8,128)(2,1)S(1)}, bf16[1536,1024]{1,0:T(8,128)(2,1)}, u32[]{:S(2)}) copy-start(bf16[1536,1024]{1,0:T(8,128)(2,1)} %get-tuple-element.40.e_ref) | copy-start | bytes 9437188
  94.3 14.3 %copy-start.11 = (bf16[1536,1024]{1,0:T(8,128)(2,1)S(1)}, bf16[1536,1024]{1,0:T(8,128)(2,1)}, u32[]{:S(2)}) copy-start(bf16[1536,1024]{1,0:T(8,128)(2,1)} %copy-done.10) | copy-start | bytes 9437188
  94.3 14.3 %copy-start.12 = (bf16[1152,1024]{1,0:T(8,128)(2,1)S(1)}, bf16[1152,1024]{1,0:T(8,128)(2,1)}, u32[]{:S(2)}) copy-start(bf16[1152,1024]{1,0:T(8,128)(2,1)} %convolution_convert_fusion.2.qk_ref) | copy-start | bytes 7077892
  94.3 33.2 %collective-permute-start.15 = (f32[160,1024]{1,0:T(8,128)S(1)}, f32[160,1024]{1,0:T(8,128)S(1)}, u32[]{:S(2)}, u32[]{:S(2)}) collective-permute-start(f32[160,1024]{1,0:T(8,128)S(1)} %get-tuple-element.51), channel_id=1, source_target_pairs={{0,16},{8,24},{16,0},{24,8},{1,17},{9,25},{17,1},{25,9},{2,18},{10... | collective-permute-start | bytes 1966088 | tf_op jit(solution)/shard_map/ppermute | solution.py:22
  105.8 21.6 %collective-permute-start.16 = (f32[160,1024]{1,0:T(8,128)S(1)}, f32[160,1024]{1,0:T(8,128)S(1)}, u32[]{:S(2)}, u32[]{:S(2)}) collective-permute-start(f32[160,1024]{1,0:T(8,128)S(1)} %get-tuple-element.52), channel_id=1, source_target_pairs={{0,24},{8,0},{16,8},{24,16},{1,25},{9,1},{17,9},{25,17},{2,26},{10... | collective-permute-start | bytes 1966088 | tf_op jit(solution)/shard_map/ppermute | solution.py:22
  121.9 9.1 %collective-permute-start.24 = (f32[40,1024]{1,0:T(8,128)S(1)}, f32[40,1024]{1,0:T(8,128)S(1)}, u32[]{:S(2)}, u32[]{:S(2)}) collective-permute-start(f32[40,1024]{1,0:T(8,128)S(1)} %get-tuple-element.70), channel_id=1, source_target_pairs={{0,8},{8,16},{16,24},{24,0},{1,9},{9,17},{17,25},{25,1},{2,10},{10... | collective-permute-start | bytes 491528 | tf_op jit(solution)/shard_map/ppermute | solution.py:22
  122.9 11.2 %collective-permute-start.26 = (f32[40,1024]{1,0:T(8,128)S(1)}, f32[40,1024]{1,0:T(8,128)S(1)}, u32[]{:S(2)}, u32[]{:S(2)}) collective-permute-start(f32[40,1024]{1,0:T(8,128)S(1)} %get-tuple-element.71), channel_id=1, source_target_pairs={{0,24},{8,0},{16,8},{24,16},{1,25},{9,1},{17,9},{25,17},{2,26},{10... | collective-permute-start | bytes 491528 | tf_op jit(solution)/shard_map/ppermute | solution.py:22
  125.3 8.8 %collective-permute-start.25 = (f32[40,1024]{1,0:T(8,128)S(1)}, f32[40,1024]{1,0:T(8,128)S(1)}, u32[]{:S(2)}, u32[]{:S(2)}) collective-permute-start(f32[40,1024]{1,0:T(8,128)S(1)} %get-tuple-element.72), channel_id=1, source_target_pairs={{0,16},{8,24},{16,0},{24,8},{1,17},{9,25},{17,1},{25,9},{2,18},{10... | collective-permute-start | bytes 491528 | tf_op jit(solution)/shard_map/ppermute | solution.py:22
  127.7 11.0 %copy-start.14 = (bf16[1152,1024]{1,0:T(8,128)(2,1)S(1)}, bf16[1152,1024]{1,0:T(8,128)(2,1)}, u32[]{:S(2)}) copy-start(bf16[1152,1024]{1,0:T(8,128)(2,1)} %get-tuple-element.36) | copy-start | bytes 7077892
  127.8 7.1 %collective-permute-start.17 = (f32[40,1024]{1,0:T(8,128)S(1)}, f32[40,1024]{1,0:T(8,128)S(1)}, u32[]{:S(2)}, u32[]{:S(2)}) collective-permute-start(f32[40,1024]{1,0:T(8,128)S(1)} %get-tuple-element.67), channel_id=1, source_target_pairs={{0,2},{2,4},{4,6},{6,0},{1,3},{3,5},{5,7},{7,1},{8,10},{10,12},{12... | collective-permute-start | bytes 491528 | tf_op jit(solution)/shard_map/ppermute | solution.py:22
  129.8 6.5 %collective-permute-start.19 = (f32[40,1024]{1,0:T(8,128)S(1)}, f32[40,1024]{1,0:T(8,128)S(1)}, u32[]{:S(2)}, u32[]{:S(2)}) collective-permute-start(f32[40,1024]{1,0:T(8,128)S(1)} %get-tuple-element.68), channel_id=1, source_target_pairs={{0,6},{2,0},{4,2},{6,4},{1,7},{3,1},{5,3},{7,5},{8,14},{10,8},{12,... | collective-permute-start | bytes 491528 | tf_op jit(solution)/shard_map/ppermute | solution.py:22
  131.1 7.6 %collective-permute-start.18 = (f32[40,1024]{1,0:T(8,128)S(1)}, f32[40,1024]{1,0:T(8,128)S(1)}, u32[]{:S(2)}, u32[]{:S(2)}) collective-permute-start(f32[40,1024]{1,0:T(8,128)S(1)} %get-tuple-element.69), channel_id=1, source_target_pairs={{0,4},{2,6},{4,0},{6,2},{1,5},{3,7},{5,1},{7,3},{8,12},{10,14},{12... | collective-permute-start | bytes 491528 | tf_op jit(solution)/shard_map/ppermute | solution.py:22
  134.1 18.0 %copy-start.1 = (bf16[1,64,36]{1,2,0:T(8,128)(2,1)S(1)}, bf16[1,64,36]{1,2,0:T(8,128)(2,1)}, u32[]{:S(2)}) copy-start(bf16[1,64,36]{1,2,0:T(8,128)(2,1)} %param.15) | copy-start | bytes 13828
  134.9 10.6 %copy-start.15 = (bf16[1152,36]{0,1:T(8,128)(2,1)S(1)}, bf16[1152,36]{0,1:T(8,128)(2,1)}, u32[]{:S(2)}) copy-start(bf16[1152,36]{0,1:T(8,128)(2,1)} %param.14) | copy-start | bytes 248836
  139.5 7.3 %collective-permute-start.27 = (f32[9,2304]{1,0:T(8,128)S(1)}, f32[9,2304]{1,0:T(8,128)S(1)}, u32[]{:S(2)}, u32[]{:S(2)}) collective-permute-start(f32[9,2304]{1,0:T(8,128)S(1)} %get-tuple-element.75), channel_id=1, source_target_pairs={{0,32},{32,64},{64,96},{96,0},{1,33},{33,65},{65,97},{97,1},{2,34}... | collective-permute-start | bytes 248840 | tf_op jit(solution)/shard_map/ppermute | solution.py:22
  141.5 7.9 %collective-permute-start.29 = (f32[9,2304]{1,0:T(8,128)S(1)}, f32[9,2304]{1,0:T(8,128)S(1)}, u32[]{:S(2)}, u32[]{:S(2)}) collective-permute-start(f32[9,2304]{1,0:T(8,128)S(1)} %get-tuple-element.76), channel_id=1, source_target_pairs={{0,96},{32,0},{64,32},{96,64},{1,97},{33,1},{65,33},{97,65},{2,98}... | collective-permute-start | bytes 248840 | tf_op jit(solution)/shard_map/ppermute | solution.py:22
  143.7 7.7 %collective-permute-start.28 = (f32[9,2304]{1,0:T(8,128)S(1)}, f32[9,2304]{1,0:T(8,128)S(1)}, u32[]{:S(2)}, u32[]{:S(2)}) collective-permute-start(f32[9,2304]{1,0:T(8,128)S(1)} %get-tuple-element.77), channel_id=1, source_target_pairs={{0,64},{32,96},{64,0},{96,32},{1,65},{33,97},{65,1},{97,33},{2,66}... | collective-permute-start | bytes 248840 | tf_op jit(solution)/shard_map/ppermute | solution.py:22

commit v5 on v4

--- a/solution.py
+++ b/solution.py
@@ -257,7 +257,10 @@
     out_ref[: width + 8, :] = jnp.where(row == width, best, both)
     row = lax.broadcasted_iota(jnp.int32, (8, cut), 0)
     out_ref[width + 8 : width + 16, :] = jnp.where(row % 2 == 0, top[:, :cut], top[:, cut:])
-    out_ref[width + 16 :, :] = lc_ref[...]
+    out_ref[width + 16 :, :] = jnp.zeros((width // 3, cut), F32)
+    for b in range(3):
+        rows = slice(width // 3 * b, width // 3 * (b + 1))
+        out_ref[width + 16 :, 128 * b : 128 * (b + 1)] = lc_ref[rows, :]
 
 
 def split_kernel(keep_ref, got_ref, *outs):
@@ -291,7 +294,14 @@
     lc = own_half(lc + shift(lc, "c", 1))
 
     frames_1 = after(frames, lc)
-    lc_y = [shift(lc, "y", k) for k in (1, 2, 3)]
+    here = lax.axis_index("y")
+    part = cols // 8
+
+    def of_row(k):
+        return lax.dynamic_slice_in_dim(lc, (here + k) % 4 * part, part, 1)
+
+    lc_y = [shift(of_row(k), "y", k) for k in (1, 2, 3)]
+    lc = of_row(0)
 
     def first(i):
         return (jnp.minimum(i, steps - 1), 0)
@@ -346,7 +356,7 @@
         functools.partial(pair_kernel, width),
         in_specs=[pl.BlockSpec(memory_space=pltpu.SMEM), vmem, vmem, vmem],
         out_specs=vmem,
-        out_shape=jax.ShapeDtypeStruct((2 * width + 16, cols // 2), F32),
+        out_shape=jax.ShapeDtypeStruct((width + 16 + width // 3, cols // 2), F32),
         compiler_params=pltpu.CompilerParams(vmem_limit_bytes=16 * 2**20),
         name="pair",
     )(core.astype(jnp.int32).reshape(1), pack, paired, lc)
@@ -355,24 +365,33 @@
     halves = [half] + [shift(half, "x", k) for k in (1, 2, 3)]
     tops = [h[width + 8 : width + 10].reshape(1, cols) for h in halves]
     top3 = jnp.maximum(jnp.maximum(tops[0], tops[1]), jnp.maximum(tops[2], tops[3]))
-    q_key = dot(after(w_key, turned), spread_q).astype(BF16)
-    halves[0] = after(halves[0], q_key)
+    halves[0] = after(halves[0], turned)
     half = merge([h[: width + 8] for h in halves], width)
     lc = sum(h[width + 16 :] for h in halves)
-    lc = whole(lc, shift(lc, "c", 1))
-    spread_lc = spread(lc, width)
-
+
+    half = jnp.concatenate([half, lc], axis=0)
     half_y = [shift(half, "y", k) for k in (1, 2, 3)]
     u_send = dot(turned[half_rows:], after(expo, half))
     u_got = shift(u_send, "c", 1)
     u = dot(turned[:half_rows], after(expo, u_send))
-    half = merge([after(half, u, spread_lc)] + half_y, width)
+    half_y = [after(half, u)] + half_y
+    column = lax.broadcasted_iota(jnp.int32, (width, cols // 2), 1) // part
+    lc = jnp.zeros((width, cols // 2), F32)
+    for k in range(4):
+        got = half_y[k][width + 8 :]
+        got = jnp.concatenate([got[:, 128 * b : 128 * (b + 1)] for b in range(3)], axis=0)
+        lc = jnp.where(column == (here - k) % 4, jnp.tile(got, (1, 4)), lc)
+    half = merge([h[: width + 8] for h in half_y], width)
+    half = jnp.concatenate([half, lc], axis=0)
     pack = whole(half, shift(half, "c", 1))
+    pack, lc = pack[: width + 8], pack[width + 8 :]
     gtop, gtotal = pack[width : width + 1], pack[width + 1 : width + 2]
     attn = pack[:width] / gtotal
     factor = jnp.exp(top - gtop) / gtotal
     drift = jnp.sum(lc * attn, axis=0, keepdims=True)
     state = jnp.concatenate([drift, factor * scale, factor, jnp.zeros((5, cols), F32)], axis=0)
+
+    spread_lc = spread(lc, width)
 
     dscore, w, w_send = call(
         functools.partial(grad_kernel, width, nlat),
@@ -411,6 +430,7 @@
     )(w, w_got)
 
 
+    q_key = dot(after(w_key, parts[0]), spread_q).astype(BF16)
     q_value = dot(after(w_value, parts[0]), spread_lc).astype(BF16)
     patch_grad = call(
         back_kernel,

time: 152 us -> 153 us (level)
  waiting for transfers between devices: 22.9 us -> 32.3 us
  starting transfers between devices: 41.8 us -> 33.4 us
    ppermute x30 -> x29, waiting for transfers between devices: 22.9 us -> 32.3 us  [shift(): return lax.ppermute(value, axis, [(i, (i + step) % n) for i in range(n)])]
    ppermute x30 -> x29, starting transfers between devices: 41.8 us -> 33.4 us  [shift(): return lax.ppermute(value, axis, [(i, (i + step) % n) for i in range(n)])]
    unnamed x41 -> x37, local copies, waits for them, and re-layouts: 4.23 us -> 4.23 us
  transfers between devices with their start and end apart: 30 -> 29, of which waited for: 13 -> 17; matrix products, arithmetic and copies ran while one was open for 21% -> 20% of each run, Pallas kernels for 31% -> 31%
where the time goes in v5:
time: 153 us
  Pallas kernels  47 us (31%)
  starting transfers between devices  33.4 us (22%)
  waiting for transfers between devices  32.3 us (21%)
  matrix products  24.9 us (16%)
  local copies, waits for them, and re-layouts  7.17 us (5%)
  other arithmetic  6.74 us (4%)
    pallas_call x3, Pallas kernels, call(): pl.pallas_call(body, grid=(steps,), in_specs=[spec(b, m, 1) for _, b, m i...  44.8 us
    ppermute x29, starting transfers between devices, shift(): return lax.ppermute(value, axis, [(i, (i + step) % n) for i in range(n)])  33.4 us
    ppermute x29, waiting for transfers between devices, shift(): return lax.ppermute(value, axis, [(i, (i + step) % n) for i in range(n)])  32.3 us
    dot_general x9, matrix products, dot(): lax.dot_general(a, b, (((ca,), (cb,)), ((), ())), preferred_element_type=...  24.9 us
    unnamed x37, local copies, waits for them, and re-layouts  4.23 us
    add x1, other arithmetic, per_device(): after(u, w_send) * jnp.exp(top - top2) + u_got * jnp.exp(top_pair - top2)  3.4 us
  transfers between devices with their start and end apart: 29, of which 17 were waited for; matrix products, arithmetic and copies ran while one was open for 20% of the time, Pallas kernels for 31%

profile of v5, /device:TPU:0, one launch (start us, length us, event | category | flops | bytes accessed | tf_op | source)
XLA Modules:
  0.0 152.8 jit_solution(10281989478183233174)
XLA Ops:
  0.6 1.2 dot_general.29
  1.8 0.3 fusion.22
  2.5 23.2 %softmax.1 = (bf16[1536,1152]{1,0:T(8,128)(2,1)}, bf16[1536,1152]{1,0:T(8,128)(2,1)}, bf16[1536,1024]{1,0:T(8,128)(2,1)}, f32[80,1024]{1,0:T(8,128)}, bf16[1152,1024]{1,0:T(8,128)(2,1)}) custom-call(bf16[1458,1152]{1,0:T(8,128)(2,1)} %bitcast.103, bf16[1152]{0:T(1024)(128)(2,1)} %gain_ref.3, bf16[1152,1152]{1,0:T(8,128)(2,1)} %wk_far.1, ...), custom_call_target="tpu_custom_call" | custom-call | flops 10569646080 | bytes 21430272 | tf_op jit(solution)/shard_map/softmax/pallas_call | solution.py:82
  25.9 1.7 %collective-permute-start.1 = (f32[72,128]{1,0:T(8,128)S(1)}, f32[72,128]{1,0:T(8,128)S(1)}, u32[]{:S(2)}, u32[]{:S(2)}) collective-permute-start(f32[72,128]{1,0:T(8,128)S(1)} %get-tuple-element.82), channel_id=1, source_target_pairs={{0,8},{8,16},{16,24},{24,0},{1,9},{9,17},{17,25},{25,1},{2,10},{10... | collective-permute-start | bytes 110600 | tf_op jit(solution)/shard_map/ppermute | solution.py:22
  27.7 1.6 %collective-permute-start.3 = (f32[72,128]{1,0:T(8,128)S(1)}, f32[72,128]{1,0:T(8,128)S(1)}, u32[]{:S(2)}, u32[]{:S(2)}) collective-permute-start(f32[72,128]{1,0:T(8,128)S(1)} %get-tuple-element.83), channel_id=1, source_target_pairs={{0,24},{8,0},{16,8},{24,16},{1,25},{9,1},{17,9},{25,17},{2,26},{10... | collective-permute-start | bytes 110600 | tf_op jit(solution)/shard_map/ppermute | solution.py:22
  29.3 2.1 %collective-permute-start.2 = (f32[72,128]{1,0:T(8,128)S(1)}, f32[72,128]{1,0:T(8,128)S(1)}, u32[]{:S(2)}, u32[]{:S(2)}) collective-permute-start(f32[72,128]{1,0:T(8,128)S(1)} %get-tuple-element.84), channel_id=1, source_target_pairs={{0,16},{8,24},{16,0},{24,8},{1,17},{9,25},{17,1},{25,9},{2,18},{10... | collective-permute-start | bytes 110600 | tf_op jit(solution)/shard_map/ppermute | solution.py:22
  31.4 0.2 collective-permute-done.3
  31.6 3.1 %collective-permute-done.2 = f32[72,128]{1,0:T(8,128)S(1)} collective-permute-done((f32[72,128]{1,0:T(8,128)S(1)}, f32[72,128]{1,0:T(8,128)S(1)}, u32[]{:S(2)}, u32[]{:S(2)}) %collective-permute-start.2) | collective-permute-done | bytes 36896 | tf_op jit(solution)/shard_map/ppermute | solution.py:22
  34.9 1.7 %collective-permute-done.4.got_ref = f32[80,1024]{1,0:T(8,128)S(1)} collective-permute-done((f32[80,1024]{1,0:T(8,128)}, f32[80,1024]{1,0:T(8,128)S(1)}, u32[]{:S(2)}, u32[]{:S(2)}) %collective-permute-start.4) | collective-permute-done | bytes 327712 | tf_op jit(solution)/shard_map/ppermute | solution.py:22
  36.7 1.0 copy-done.4
  37.7 2.9 %collective-permute-start.7 = (f32[112,512]{1,0:T(8,128)S(1)}, f32[112,512]{1,0:T(8,128)S(1)}, u32[]{:S(2)}, u32[]{:S(2)}) collective-permute-start(f32[112,512]{1,0:T(8,128)S(1)} %pair.1), channel_id=1, source_target_pairs={{0,6},{2,0},{4,2},{6,4},{1,7},{3,1},{5,3},{7,5},{8,14},{10,8},{12,... | collective-permute-start | bytes 688136 | tf_op jit(solution)/shard_map/ppermute | solution.py:22
  40.6 0.8 collective-permute-start.6
  41.4 0.9 collective-permute-start.5
  42.3 7.8 %convolution_convert_fusion.t_ref = bf16[1280,1536]{1,0:T(8,128)(2,1)S(1)} fusion(bf16[1536,1152]{1,0:T(8,128)(2,1)} %get-tuple-element.32, s32[1280]{0:T(1024)S(1)} %fusion.49), kind=kOutput, calls=%fused_computation | convolution fusion | flops 4533288960 | bytes 7476224 | tf_op jit(solution)/shard_map/dot_general | solution.py:17
  50.1 0.6 collective-permute-done.7
  50.7 3.7 %collective-permute-done.5 = f32[112,512]{1,0:T(8,128)S(1)} collective-permute-done((f32[112,512]{1,0:T(8,128)S(1)}, f32[112,512]{1,0:T(8,128)S(1)}, u32[]{:S(2)}, u32[]{:S(2)}) %collective-permute-start.5) | collective-permute-done | bytes 229408 | tf_op jit(solution)/shard_map/ppermute | solution.py:22
  54.5 1.9 %collective-permute-start.10 = (f32[104,512]{1,0:T(8,128)S(1)}, f32[104,512]{1,0:T(8,128)S(1)}, u32[]{:S(2)}, u32[]{:S(2)}) collective-permute-start(f32[104,512]{1,0:T(8,128)S(1)} %pad_maximum_fusion.1), channel_id=1, source_target_pairs={{0,24},{8,0},{16,8},{24,16},{1,25},{9,1},{17,9},{25,17},{2,26},{10... | collective-permute-start | bytes 638984 | tf_op jit(solution)/shard_map/ppermute | solution.py:22
  56.4 0.6 collective-permute-start.9
  57.0 1.0 collective-permute-start.8
  58.0 3.7 %fusion.2 = f32[640,1024]{1,0:T(8,128)} fusion(bf16[1536,1024]{1,0:T(8,128)(2,1)S(1)} %copy-done.7, bf16[1280,1536]{1,0:T(8,128)(2,1)S(1)} %convolution_convert_fusion.t_ref), kind=kOutput, calls=%fused_computation.9 | convolution fusion | flops 2013265920 | bytes 7733248 | tf_op jit(solution)/shard_map/dot_general | solution.py:17
  61.8 3.8 %fusion.4 = f32[640,1024]{1,0:T(8,128)} fusion(bf16[1536,1024]{1,0:T(8,128)(2,1)S(1)} %copy-done.7, bf16[1280,1536]{1,0:T(8,128)(2,1)S(1)} %convolution_convert_fusion.t_ref), kind=kOutput, calls=%fused_computation.11 | convolution fusion | flops 2013265920 | bytes 7733248 | tf_op jit(solution)/shard_map/dot_general | solution.py:17
  65.7 0.4 collective-permute-done.9
  66.1 3.2 %collective-permute-done.8 = f32[104,512]{1,0:T(8,128)S(1)} collective-permute-done((f32[104,512]{1,0:T(8,128)S(1)}, f32[104,512]{1,0:T(8,128)S(1)}, u32[]{:S(2)}, u32[]{:S(2)}) %collective-permute-start.8) | collective-permute-done | bytes 213024 | tf_op jit(solution)/shard_map/ppermute | solution.py:22
  69.9 0.5 collective-permute-start.19
  70.4 1.1 collective-permute-done.11
  71.5 0.8 broadcast_multiply_fusion
  72.4 0.5 fusion.sl_ref
  73.0 8.6 %gradient.1 = (bf16[1536,1024]{1,0:T(8,128)(2,1)S(1)}, f32[640,1024]{1,0:T(8,128)S(1)}, f32[640,1024]{1,0:T(8,128)}) custom-call(bf16[1536,1152]{1,0:T(8,128)(2,1)S(1)} %copy-done.9, bf16[1152,1024]{1,0:T(8,128)(2,1)S(1)} %fusion.sl_ref, bf16[1536,1024]{1,0:T(8,128)(2,1)S(1)} %copy-done.7, f32[8,1024]{1,0:T(8,128)S(1)} %maximum_maximum_fusion.state_ref, ...), custom_call_target="tpu_custom_call" | custom-call | flops 5234491392 | bytes 21233664 | tf_op jit(solution)/shard_map/gradient/pallas_call | solution.py:82
  81.6 1.5 copy-done.2
  83.1 1.7 %copy-done.10 = bf16[1536,1024]{1,0:T(8,128)(2,1)} copy-done((bf16[1536,1024]{1,0:T(8,128)(2,1)}, bf16[1536,1024]{1,0:T(8,128)(2,1)S(1)}, u32[]{:S(2)}) %copy-start.10) | copy-done | bytes 3145752
  85.0 0.2 convert_element_type.36
  85.2 0.4 copy.15
  85.6 0.3 convert_element_type.38
  85.9 3.4 %multiply_add_fusion = f32[640,1024]{1,0:T(8,128)S(1)} fusion(f32[640,1024]{1,0:T(8,128)} %collective-permute-done.19, f32[640,1024]{1,0:T(8,128)} %fusion.4, f32[1024]{0:T(1024)S(1)} %bitcast.125, f32[1024]{0:T(1024)S(1)} %bitcast.126), kind=kLoop, calls=%fused_computation.8 | loop fusion | flops 1966080 | bytes 7872512 | tf_op jit(solution)/shard_map/add | solution.py:418
  89.3 0.3 fusion.82
  89.7 0.9 collective-permute-start.21
  90.6 1.3 collective-permute-start.20
  91.9 2.1 %split.1 = (f32[160,1024]{1,0:T(8,128)S(1)}, f32[160,1024]{1,0:T(8,128)S(1)}, f32[160,1024]{1,0:T(8,128)S(1)}, f32[160,1024]{1,0:T(8,128)S(1)}) custom-call(f32[640,1024]{1,0:T(8,128)S(1)} %copy-done.3, f32[640,1024]{1,0:T(8,128)} %collective-permute-done.12.got_ref), custom_call_target="tpu_custom_call" | custom-call | flops 655360 | bytes 7864320 | tf_op jit(solution)/shard_map/split/pallas_call | solution.py:422
  94.2 2.0 %collective-permute-start.14 = (f32[160,1024]{1,0:T(8,128)S(1)}, f32[160,1024]{1,0:T(8,128)S(1)}, u32[]{:S(2)}, u32[]{:S(2)}) collective-permute-start(f32[160,1024]{1,0:T(8,128)S(1)} %get-tuple-element.49), channel_id=1, source_target_pairs={{0,16},{8,24},{16,0},{24,8},{1,17},{9,25},{17,1},{25,9},{2,18},{10... | collective-permute-start | bytes 1966088 | tf_op jit(solution)/shard_map/ppermute | solution.py:22
  96.2 3.5 %convolution_convert_fusion.1.qv_ref = bf16[1152,1024]{1,0:T(8,128)(2,1)S(1)} fusion(bf16[1152,1152]{1,0:T(8,128)(2,1)S(1)} %copy-done.14, bf16[1152,1024]{1,0:T(8,128)(2,1)S(1)} %fusion.sl_ref), kind=kOutput, calls=%fused_computation.5 | convolution fusion | flops 2719088640 | bytes 7372800 | tf_op jit(solution)/shard_map/dot_general | solution.py:17
  99.7 3.5 %convolution_convert_fusion.2.qk_ref = bf16[1152,1024]{1,0:T(8,128)(2,1)S(1)} fusion(bf16[1152,1152]{1,0:T(8,128)(2,1)S(1)} %copy-done.15, bf16[1152,1024]{1,0:T(8,128)(2,1)S(1)} %copy-done.12), kind=kOutput, calls=%fused_computation.6 | convolution fusion | flops 2719088640 | bytes 7372800 | tf_op jit(solution)/shard_map/dot_general | solution.py:17
  103.2 4.0 %collective-permute-done.22 = f32[4,40,1024]{2,1,0:T(8,128)S(1)} collective-permute-done((f32[4,40,1024]{2,1,0:T(8,128)S(1)}, f32[4,40,1024]{2,1,0:T(8,128)S(1)}, u32[]{:S(2)}, u32[]{:S(2)}) %collective-permute-start.22) | collective-permute-done | bytes 655392 | tf_op jit(solution)/shard_map/ppermute | solution.py:22
  107.2 0.6 collective-permute-start.15
  107.8 13.0 %back.1 = bf16[1458,1152]{1,0:T(8,128)(2,1)} custom-call(bf16[1536,1024]{1,0:T(8,128)(2,1)S(1)} %copy-done.11, bf16[1536,1024]{1,0:T(8,128)(2,1)S(1)} %copy-done.8, bf16[1152,1024]{1,0:T(8,128)(2,1)S(1)} %convolution_convert_fusion.2.qk_ref, bf16[1152,1024]{1,0:T(8,128)(2,1)S(1)} %convolution_convert_fusion.1.qv_ref, ...), custom_call_target="tpu_custom_call" | custom-call | flops 7247757312 | bytes 18087936 | tf_op jit(solution)/shard_map/back/pallas_call | solution.py:82
  120.8 1.5 collective-permute-done.20
  122.3 0.3 add_multiply_fusion
  122.7 3.2 %collective-permute-start.25 = (f32[40,1024]{1,0:T(8,128)S(1)}, f32[40,1024]{1,0:T(8,128)S(1)}, u32[]{:S(2)}, u32[]{:S(2)}) collective-permute-start(f32[40,1024]{1,0:T(8,128)S(1)} %get-tuple-element.69), channel_id=1, source_target_pairs={{0,24},{8,0},{16,8},{24,16},{1,25},{9,1},{17,9},{25,17},{2,26},{10... | collective-permute-start | bytes 491528 | tf_op jit(solution)/shard_map/ppermute | solution.py:22
  126.0 1.0 collective-permute-done.15
  127.0 0.2 add_add_fusion
  127.3 2.4 %collective-permute-start.16 = (f32[40,1024]{1,0:T(8,128)S(1)}, f32[40,1024]{1,0:T(8,128)S(1)}, u32[]{:S(2)}, u32[]{:S(2)}) collective-permute-start(f32[40,1024]{1,0:T(8,128)S(1)} %get-tuple-element.65), channel_id=1, source_target_pairs={{0,2},{2,4},{4,6},{6,0},{1,3},{3,5},{5,7},{7,1},{8,10},{10,12},{12... | collective-permute-start | bytes 491528 | tf_op jit(solution)/shard_map/ppermute | solution.py:22
  129.7 1.2 collective-permute-start.18
  130.9 2.7 %collective-permute-done.23 = f32[40,1024]{1,0:T(8,128)S(1)} collective-permute-done((f32[40,1024]{1,0:T(8,128)S(1)}, f32[40,1024]{1,0:T(8,128)S(1)}, u32[]{:S(2)}, u32[]{:S(2)}) %collective-permute-start.23) | collective-permute-done | bytes 163872 | tf_op jit(solution)/shard_map/ppermute | solution.py:22
  133.6 1.2 collective-permute-start.17
  134.8 0.8 fusion.36
  135.6 0.8 collective-permute-done.18
  136.4 4.0 %collective-permute-done.17 = f32[40,1024]{1,0:T(8,128)S(1)} collective-permute-done((f32[40,1024]{1,0:T(8,128)S(1)}, f32[40,1024]{1,0:T(8,128)S(1)}, u32[]{:S(2)}, u32[]{:S(2)}) %collective-permute-start.17) | collective-permute-done | bytes 163872 | tf_op jit(solution)/shard_map/ppermute | solution.py:22
  140.4 0.8 fusion.34
  141.3 2.0 %collective-permute-start.26 = (f32[9,2304]{1,0:T(8,128)S(1)}, f32[9,2304]{1,0:T(8,128)S(1)}, u32[]{:S(2)}, u32[]{:S(2)}) collective-permute-start(f32[9,2304]{1,0:T(8,128)S(1)} %get-tuple-element.77), channel_id=1, source_target_pairs={{0,32},{32,64},{64,96},{96,0},{1,33},{33,65},{65,97},{97,1},{2,34}... | collective-permute-start | bytes 248840 | tf_op jit(solution)/shard_map/ppermute | solution.py:22
  143.2 2.2 %collective-permute-start.28 = (f32[9,2304]{1,0:T(8,128)S(1)}, f32[9,2304]{1,0:T(8,128)S(1)}, u32[]{:S(2)}, u32[]{:S(2)}) collective-permute-start(f32[9,2304]{1,0:T(8,128)S(1)} %get-tuple-element.78), channel_id=1, source_target_pairs={{0,96},{32,0},{64,32},{96,64},{1,97},{33,1},{65,33},{97,65},{2,98}... | collective-permute-start | bytes 248840 | tf_op jit(solution)/shard_map/ppermute | solution.py:22
  145.4 1.8 %collective-permute-start.27 = (f32[9,2304]{1,0:T(8,128)S(1)}, f32[9,2304]{1,0:T(8,128)S(1)}, u32[]{:S(2)}, u32[]{:S(2)}) collective-permute-start(f32[9,2304]{1,0:T(8,128)S(1)} %get-tuple-element.79), channel_id=1, source_target_pairs={{0,64},{32,96},{64,0},{96,32},{1,65},{33,97},{65,1},{97,33},{2,66}... | collective-permute-start | bytes 248840 | tf_op jit(solution)/shard_map/ppermute | solution.py:22
  147.2 0.8 fusion.6
  148.0 1.1 collective-permute-done.26
  149.1 3.0 %collective-permute-done.27 = f32[9,2304]{1,0:T(8,128)S(1)} collective-permute-done((f32[9,2304]{1,0:T(8,128)S(1)}, f32[9,2304]{1,0:T(8,128)S(1)}, u32[]{:S(2)}, u32[]{:S(2)}) %collective-permute-start.27) | collective-permute-done | bytes 82976 | tf_op jit(solution)/shard_map/ppermute | solution.py:22
  152.1 0.7 fusion.28
  (102 shorter events, 2.3 us)
Async XLA Ops:
  0.6 1.2 copy-start
  2.3 23.5 %collective-permute-start = (f32[72,1024]{1,0:T(8,128)S(1)}, f32[72,1024]{1,0:T(8,128)S(1)}, u32[]{:S(2)}, u32[]{:S(2)}) collective-permute-start(f32[72,1024]{1,0:T(8,128)S(1)} %copy.16), channel_id=1, source_target_pairs={{0,1},{1,0},{2,3},{3,2},{4,5},{5,4},{6,7},{7,6},{8,9},{9,8},{10,11... | collective-permute-start | bytes 884744 | tf_op jit(solution)/shard_map/ppermute | solution.py:22
  25.9 5.5 %collective-permute-start.1 = (f32[72,128]{1,0:T(8,128)S(1)}, f32[72,128]{1,0:T(8,128)S(1)}, u32[]{:S(2)}, u32[]{:S(2)}) collective-permute-start(f32[72,128]{1,0:T(8,128)S(1)} %get-tuple-element.82), channel_id=1, source_target_pairs={{0,8},{8,16},{16,24},{24,0},{1,9},{9,17},{17,25},{25,1},{2,10},{10... | collective-permute-start | bytes 110600 | tf_op jit(solution)/shard_map/ppermute | solution.py:22
  27.7 4.0 %collective-permute-start.3 = (f32[72,128]{1,0:T(8,128)S(1)}, f32[72,128]{1,0:T(8,128)S(1)}, u32[]{:S(2)}, u32[]{:S(2)}) collective-permute-start(f32[72,128]{1,0:T(8,128)S(1)} %get-tuple-element.83), channel_id=1, source_target_pairs={{0,24},{8,0},{16,8},{24,16},{1,25},{9,1},{17,9},{25,17},{2,26},{10... | collective-permute-start | bytes 110600 | tf_op jit(solution)/shard_map/ppermute | solution.py:22
  29.3 5.5 %collective-permute-start.2 = (f32[72,128]{1,0:T(8,128)S(1)}, f32[72,128]{1,0:T(8,128)S(1)}, u32[]{:S(2)}, u32[]{:S(2)}) collective-permute-start(f32[72,128]{1,0:T(8,128)S(1)} %get-tuple-element.84), channel_id=1, source_target_pairs={{0,16},{8,24},{16,0},{24,8},{1,17},{9,25},{17,1},{25,9},{2,18},{10... | collective-permute-start | bytes 110600 | tf_op jit(solution)/shard_map/ppermute | solution.py:22
  34.7 1.9 %collective-permute-start.4 = (f32[80,1024]{1,0:T(8,128)}, f32[80,1024]{1,0:T(8,128)S(1)}, u32[]{:S(2)}, u32[]{:S(2)}) collective-permute-start(f32[80,1024]{1,0:T(8,128)} %get-tuple-element.30.own_ref), channel_id=1, source_target_pairs={{0,1},{1,0},{2,3},{3,2},{4,5},{5,4},{6,7},{7,6},{8,9},{9,8},{10,11... | collective-permute-start | bytes 983048 | tf_op jit(solution)/shard_map/ppermute | solution.py:22
  36.7 1.0 copy-start.4
  37.7 13.0 %collective-permute-start.7 = (f32[112,512]{1,0:T(8,128)S(1)}, f32[112,512]{1,0:T(8,128)S(1)}, u32[]{:S(2)}, u32[]{:S(2)}) collective-permute-start(f32[112,512]{1,0:T(8,128)S(1)} %pair.1), channel_id=1, source_target_pairs={{0,6},{2,0},{4,2},{6,4},{1,7},{3,1},{5,3},{7,5},{8,14},{10,8},{12,... | collective-permute-start | bytes 688136 | tf_op jit(solution)/shard_map/ppermute | solution.py:22
  40.6 10.1 %collective-permute-start.6 = (f32[112,512]{1,0:T(8,128)S(1)}, f32[112,512]{1,0:T(8,128)S(1)}, u32[]{:S(2)}, u32[]{:S(2)}) collective-permute-start(f32[112,512]{1,0:T(8,128)S(1)} %pair.1), channel_id=1, source_target_pairs={{0,4},{2,6},{4,0},{6,2},{1,5},{3,7},{5,1},{7,3},{8,12},{10,14},{12... | collective-permute-start | bytes 688136 | tf_op jit(solution)/shard_map/ppermute | solution.py:22
  41.4 13.0 %collective-permute-start.5 = (f32[112,512]{1,0:T(8,128)S(1)}, f32[112,512]{1,0:T(8,128)S(1)}, u32[]{:S(2)}, u32[]{:S(2)}) collective-permute-start(f32[112,512]{1,0:T(8,128)S(1)} %pair.1), channel_id=1, source_target_pairs={{0,2},{2,4},{4,6},{6,0},{1,3},{3,5},{5,7},{7,1},{8,10},{10,12},{12... | collective-permute-start | bytes 688136 | tf_op jit(solution)/shard_map/ppermute | solution.py:22
  42.3 15.8 %copy-start.7 = (bf16[1536,1024]{1,0:T(8,128)(2,1)S(1)}, bf16[1536,1024]{1,0:T(8,128)(2,1)}, u32[]{:S(2)}) copy-start(bf16[1536,1024]{1,0:T(8,128)(2,1)} %get-tuple-element.36.e_ref) | copy-start | bytes 9437188
  54.5 11.2 %collective-permute-start.10 = (f32[104,512]{1,0:T(8,128)S(1)}, f32[104,512]{1,0:T(8,128)S(1)}, u32[]{:S(2)}, u32[]{:S(2)}) collective-permute-start(f32[104,512]{1,0:T(8,128)S(1)} %pad_maximum_fusion.1), channel_id=1, source_target_pairs={{0,24},{8,0},{16,8},{24,16},{1,25},{9,1},{17,9},{25,17},{2,26},{10... | collective-permute-start | bytes 638984 | tf_op jit(solution)/shard_map/ppermute | solution.py:22
  56.4 9.7 %collective-permute-start.9 = (f32[104,512]{1,0:T(8,128)S(1)}, f32[104,512]{1,0:T(8,128)S(1)}, u32[]{:S(2)}, u32[]{:S(2)}) collective-permute-start(f32[104,512]{1,0:T(8,128)S(1)} %pad_maximum_fusion.1), channel_id=1, source_target_pairs={{0,16},{8,24},{16,0},{24,8},{1,17},{9,25},{17,1},{25,9},{2,18},{10... | collective-permute-start | bytes 638984 | tf_op jit(solution)/shard_map/ppermute | solution.py:22
  57.0 12.3 %collective-permute-start.8 = (f32[104,512]{1,0:T(8,128)S(1)}, f32[104,512]{1,0:T(8,128)S(1)}, u32[]{:S(2)}, u32[]{:S(2)}) collective-permute-start(f32[104,512]{1,0:T(8,128)S(1)} %pad_maximum_fusion.1), channel_id=1, source_target_pairs={{0,8},{8,16},{16,24},{24,0},{1,9},{9,17},{17,25},{25,1},{2,10},{10... | collective-permute-start | bytes 638984 | tf_op jit(solution)/shard_map/ppermute | solution.py:22
  69.8 3.3 %copy-start.9 = (bf16[1536,1152]{1,0:T(8,128)(2,1)S(1)}, bf16[1536,1152]{1,0:T(8,128)(2,1)}, u32[]{:S(2)}) copy-start(bf16[1536,1152]{1,0:T(8,128)(2,1)} %get-tuple-element.38.v_ref) | copy-start | bytes 10616836
  69.8 1.7 %collective-permute-start.11 = (f32[152,512]{1,0:T(8,128)S(1)}, f32[152,512]{1,0:T(8,128)S(1)}, u32[]{:S(2)}, u32[]{:S(2)}) collective-permute-start(f32[152,512]{1,0:T(8,128)S(1)} %pad_maximum_fusion), channel_id=1, source_target_pairs={{0,1},{1,0},{2,3},{3,2},{4,5},{5,4},{6,7},{7,6},{8,9},{9,8},{10,11... | collective-permute-start | bytes 933896 | tf_op jit(solution)/shard_map/ppermute | solution.py:22
  69.9 16.0 %collective-permute-start.19 = (f32[640,1024]{1,0:T(8,128)}, f32[640,1024]{1,0:T(8,128)}, u32[]{:S(2)}, u32[]{:S(2)}) collective-permute-start(f32[640,1024]{1,0:T(8,128)} %fusion.2), channel_id=1, source_target_pairs={{0,1},{1,0},{2,3},{3,2},{4,5},{5,4},{6,7},{7,6},{8,9},{9,8},{10,11... | collective-permute-start | bytes 7864328 | tf_op jit(solution)/shard_map/ppermute | solution.py:22
  81.6 1.5 copy-start.2
  83.1 1.7 %copy-start.10 = (bf16[1536,1024]{1,0:T(8,128)(2,1)}, bf16[1536,1024]{1,0:T(8,128)(2,1)S(1)}, u32[]{:S(2)}) copy-start(bf16[1536,1024]{1,0:T(8,128)(2,1)S(1)} %get-tuple-element.43.d_ref) | copy-start | bytes 9437188
  84.8 7.1 %collective-permute-start.12 = (f32[640,1024]{1,0:T(8,128)}, f32[640,1024]{1,0:T(8,128)}, u32[]{:S(2)}, u32[]{:S(2)}) collective-permute-start(f32[640,1024]{1,0:T(8,128)} %get-tuple-element.41), channel_id=1, source_target_pairs={{0,1},{1,0},{2,3},{3,2},{4,5},{5,4},{6,7},{7,6},{8,9},{9,8},{10,11... | collective-permute-start | bytes 7864328 | tf_op jit(solution)/shard_map/ppermute | solution.py:22
  89.3 2.6 %copy-start.3 = (f32[640,1024]{1,0:T(8,128)S(1)}, f32[640,1024]{1,0:T(8,128)}, u32[]{:S(2)}) copy-start(f32[640,1024]{1,0:T(8,128)} %copy-done.2) | copy-start | bytes 7864324
  89.6 17.6 %collective-permute-start.22 = (f32[4,40,1024]{2,1,0:T(8,128)S(1)}, f32[4,40,1024]{2,1,0:T(8,128)S(1)}, u32[]{:S(2)}, u32[]{:S(2)}) collective-permute-start(f32[4,40,1024]{2,1,0:T(8,128)S(1)} %bitcast.110), channel_id=1, source_target_pairs={{0,6},{2,0},{4,2},{6,4},{1,7},{3,1},{5,3},{7,5},{8,14},{10,8},{12,... | collective-permute-start | bytes 1966088 | tf_op jit(solution)/shard_map/ppermute | solution.py:22
  89.7 31.2 %collective-permute-start.21 = (f32[4,40,1024]{2,1,0:T(8,128)S(1)}, f32[4,40,1024]{2,1,0:T(8,128)S(1)}, u32[]{:S(2)}, u32[]{:S(2)}) collective-permute-start(f32[4,40,1024]{2,1,0:T(8,128)S(1)} %bitcast.109), channel_id=1, source_target_pairs={{0,4},{2,6},{4,0},{6,2},{1,5},{3,7},{5,1},{7,3},{8,12},{10,14},{12... | collective-permute-start | bytes 1966088 | tf_op jit(solution)/shard_map/ppermute | solution.py:22
  90.6 31.7 %collective-permute-start.20 = (f32[4,40,1024]{2,1,0:T(8,128)S(1)}, f32[4,40,1024]{2,1,0:T(8,128)S(1)}, u32[]{:S(2)}, u32[]{:S(2)}) collective-permute-start(f32[4,40,1024]{2,1,0:T(8,128)S(1)} %bitcast.108), channel_id=1, source_target_pairs={{0,2},{2,4},{4,6},{6,0},{1,3},{3,5},{5,7},{7,1},{8,10},{10,12},{12... | collective-permute-start | bytes 1966088 | tf_op jit(solution)/shard_map/ppermute | solution.py:22
  91.9 4.3 %copy-start.14 = (bf16[1152,1152]{1,0:T(8,128)(2,1)S(1)}, bf16[1152,1152]{1,0:T(8,128)(2,1)}, u32[]{:S(2)}) copy-start(bf16[1152,1152]{1,0:T(8,128)(2,1)} %wv_far.1) | copy-start | bytes 7962628
  94.1 31.9 %collective-permute-start.13 = (f32[160,1024]{1,0:T(8,128)S(1)}, f32[160,1024]{1,0:T(8,128)S(1)}, u32[]{:S(2)}, u32[]{:S(2)}) collective-permute-start(f32[160,1024]{1,0:T(8,128)S(1)} %get-tuple-element.48), channel_id=1, source_target_pairs={{0,8},{8,16},{16,24},{24,0},{1,9},{9,17},{17,25},{25,1},{2,10},{10... | collective-permute-start | bytes 1966088 | tf_op jit(solution)/shard_map/ppermute | solution.py:22
  94.1 5.5 %copy-start.12 = (bf16[1152,1024]{1,0:T(8,128)(2,1)S(1)}, bf16[1152,1024]{1,0:T(8,128)(2,1)}, u32[]{:S(2)}) copy-start(bf16[1152,1024]{1,0:T(8,128)(2,1)} %get-tuple-element.45) | copy-start | bytes 7077892
  94.1 5.5 %copy-start.15 = (bf16[1152,1152]{1,0:T(8,128)(2,1)S(1)}, bf16[1152,1152]{1,0:T(8,128)(2,1)}, u32[]{:S(2)}) copy-start(bf16[1152,1152]{1,0:T(8,128)(2,1)} %wk_far.1) | copy-start | bytes 7962628
  94.2 31.8 %collective-permute-start.14 = (f32[160,1024]{1,0:T(8,128)S(1)}, f32[160,1024]{1,0:T(8,128)S(1)}, u32[]{:S(2)}, u32[]{:S(2)}) collective-permute-start(f32[160,1024]{1,0:T(8,128)S(1)} %get-tuple-element.49), channel_id=1, source_target_pairs={{0,16},{8,24},{16,0},{24,8},{1,17},{9,25},{17,1},{25,9},{2,18},{10... | collective-permute-start | bytes 1966088 | tf_op jit(solution)/shard_map/ppermute | solution.py:22
  99.7 8.1 %copy-start.5 = (bf16[1,1458,1152]{2,1,0:T(8,128)(2,1)S(1)}, bf16[1,1458,1152]{2,1,0:T(8,128)(2,1)}, u32[]{:S(2)}) copy-start(bf16[1,1458,1152]{2,1,0:T(8,128)(2,1)} %param.8) | copy-start | bytes 10077700
  99.7 8.1 %copy-start.6 = (bf16[1152]{0:T(1024)(128)(2,1)S(1)}, bf16[1152]{0:T(1024)(128)(2,1)}, u32[]{:S(2)}) copy-start(bf16[1152]{0:T(1024)(128)(2,1)} %gain_ref.3) | copy-start | bytes 6916
  99.7 8.1 %copy-start.8 = (bf16[1536,1024]{1,0:T(8,128)(2,1)S(1)}, bf16[1536,1024]{1,0:T(8,128)(2,1)}, u32[]{:S(2)}) copy-start(bf16[1536,1024]{1,0:T(8,128)(2,1)} %get-tuple-element.36.e_ref) | copy-start | bytes 9437188
  99.7 8.1 %copy-start.11 = (bf16[1536,1024]{1,0:T(8,128)(2,1)S(1)}, bf16[1536,1024]{1,0:T(8,128)(2,1)}, u32[]{:S(2)}) copy-start(bf16[1536,1024]{1,0:T(8,128)(2,1)} %copy-done.10) | copy-start | bytes 9437188
  107.2 19.8 %collective-permute-start.15 = (f32[160,1024]{1,0:T(8,128)S(1)}, f32[160,1024]{1,0:T(8,128)S(1)}, u32[]{:S(2)}, u32[]{:S(2)}) collective-permute-start(f32[160,1024]{1,0:T(8,128)S(1)} %get-tuple-element.50), channel_id=1, source_target_pairs={{0,24},{8,0},{16,8},{24,16},{1,25},{9,1},{17,9},{25,17},{2,26},{10... | collective-permute-start | bytes 1966088 | tf_op jit(solution)/shard_map/ppermute | solution.py:22
  122.7 10.9 %collective-permute-start.23 = (f32[40,1024]{1,0:T(8,128)S(1)}, f32[40,1024]{1,0:T(8,128)S(1)}, u32[]{:S(2)}, u32[]{:S(2)}) collective-permute-start(f32[40,1024]{1,0:T(8,128)S(1)} %get-tuple-element.68), channel_id=1, source_target_pairs={{0,8},{8,16},{16,24},{24,0},{1,9},{9,17},{17,25},{25,1},{2,10},{10... | collective-permute-start | bytes 491528 | tf_op jit(solution)/shard_map/ppermute | solution.py:22
  122.7 12.0 %collective-permute-start.25 = (f32[40,1024]{1,0:T(8,128)S(1)}, f32[40,1024]{1,0:T(8,128)S(1)}, u32[]{:S(2)}, u32[]{:S(2)}) collective-permute-start(f32[40,1024]{1,0:T(8,128)S(1)} %get-tuple-element.69), channel_id=1, source_target_pairs={{0,24},{8,0},{16,8},{24,16},{1,25},{9,1},{17,9},{25,17},{2,26},{10... | collective-permute-start | bytes 491528 | tf_op jit(solution)/shard_map/ppermute | solution.py:22
  126.0 8.8 %collective-permute-start.24 = (f32[40,1024]{1,0:T(8,128)S(1)}, f32[40,1024]{1,0:T(8,128)S(1)}, u32[]{:S(2)}, u32[]{:S(2)}) collective-permute-start(f32[40,1024]{1,0:T(8,128)S(1)} %get-tuple-element.70), channel_id=1, source_target_pairs={{0,16},{8,24},{16,0},{24,8},{1,17},{9,25},{17,1},{25,9},{2,18},{10... | collective-permute-start | bytes 491528 | tf_op jit(solution)/shard_map/ppermute | solution.py:22
  127.3 8.3 %collective-permute-start.16 = (f32[40,1024]{1,0:T(8,128)S(1)}, f32[40,1024]{1,0:T(8,128)S(1)}, u32[]{:S(2)}, u32[]{:S(2)}) collective-permute-start(f32[40,1024]{1,0:T(8,128)S(1)} %get-tuple-element.65), channel_id=1, source_target_pairs={{0,2},{2,4},{4,6},{6,0},{1,3},{3,5},{5,7},{7,1},{8,10},{10,12},{12... | collective-permute-start | bytes 491528 | tf_op jit(solution)/shard_map/ppermute | solution.py:22
  129.7 6.7 %collective-permute-start.18 = (f32[40,1024]{1,0:T(8,128)S(1)}, f32[40,1024]{1,0:T(8,128)S(1)}, u32[]{:S(2)}, u32[]{:S(2)}) collective-permute-start(f32[40,1024]{1,0:T(8,128)S(1)} %get-tuple-element.66), channel_id=1, source_target_pairs={{0,6},{2,0},{4,2},{6,4},{1,7},{3,1},{5,3},{7,5},{8,14},{10,8},{12,... | collective-permute-start | bytes 491528 | tf_op jit(solution)/shard_map/ppermute | solution.py:22
  133.6 6.8 %collective-permute-start.17 = (f32[40,1024]{1,0:T(8,128)S(1)}, f32[40,1024]{1,0:T(8,128)S(1)}, u32[]{:S(2)}, u32[]{:S(2)}) collective-permute-start(f32[40,1024]{1,0:T(8,128)S(1)} %get-tuple-element.67), channel_id=1, source_target_pairs={{0,4},{2,6},{4,0},{6,2},{1,5},{3,7},{5,1},{7,3},{8,12},{10,14},{12... | collective-permute-start | bytes 491528 | tf_op jit(solution)/shard_map/ppermute | solution.py:22
  134.7 18.0 %copy-start.1 = (bf16[1,64,36]{1,2,0:T(8,128)(2,1)S(1)}, bf16[1,64,36]{1,2,0:T(8,128)(2,1)}, u32[]{:S(2)}) copy-start(bf16[1,64,36]{1,2,0:T(8,128)(2,1)} %param.15) | copy-start | bytes 13828
  135.6 11.7 %copy-start.13 = (bf16[1152,36]{0,1:T(8,128)(2,1)S(1)}, bf16[1152,36]{0,1:T(8,128)(2,1)}, u32[]{:S(2)}) copy-start(bf16[1152,36]{0,1:T(8,128)(2,1)} %param.14) | copy-start | bytes 248836
  141.3 7.9 %collective-permute-start.26 = (f32[9,2304]{1,0:T(8,128)S(1)}, f32[9,2304]{1,0:T(8,128)S(1)}, u32[]{:S(2)}, u32[]{:S(2)}) collective-permute-start(f32[9,2304]{1,0:T(8,128)S(1)} %get-tuple-element.77), channel_id=1, source_target_pairs={{0,32},{32,64},{64,96},{96,0},{1,33},{33,65},{65,97},{97,1},{2,34}... | collective-permute-start | bytes 248840 | tf_op jit(solution)/shard_map/ppermute | solution.py:22
  143.2 5.9 %collective-permute-start.28 = (f32[9,2304]{1,0:T(8,128)S(1)}, f32[9,2304]{1,0:T(8,128)S(1)}, u32[]{:S(2)}, u32[]{:S(2)}) collective-permute-start(f32[9,2304]{1,0:T(8,128)S(1)} %get-tuple-element.78), channel_id=1, source_target_pairs={{0,96},{32,0},{64,32},{96,64},{1,97},{33,1},{65,33},{97,65},{2,98}... | collective-permute-start | bytes 248840 | tf_op jit(solution)/shard_map/ppermute | solution.py:22
  145.4 6.6 %collective-permute-start.27 = (f32[9,2304]{1,0:T(8,128)S(1)}, f32[9,2304]{1,0:T(8,128)S(1)}, u32[]{:S(2)}, u32[]{:S(2)}) collective-permute-start(f32[9,2304]{1,0:T(8,128)S(1)} %get-tuple-element.79), channel_id=1, source_target_pairs={{0,64},{32,96},{64,0},{96,32},{1,65},{33,97},{65,1},{97,33},{2,66}... | collective-permute-start | bytes 248840 | tf_op jit(solution)/shard_map/ppermute | solution.py:22

commit v6 on v4

--- a/solution.py
+++ b/solution.py
@@ -60,7 +60,7 @@
     return lax.optimization_barrier((value, *others))[0]
 
 
-STEP = 256
+STEP = 512
 LONG = 512
 GROUP = 4
 WINDOW = 384
@@ -355,8 +355,7 @@
     halves = [half] + [shift(half, "x", k) for k in (1, 2, 3)]
     tops = [h[width + 8 : width + 10].reshape(1, cols) for h in halves]
     top3 = jnp.maximum(jnp.maximum(tops[0], tops[1]), jnp.maximum(tops[2], tops[3]))
-    q_key = dot(after(w_key, turned), spread_q).astype(BF16)
-    halves[0] = after(halves[0], q_key)
+    halves[0] = after(halves[0], turned)
     half = merge([h[: width + 8] for h in halves], width)
     lc = sum(h[width + 16 :] for h in halves)
     lc = whole(lc, shift(lc, "c", 1))
@@ -411,6 +410,7 @@
     )(w, w_got)
 
 
+    q_key = dot(after(w_key, parts[0]), spread_q).astype(BF16)
     q_value = dot(after(w_value, parts[0]), spread_lc).astype(BF16)
     patch_grad = call(
         back_kernel,

time: 152 us -> 152 us (level)
    unnamed x41 -> x37, local copies, waits for them, and re-layouts: 4.23 us -> 4.22 us
  transfers between devices with their start and end apart: 30 -> 30, of which waited for: 13 -> 13; matrix products, arithmetic and copies ran while one was open for 21% -> 20% of each run, Pallas kernels for 31% -> 30%
where the time goes in v6:
time: 152 us; the launch traced here: 151 us
  Pallas kernels  45.9 us (30%)
  starting transfers between devices  42.5 us (28%)
  matrix products  24.9 us (16%)
  waiting for transfers between devices  23.8 us (16%)
  local copies, waits for them, and re-layouts  6.91 us (5%)
  other arithmetic  6.37 us (4%)
    pallas_call x3, Pallas kernels, call(): pl.pallas_call(body, grid=(steps,), in_specs=[spec(b, m, 1) for _, b, m i...  43.7 us
    ppermute x30, starting transfers between devices, shift(): return lax.ppermute(value, axis, [(i, (i + step) % n) for i in range(n)])  42.5 us
    dot_general x9, matrix products, dot(): lax.dot_general(a, b, (((ca,), (cb,)), ((), ())), preferred_element_type=...  24.9 us
    ppermute x30, waiting for transfers between devices, shift(): return lax.ppermute(value, axis, [(i, (i + step) % n) for i in range(n)])  23.8 us
    unnamed x37, local copies, waits for them, and re-layouts  4.22 us
    add x1, other arithmetic, per_device(): after(u, w_send) * jnp.exp(top - top2) + u_got * jnp.exp(top_pair - top2)  3.16 us
  transfers between devices with their start and end apart: 30, of which 13 were waited for; matrix products, arithmetic and copies ran while one was open for 20% of the time, Pallas kernels for 30%

profile of v6, /device:TPU:0, one launch (start us, length us, event | category | flops | bytes accessed | tf_op | source)
XLA Modules:
  0.0 151.3 jit_solution(2058276531040281484)
XLA Ops:
  0.6 1.2 dot_general.29
  1.8 0.3 fusion.18
  2.5 1.4 collective-permute-done
  4.0 3.4 %collective-permute-start.2 = (f32[72,512]{1,0:T(8,128)S(1)}, f32[72,512]{1,0:T(8,128)S(1)}, u32[]{:S(2)}, u32[]{:S(2)}) collective-permute-start(f32[72,512]{1,0:T(8,128)S(1)} %dynamic-slice_add_fusion), channel_id=1, source_target_pairs={{0,16},{8,24},{16,0},{24,8},{1,17},{9,25},{17,1},{25,9},{2,18},{10... | collective-permute-start | bytes 442376 | tf_op jit(solution)/shard_map/ppermute | solution.py:22
  7.3 0.7 collective-permute-start.1
  8.0 2.6 %collective-permute-start.3 = (f32[72,512]{1,0:T(8,128)S(1)}, f32[72,512]{1,0:T(8,128)S(1)}, u32[]{:S(2)}, u32[]{:S(2)}) collective-permute-start(f32[72,512]{1,0:T(8,128)S(1)} %dynamic-slice_add_fusion), channel_id=1, source_target_pairs={{0,24},{8,0},{16,8},{24,16},{1,25},{9,1},{17,9},{25,17},{2,26},{10... | collective-permute-start | bytes 442376 | tf_op jit(solution)/shard_map/ppermute | solution.py:22
  10.6 22.4 %softmax.1 = (bf16[1536,1152]{1,0:T(8,128)(2,1)}, bf16[1536,1152]{1,0:T(8,128)(2,1)}, bf16[1536,1024]{1,0:T(8,128)(2,1)}, f32[80,1024]{1,0:T(8,128)}, bf16[1152,1024]{1,0:T(8,128)(2,1)}) custom-call(bf16[1458,1152]{1,0:T(8,128)(2,1)} %bitcast.85, bf16[1152]{0:T(1024)(128)(2,1)} %gain_ref.3, bf16[1152,1152]{1,0:T(8,128)(2,1)} %wk_far.1, ...), custom_call_target="tpu_custom_call" | custom-call | flops 10569646080 | bytes 21430272 | tf_op jit(solution)/shard_map/softmax/pallas_call | solution.py:82
  33.3 1.7 %collective-permute-done.4.got_ref = f32[80,1024]{1,0:T(8,128)S(1)} collective-permute-done((f32[80,1024]{1,0:T(8,128)}, f32[80,1024]{1,0:T(8,128)S(1)}, u32[]{:S(2)}, u32[]{:S(2)}) %collective-permute-start.4) | collective-permute-done | bytes 327712 | tf_op jit(solution)/shard_map/ppermute | solution.py:22
  35.0 1.0 copy-done.4
  36.0 2.8 %collective-permute-start.7 = (f32[160,512]{1,0:T(8,128)S(1)}, f32[160,512]{1,0:T(8,128)S(1)}, u32[]{:S(2)}, u32[]{:S(2)}) collective-permute-start(f32[160,512]{1,0:T(8,128)S(1)} %pair.1), channel_id=1, source_target_pairs={{0,6},{2,0},{4,2},{6,4},{1,7},{3,1},{5,3},{7,5},{8,14},{10,8},{12,... | collective-permute-start | bytes 983048 | tf_op jit(solution)/shard_map/ppermute | solution.py:22
  38.9 0.8 collective-permute-start.6
  39.7 0.9 collective-permute-start.5
  40.6 7.8 %convolution_convert_fusion.t_ref = bf16[1280,1536]{1,0:T(8,128)(2,1)S(1)} fusion(bf16[1536,1152]{1,0:T(8,128)(2,1)} %get-tuple-element.34, s32[1280]{0:T(1024)S(1)} %fusion.42), kind=kOutput, calls=%fused_computation | convolution fusion | flops 4533288960 | bytes 7476224 | tf_op jit(solution)/shard_map/dot_general | solution.py:17
  48.4 4.8 %collective-permute-done.7 = f32[160,512]{1,0:T(8,128)S(1)} collective-permute-done((f32[160,512]{1,0:T(8,128)S(1)}, f32[160,512]{1,0:T(8,128)S(1)}, u32[]{:S(2)}, u32[]{:S(2)}) %collective-permute-start.7) | collective-permute-done | bytes 327712 | tf_op jit(solution)/shard_map/ppermute | solution.py:22
  53.2 3.7 %collective-permute-done.5 = f32[160,512]{1,0:T(8,128)S(1)} collective-permute-done((f32[160,512]{1,0:T(8,128)S(1)}, f32[160,512]{1,0:T(8,128)S(1)}, u32[]{:S(2)}, u32[]{:S(2)}) %collective-permute-start.5) | collective-permute-done | bytes 327712 | tf_op jit(solution)/shard_map/ppermute | solution.py:22
  57.1 1.5 collective-permute-start.10
  58.6 0.5 collective-permute-start.9
  59.1 3.7 %fusion.2 = f32[640,1024]{1,0:T(8,128)} fusion(bf16[1536,1024]{1,0:T(8,128)(2,1)S(1)} %copy-done.7, bf16[1280,1536]{1,0:T(8,128)(2,1)S(1)} %convolution_convert_fusion.t_ref), kind=kOutput, calls=%fused_computation.9 | convolution fusion | flops 2013265920 | bytes 7733248 | tf_op jit(solution)/shard_map/dot_general | solution.py:17
  62.9 0.6 collective-permute-start.8
  63.5 3.8 %fusion.4 = f32[640,1024]{1,0:T(8,128)} fusion(bf16[1536,1024]{1,0:T(8,128)(2,1)S(1)} %copy-done.7, bf16[1280,1536]{1,0:T(8,128)(2,1)S(1)} %convolution_convert_fusion.t_ref), kind=kOutput, calls=%fused_computation.11 | convolution fusion | flops 2013265920 | bytes 7733248 | tf_op jit(solution)/shard_map/dot_general | solution.py:17
  67.3 0.3 collective-permute-done.8
  67.6 0.5 fusion.sl_ref
  68.4 0.4 collective-permute-start.12
  68.8 1.1 collective-permute-done.12
  69.9 0.8 broadcast_multiply_fusion
  70.9 8.7 %gradient.1 = (bf16[1536,1024]{1,0:T(8,128)(2,1)S(1)}, f32[640,1024]{1,0:T(8,128)S(1)}, f32[640,1024]{1,0:T(8,128)}) custom-call(bf16[1536,1152]{1,0:T(8,128)(2,1)S(1)} %copy-done.9, bf16[1152,1024]{1,0:T(8,128)(2,1)S(1)} %fusion.sl_ref, bf16[1536,1024]{1,0:T(8,128)(2,1)S(1)} %copy-done.7, f32[8,1024]{1,0:T(8,128)S(1)} %maximum_maximum_fusion.state_ref, ...), custom_call_target="tpu_custom_call" | custom-call | flops 5234491392 | bytes 21233664 | tf_op jit(solution)/shard_map/gradient/pallas_call | solution.py:82
  79.5 1.5 copy-done.2
  81.0 1.7 %copy-done.10 = bf16[1536,1024]{1,0:T(8,128)(2,1)} copy-done((bf16[1536,1024]{1,0:T(8,128)(2,1)}, bf16[1536,1024]{1,0:T(8,128)(2,1)S(1)}, u32[]{:S(2)}) %copy-start.10) | copy-done | bytes 3145752
  82.7 0.3 collective-permute-start.13
  83.3 0.4 copy.15
  83.7 0.3 convert_element_type.39
  84.0 3.2 %multiply_add_fusion = f32[640,1024]{1,0:T(8,128)S(1)} fusion(f32[640,1024]{1,0:T(8,128)} %collective-permute-done.20, f32[640,1024]{1,0:T(8,128)} %fusion.4, f32[1024]{0:T(1024)S(1)} %bitcast.103, f32[1024]{0:T(1024)S(1)} %bitcast.104), kind=kLoop, calls=%fused_computation.8 | loop fusion | flops 1966080 | bytes 7872512 | tf_op jit(solution)/shard_map/add | solution.py:398
  87.2 0.3 fusion.72
  87.5 0.7 collective-permute-start.23
  88.1 0.8 collective-permute-start.22
  89.0 0.8 collective-permute-start.21
  89.8 2.1 %split.1 = (f32[160,1024]{1,0:T(8,128)S(1)}, f32[160,1024]{1,0:T(8,128)S(1)}, f32[160,1024]{1,0:T(8,128)S(1)}, f32[160,1024]{1,0:T(8,128)S(1)}) custom-call(f32[640,1024]{1,0:T(8,128)S(1)} %copy-done.3, f32[640,1024]{1,0:T(8,128)} %collective-permute-done.13.got_ref), custom_call_target="tpu_custom_call" | custom-call | flops 655360 | bytes 7864320 | tf_op jit(solution)/shard_map/split/pallas_call | solution.py:402
  91.9 1.6 %collective-permute-start.14 = (f32[160,1024]{1,0:T(8,128)S(1)}, f32[160,1024]{1,0:T(8,128)S(1)}, u32[]{:S(2)}, u32[]{:S(2)}) collective-permute-start(f32[160,1024]{1,0:T(8,128)S(1)} %get-tuple-element.50), channel_id=1, source_target_pairs={{0,8},{8,16},{16,24},{24,0},{1,9},{9,17},{17,25},{25,1},{2,10},{10... | collective-permute-start | bytes 1966088 | tf_op jit(solution)/shard_map/ppermute | solution.py:22
  93.5 2.9 %collective-permute-start.15 = (f32[160,1024]{1,0:T(8,128)S(1)}, f32[160,1024]{1,0:T(8,128)S(1)}, u32[]{:S(2)}, u32[]{:S(2)}) collective-permute-start(f32[160,1024]{1,0:T(8,128)S(1)} %get-tuple-element.51), channel_id=1, source_target_pairs={{0,16},{8,24},{16,0},{24,8},{1,17},{9,25},{17,1},{25,9},{2,18},{10... | collective-permute-start | bytes 1966088 | tf_op jit(solution)/shard_map/ppermute | solution.py:22
  96.5 3.5 %convolution_convert_fusion.1.qv_ref = bf16[1152,1024]{1,0:T(8,128)(2,1)S(1)} fusion(bf16[1152,1152]{1,0:T(8,128)(2,1)S(1)} %copy-done.14, bf16[1152,1024]{1,0:T(8,128)(2,1)S(1)} %fusion.sl_ref), kind=kOutput, calls=%fused_computation.5 | convolution fusion | flops 2719088640 | bytes 7372800 | tf_op jit(solution)/shard_map/dot_general | solution.py:17
  100.0 3.4 %convolution_convert_fusion.2.qk_ref = bf16[1152,1024]{1,0:T(8,128)(2,1)S(1)} fusion(bf16[1152,1152]{1,0:T(8,128)(2,1)S(1)} %copy-done.15, bf16[1152,1024]{1,0:T(8,128)(2,1)S(1)} %copy-done.12), kind=kOutput, calls=%fused_computation.6 | convolution fusion | flops 2719088640 | bytes 7372800 | tf_op jit(solution)/shard_map/dot_general | solution.py:17
  103.4 1.7 %collective-permute-done.23 = f32[4,40,1024]{2,1,0:T(8,128)S(1)} collective-permute-done((f32[4,40,1024]{2,1,0:T(8,128)S(1)}, f32[4,40,1024]{2,1,0:T(8,128)S(1)}, u32[]{:S(2)}, u32[]{:S(2)}) %collective-permute-start.23) | collective-permute-done | bytes 655392 | tf_op jit(solution)/shard_map/ppermute | solution.py:22
  105.1 2.8 %collective-permute-start.16 = (f32[160,1024]{1,0:T(8,128)S(1)}, f32[160,1024]{1,0:T(8,128)S(1)}, u32[]{:S(2)}, u32[]{:S(2)}) collective-permute-start(f32[160,1024]{1,0:T(8,128)S(1)} %get-tuple-element.52), channel_id=1, source_target_pairs={{0,24},{8,0},{16,8},{24,16},{1,25},{9,1},{17,9},{25,17},{2,26},{10... | collective-permute-start | bytes 1966088 | tf_op jit(solution)/shard_map/ppermute | solution.py:22
  107.9 12.6 %back.1 = bf16[1458,1152]{1,0:T(8,128)(2,1)} custom-call(bf16[1536,1024]{1,0:T(8,128)(2,1)S(1)} %copy-done.11, bf16[1536,1024]{1,0:T(8,128)(2,1)S(1)} %copy-done.8, bf16[1152,1024]{1,0:T(8,128)(2,1)S(1)} %convolution_convert_fusion.2.qk_ref, bf16[1152,1024]{1,0:T(8,128)(2,1)S(1)} %convolution_convert_fusion.1.qv_ref, ...), custom_call_target="tpu_custom_call" | custom-call | flops 7247757312 | bytes 18087936 | tf_op jit(solution)/shard_map/back/pallas_call | solution.py:82
  120.5 0.3 add_multiply_fusion
  120.8 1.4 collective-permute-start.24
  122.1 1.9 %collective-permute-start.26 = (f32[40,1024]{1,0:T(8,128)S(1)}, f32[40,1024]{1,0:T(8,128)S(1)}, u32[]{:S(2)}, u32[]{:S(2)}) collective-permute-start(f32[40,1024]{1,0:T(8,128)S(1)} %get-tuple-element.71), channel_id=1, source_target_pairs={{0,24},{8,0},{16,8},{24,16},{1,25},{9,1},{17,9},{25,17},{2,26},{10... | collective-permute-start | bytes 491528 | tf_op jit(solution)/shard_map/ppermute | solution.py:22
  124.1 2.7 %collective-permute-start.25 = (f32[40,1024]{1,0:T(8,128)S(1)}, f32[40,1024]{1,0:T(8,128)S(1)}, u32[]{:S(2)}, u32[]{:S(2)}) collective-permute-start(f32[40,1024]{1,0:T(8,128)S(1)} %get-tuple-element.72), channel_id=1, source_target_pairs={{0,16},{8,24},{16,0},{24,8},{1,17},{9,25},{17,1},{25,9},{2,18},{10... | collective-permute-start | bytes 491528 | tf_op jit(solution)/shard_map/ppermute | solution.py:22
  126.7 0.2 add_add_fusion
  127.0 2.1 %collective-permute-start.17 = (f32[40,1024]{1,0:T(8,128)S(1)}, f32[40,1024]{1,0:T(8,128)S(1)}, u32[]{:S(2)}, u32[]{:S(2)}) collective-permute-start(f32[40,1024]{1,0:T(8,128)S(1)} %get-tuple-element.67), channel_id=1, source_target_pairs={{0,2},{2,4},{4,6},{6,0},{1,3},{3,5},{5,7},{7,1},{8,10},{10,12},{12... | collective-permute-start | bytes 491528 | tf_op jit(solution)/shard_map/ppermute | solution.py:22
  129.1 1.2 collective-permute-start.19
  130.3 3.0 %collective-permute-start.18 = (f32[40,1024]{1,0:T(8,128)S(1)}, f32[40,1024]{1,0:T(8,128)S(1)}, u32[]{:S(2)}, u32[]{:S(2)}) collective-permute-start(f32[40,1024]{1,0:T(8,128)S(1)} %get-tuple-element.69), channel_id=1, source_target_pairs={{0,4},{2,6},{4,0},{6,2},{1,5},{3,7},{5,1},{7,3},{8,12},{10,14},{12... | collective-permute-start | bytes 491528 | tf_op jit(solution)/shard_map/ppermute | solution.py:22
  133.3 0.8 fusion.29
  134.2 1.9 %collective-permute-done.19 = f32[40,1024]{1,0:T(8,128)S(1)} collective-permute-done((f32[40,1024]{1,0:T(8,128)S(1)}, f32[40,1024]{1,0:T(8,128)S(1)}, u32[]{:S(2)}, u32[]{:S(2)}) %collective-permute-start.19) | collective-permute-done | bytes 163872 | tf_op jit(solution)/shard_map/ppermute | solution.py:22
  136.1 1.9 %collective-permute-done.18 = f32[40,1024]{1,0:T(8,128)S(1)} collective-permute-done((f32[40,1024]{1,0:T(8,128)S(1)}, f32[40,1024]{1,0:T(8,128)S(1)}, u32[]{:S(2)}, u32[]{:S(2)}) %collective-permute-start.18) | collective-permute-done | bytes 163872 | tf_op jit(solution)/shard_map/ppermute | solution.py:22
  137.9 0.8 fusion.27
  138.8 2.0 %collective-permute-start.27 = (f32[9,2304]{1,0:T(8,128)S(1)}, f32[9,2304]{1,0:T(8,128)S(1)}, u32[]{:S(2)}, u32[]{:S(2)}) collective-permute-start(f32[9,2304]{1,0:T(8,128)S(1)} %get-tuple-element.75), channel_id=1, source_target_pairs={{0,32},{32,64},{64,96},{96,0},{1,33},{33,65},{65,97},{97,1},{2,34}... | collective-permute-start | bytes 248840 | tf_op jit(solution)/shard_map/ppermute | solution.py:22
  140.8 2.2 %collective-permute-start.29 = (f32[9,2304]{1,0:T(8,128)S(1)}, f32[9,2304]{1,0:T(8,128)S(1)}, u32[]{:S(2)}, u32[]{:S(2)}) collective-permute-start(f32[9,2304]{1,0:T(8,128)S(1)} %get-tuple-element.76), channel_id=1, source_target_pairs={{0,96},{32,0},{64,32},{96,64},{1,97},{33,1},{65,33},{97,65},{2,98}... | collective-permute-start | bytes 248840 | tf_op jit(solution)/shard_map/ppermute | solution.py:22
  143.0 1.8 %collective-permute-start.28 = (f32[9,2304]{1,0:T(8,128)S(1)}, f32[9,2304]{1,0:T(8,128)S(1)}, u32[]{:S(2)}, u32[]{:S(2)}) collective-permute-start(f32[9,2304]{1,0:T(8,128)S(1)} %get-tuple-element.77), channel_id=1, source_target_pairs={{0,64},{32,96},{64,0},{96,32},{1,65},{33,97},{65,1},{97,33},{2,66}... | collective-permute-start | bytes 248840 | tf_op jit(solution)/shard_map/ppermute | solution.py:22
  144.7 0.8 fusion.6
  145.5 0.6 collective-permute-done.27
  146.1 2.6 %collective-permute-done.29 = f32[9,2304]{1,0:T(8,128)S(1)} collective-permute-done((f32[9,2304]{1,0:T(8,128)S(1)}, f32[9,2304]{1,0:T(8,128)S(1)}, u32[]{:S(2)}, u32[]{:S(2)}) %collective-permute-start.29) | collective-permute-done | bytes 82976 | tf_op jit(solution)/shard_map/ppermute | solution.py:22
  148.7 1.9 %collective-permute-done.28 = f32[9,2304]{1,0:T(8,128)S(1)} collective-permute-done((f32[9,2304]{1,0:T(8,128)S(1)}, f32[9,2304]{1,0:T(8,128)S(1)}, u32[]{:S(2)}, u32[]{:S(2)}) %collective-permute-start.28) | collective-permute-done | bytes 82976 | tf_op jit(solution)/shard_map/ppermute | solution.py:22
  150.6 0.7 fusion.24
  (86 shorter events, 1.8 us)
Async XLA Ops:
  0.6 1.2 copy-start
  2.3 1.7 %collective-permute-start = (f32[72,1024]{1,0:T(8,128)S(1)}, f32[72,1024]{1,0:T(8,128)S(1)}, u32[]{:S(2)}, u32[]{:S(2)}) collective-permute-start(f32[72,1024]{1,0:T(8,128)S(1)} %copy.16), channel_id=1, source_target_pairs={{0,1},{1,0},{2,3},{3,2},{4,5},{5,4},{6,7},{7,6},{8,9},{9,8},{10,11... | collective-permute-start | bytes 884744 | tf_op jit(solution)/shard_map/ppermute | solution.py:22
  4.0 29.0 %collective-permute-start.2 = (f32[72,512]{1,0:T(8,128)S(1)}, f32[72,512]{1,0:T(8,128)S(1)}, u32[]{:S(2)}, u32[]{:S(2)}) collective-permute-start(f32[72,512]{1,0:T(8,128)S(1)} %dynamic-slice_add_fusion), channel_id=1, source_target_pairs={{0,16},{8,24},{16,0},{24,8},{1,17},{9,25},{17,1},{25,9},{2,18},{10... | collective-permute-start | bytes 442376 | tf_op jit(solution)/shard_map/ppermute | solution.py:22
  7.3 25.7 %collective-permute-start.1 = (f32[72,512]{1,0:T(8,128)S(1)}, f32[72,512]{1,0:T(8,128)S(1)}, u32[]{:S(2)}, u32[]{:S(2)}) collective-permute-start(f32[72,512]{1,0:T(8,128)S(1)} %dynamic-slice_add_fusion), channel_id=1, source_target_pairs={{0,8},{8,16},{16,24},{24,0},{1,9},{9,17},{17,25},{25,1},{2,10},{10... | collective-permute-start | bytes 442376 | tf_op jit(solution)/shard_map/ppermute | solution.py:22
  8.0 25.0 %collective-permute-start.3 = (f32[72,512]{1,0:T(8,128)S(1)}, f32[72,512]{1,0:T(8,128)S(1)}, u32[]{:S(2)}, u32[]{:S(2)}) collective-permute-start(f32[72,512]{1,0:T(8,128)S(1)} %dynamic-slice_add_fusion), channel_id=1, source_target_pairs={{0,24},{8,0},{16,8},{24,16},{1,25},{9,1},{17,9},{25,17},{2,26},{10... | collective-permute-start | bytes 442376 | tf_op jit(solution)/shard_map/ppermute | solution.py:22
  33.1 1.9 %collective-permute-start.4 = (f32[80,1024]{1,0:T(8,128)}, f32[80,1024]{1,0:T(8,128)S(1)}, u32[]{:S(2)}, u32[]{:S(2)}) collective-permute-start(f32[80,1024]{1,0:T(8,128)} %get-tuple-element.32.own_ref), channel_id=1, source_target_pairs={{0,1},{1,0},{2,3},{3,2},{4,5},{5,4},{6,7},{7,6},{8,9},{9,8},{10,11... | collective-permute-start | bytes 983048 | tf_op jit(solution)/shard_map/ppermute | solution.py:22
  35.0 1.0 copy-start.4
  36.0 17.2 %collective-permute-start.7 = (f32[160,512]{1,0:T(8,128)S(1)}, f32[160,512]{1,0:T(8,128)S(1)}, u32[]{:S(2)}, u32[]{:S(2)}) collective-permute-start(f32[160,512]{1,0:T(8,128)S(1)} %pair.1), channel_id=1, source_target_pairs={{0,6},{2,0},{4,2},{6,4},{1,7},{3,1},{5,3},{7,5},{8,14},{10,8},{12,... | collective-permute-start | bytes 983048 | tf_op jit(solution)/shard_map/ppermute | solution.py:22
  38.9 14.3 %collective-permute-start.6 = (f32[160,512]{1,0:T(8,128)S(1)}, f32[160,512]{1,0:T(8,128)S(1)}, u32[]{:S(2)}, u32[]{:S(2)}) collective-permute-start(f32[160,512]{1,0:T(8,128)S(1)} %pair.1), channel_id=1, source_target_pairs={{0,4},{2,6},{4,0},{6,2},{1,5},{3,7},{5,1},{7,3},{8,12},{10,14},{12... | collective-permute-start | bytes 983048 | tf_op jit(solution)/shard_map/ppermute | solution.py:22
  39.7 17.2 %collective-permute-start.5 = (f32[160,512]{1,0:T(8,128)S(1)}, f32[160,512]{1,0:T(8,128)S(1)}, u32[]{:S(2)}, u32[]{:S(2)}) collective-permute-start(f32[160,512]{1,0:T(8,128)S(1)} %pair.1), channel_id=1, source_target_pairs={{0,2},{2,4},{4,6},{6,0},{1,3},{3,5},{5,7},{7,1},{8,10},{10,12},{12... | collective-permute-start | bytes 983048 | tf_op jit(solution)/shard_map/ppermute | solution.py:22
  40.6 18.6 %copy-start.7 = (bf16[1536,1024]{1,0:T(8,128)(2,1)S(1)}, bf16[1536,1024]{1,0:T(8,128)(2,1)}, u32[]{:S(2)}) copy-start(bf16[1536,1024]{1,0:T(8,128)(2,1)} %get-tuple-element.38.e_ref) | copy-start | bytes 9437188
  57.0 11.2 %collective-permute-start.11 = (f32[80,512]{1,0:T(8,128)S(1)}, f32[80,512]{1,0:T(8,128)S(1)}, u32[]{:S(2)}, u32[]{:S(2)}) collective-permute-start(f32[80,512]{1,0:T(8,128)S(1)} %fusion.15), channel_id=1, source_target_pairs={{0,24},{8,0},{16,8},{24,16},{1,25},{9,1},{17,9},{25,17},{2,26},{10... | collective-permute-start | bytes 491528 | tf_op jit(solution)/shard_map/ppermute | solution.py:22
  57.1 11.1 %collective-permute-start.10 = (f32[80,512]{1,0:T(8,128)S(1)}, f32[80,512]{1,0:T(8,128)S(1)}, u32[]{:S(2)}, u32[]{:S(2)}) collective-permute-start(f32[80,512]{1,0:T(8,128)S(1)} %fusion.15), channel_id=1, source_target_pairs={{0,16},{8,24},{16,0},{24,8},{1,17},{9,25},{17,1},{25,9},{2,18},{10... | collective-permute-start | bytes 491528 | tf_op jit(solution)/shard_map/ppermute | solution.py:22
  58.6 9.7 %collective-permute-start.9 = (f32[80,512]{1,0:T(8,128)S(1)}, f32[80,512]{1,0:T(8,128)S(1)}, u32[]{:S(2)}, u32[]{:S(2)}) collective-permute-start(f32[80,512]{1,0:T(8,128)S(1)} %fusion.15), channel_id=1, source_target_pairs={{0,8},{8,16},{16,24},{24,0},{1,9},{9,17},{17,25},{25,1},{2,10},{10... | collective-permute-start | bytes 491528 | tf_op jit(solution)/shard_map/ppermute | solution.py:22
  62.9 21.1 %collective-permute-start.20 = (f32[640,1024]{1,0:T(8,128)}, f32[640,1024]{1,0:T(8,128)}, u32[]{:S(2)}, u32[]{:S(2)}) collective-permute-start(f32[640,1024]{1,0:T(8,128)} %fusion.2), channel_id=1, source_target_pairs={{0,1},{1,0},{2,3},{3,2},{4,5},{5,4},{6,7},{7,6},{8,9},{9,8},{10,11... | collective-permute-start | bytes 7864328 | tf_op jit(solution)/shard_map/ppermute | solution.py:22
  62.9 4.7 %collective-permute-start.8 = (f32[72,512]{1,0:T(8,128)S(1)}, f32[72,512]{1,0:T(8,128)S(1)}, u32[]{:S(2)}, u32[]{:S(2)}) collective-permute-start(f32[72,512]{1,0:T(8,128)S(1)} %slice_add_fusion.1), channel_id=1, source_target_pairs={{0,1},{1,0},{2,3},{3,2},{4,5},{5,4},{6,7},{7,6},{8,9},{9,8},{10,11... | collective-permute-start | bytes 442376 | tf_op jit(solution)/shard_map/ppermute | solution.py:22
  67.6 3.2 %copy-start.9 = (bf16[1536,1152]{1,0:T(8,128)(2,1)S(1)}, bf16[1536,1152]{1,0:T(8,128)(2,1)}, u32[]{:S(2)}) copy-start(bf16[1536,1152]{1,0:T(8,128)(2,1)} %get-tuple-element.40.v_ref) | copy-start | bytes 10616836
  68.4 1.5 collective-permute-start.12
  79.5 1.5 copy-start.2
  81.0 1.7 %copy-start.10 = (bf16[1536,1024]{1,0:T(8,128)(2,1)}, bf16[1536,1024]{1,0:T(8,128)(2,1)S(1)}, u32[]{:S(2)}) copy-start(bf16[1536,1024]{1,0:T(8,128)(2,1)S(1)} %get-tuple-element.45.d_ref) | copy-start | bytes 9437188
  82.7 7.1 %collective-permute-start.13 = (f32[640,1024]{1,0:T(8,128)}, f32[640,1024]{1,0:T(8,128)}, u32[]{:S(2)}, u32[]{:S(2)}) collective-permute-start(f32[640,1024]{1,0:T(8,128)} %get-tuple-element.43), channel_id=1, source_target_pairs={{0,1},{1,0},{2,3},{3,2},{4,5},{5,4},{6,7},{7,6},{8,9},{9,8},{10,11... | collective-permute-start | bytes 7864328 | tf_op jit(solution)/shard_map/ppermute | solution.py:22
  87.2 2.6 %copy-start.3 = (f32[640,1024]{1,0:T(8,128)S(1)}, f32[640,1024]{1,0:T(8,128)}, u32[]{:S(2)}) copy-start(f32[640,1024]{1,0:T(8,128)} %copy-done.2) | copy-start | bytes 7864324
  87.5 17.6 %collective-permute-start.23 = (f32[4,40,1024]{2,1,0:T(8,128)S(1)}, f32[4,40,1024]{2,1,0:T(8,128)S(1)}, u32[]{:S(2)}, u32[]{:S(2)}) collective-permute-start(f32[4,40,1024]{2,1,0:T(8,128)S(1)} %bitcast.92), channel_id=1, source_target_pairs={{0,6},{2,0},{4,2},{6,4},{1,7},{3,1},{5,3},{7,5},{8,14},{10,8},{12,... | collective-permute-start | bytes 1966088 | tf_op jit(solution)/shard_map/ppermute | solution.py:22
  88.1 32.3 %collective-permute-start.22 = (f32[4,40,1024]{2,1,0:T(8,128)S(1)}, f32[4,40,1024]{2,1,0:T(8,128)S(1)}, u32[]{:S(2)}, u32[]{:S(2)}) collective-permute-start(f32[4,40,1024]{2,1,0:T(8,128)S(1)} %bitcast.91), channel_id=1, source_target_pairs={{0,4},{2,6},{4,0},{6,2},{1,5},{3,7},{5,1},{7,3},{8,12},{10,14},{12... | collective-permute-start | bytes 1966088 | tf_op jit(solution)/shard_map/ppermute | solution.py:22
  89.0 31.5 %collective-permute-start.21 = (f32[4,40,1024]{2,1,0:T(8,128)S(1)}, f32[4,40,1024]{2,1,0:T(8,128)S(1)}, u32[]{:S(2)}, u32[]{:S(2)}) collective-permute-start(f32[4,40,1024]{2,1,0:T(8,128)S(1)} %bitcast.90), channel_id=1, source_target_pairs={{0,2},{2,4},{4,6},{6,0},{1,3},{3,5},{5,7},{7,1},{8,10},{10,12},{12... | collective-permute-start | bytes 1966088 | tf_op jit(solution)/shard_map/ppermute | solution.py:22
  89.8 6.7 %copy-start.14 = (bf16[1152,1152]{1,0:T(8,128)(2,1)S(1)}, bf16[1152,1152]{1,0:T(8,128)(2,1)}, u32[]{:S(2)}) copy-start(bf16[1152,1152]{1,0:T(8,128)(2,1)} %wv_far.1) | copy-start | bytes 7962628
  91.9 32.1 %collective-permute-start.14 = (f32[160,1024]{1,0:T(8,128)S(1)}, f32[160,1024]{1,0:T(8,128)S(1)}, u32[]{:S(2)}, u32[]{:S(2)}) collective-permute-start(f32[160,1024]{1,0:T(8,128)S(1)} %get-tuple-element.50), channel_id=1, source_target_pairs={{0,8},{8,16},{16,24},{24,0},{1,9},{9,17},{17,25},{25,1},{2,10},{10... | collective-permute-start | bytes 1966088 | tf_op jit(solution)/shard_map/ppermute | solution.py:22
  93.5 6.4 %copy-start.12 = (bf16[1152,1024]{1,0:T(8,128)(2,1)S(1)}, bf16[1152,1024]{1,0:T(8,128)(2,1)}, u32[]{:S(2)}) copy-start(bf16[1152,1024]{1,0:T(8,128)(2,1)} %get-tuple-element.47) | copy-start | bytes 7077892
  93.5 6.4 %copy-start.15 = (bf16[1152,1152]{1,0:T(8,128)(2,1)S(1)}, bf16[1152,1152]{1,0:T(8,128)(2,1)}, u32[]{:S(2)}) copy-start(bf16[1152,1152]{1,0:T(8,128)(2,1)} %wk_far.1) | copy-start | bytes 7962628
  93.5 33.2 %collective-permute-start.15 = (f32[160,1024]{1,0:T(8,128)S(1)}, f32[160,1024]{1,0:T(8,128)S(1)}, u32[]{:S(2)}, u32[]{:S(2)}) collective-permute-start(f32[160,1024]{1,0:T(8,128)S(1)} %get-tuple-element.51), channel_id=1, source_target_pairs={{0,16},{8,24},{16,0},{24,8},{1,17},{9,25},{17,1},{25,9},{2,18},{10... | collective-permute-start | bytes 1966088 | tf_op jit(solution)/shard_map/ppermute | solution.py:22
  100.0 7.9 %copy-start.5 = (bf16[1,1458,1152]{2,1,0:T(8,128)(2,1)S(1)}, bf16[1,1458,1152]{2,1,0:T(8,128)(2,1)}, u32[]{:S(2)}) copy-start(bf16[1,1458,1152]{2,1,0:T(8,128)(2,1)} %param.8) | copy-start | bytes 10077700
  100.0 7.9 %copy-start.6 = (bf16[1152]{0:T(1024)(128)(2,1)S(1)}, bf16[1152]{0:T(1024)(128)(2,1)}, u32[]{:S(2)}) copy-start(bf16[1152]{0:T(1024)(128)(2,1)} %gain_ref.3) | copy-start | bytes 6916
  100.0 7.9 %copy-start.8 = (bf16[1536,1024]{1,0:T(8,128)(2,1)S(1)}, bf16[1536,1024]{1,0:T(8,128)(2,1)}, u32[]{:S(2)}) copy-start(bf16[1536,1024]{1,0:T(8,128)(2,1)} %get-tuple-element.38.e_ref) | copy-start | bytes 9437188
  100.0 7.9 %copy-start.11 = (bf16[1536,1024]{1,0:T(8,128)(2,1)S(1)}, bf16[1536,1024]{1,0:T(8,128)(2,1)}, u32[]{:S(2)}) copy-start(bf16[1536,1024]{1,0:T(8,128)(2,1)} %copy-done.10) | copy-start | bytes 9437188
  105.1 21.6 %collective-permute-start.16 = (f32[160,1024]{1,0:T(8,128)S(1)}, f32[160,1024]{1,0:T(8,128)S(1)}, u32[]{:S(2)}, u32[]{:S(2)}) collective-permute-start(f32[160,1024]{1,0:T(8,128)S(1)} %get-tuple-element.52), channel_id=1, source_target_pairs={{0,24},{8,0},{16,8},{24,16},{1,25},{9,1},{17,9},{25,17},{2,26},{10... | collective-permute-start | bytes 1966088 | tf_op jit(solution)/shard_map/ppermute | solution.py:22
  120.8 9.5 %collective-permute-start.24 = (f32[40,1024]{1,0:T(8,128)S(1)}, f32[40,1024]{1,0:T(8,128)S(1)}, u32[]{:S(2)}, u32[]{:S(2)}) collective-permute-start(f32[40,1024]{1,0:T(8,128)S(1)} %get-tuple-element.70), channel_id=1, source_target_pairs={{0,8},{8,16},{16,24},{24,0},{1,9},{9,17},{17,25},{25,1},{2,10},{10... | collective-permute-start | bytes 491528 | tf_op jit(solution)/shard_map/ppermute | solution.py:22
  122.1 11.2 %collective-permute-start.26 = (f32[40,1024]{1,0:T(8,128)S(1)}, f32[40,1024]{1,0:T(8,128)S(1)}, u32[]{:S(2)}, u32[]{:S(2)}) collective-permute-start(f32[40,1024]{1,0:T(8,128)S(1)} %get-tuple-element.71), channel_id=1, source_target_pairs={{0,24},{8,0},{16,8},{24,16},{1,25},{9,1},{17,9},{25,17},{2,26},{10... | collective-permute-start | bytes 491528 | tf_op jit(solution)/shard_map/ppermute | solution.py:22
  124.1 9.3 %collective-permute-start.25 = (f32[40,1024]{1,0:T(8,128)S(1)}, f32[40,1024]{1,0:T(8,128)S(1)}, u32[]{:S(2)}, u32[]{:S(2)}) collective-permute-start(f32[40,1024]{1,0:T(8,128)S(1)} %get-tuple-element.72), channel_id=1, source_target_pairs={{0,16},{8,24},{16,0},{24,8},{1,17},{9,25},{17,1},{25,9},{2,18},{10... | collective-permute-start | bytes 491528 | tf_op jit(solution)/shard_map/ppermute | solution.py:22
  127.0 7.2 %collective-permute-start.17 = (f32[40,1024]{1,0:T(8,128)S(1)}, f32[40,1024]{1,0:T(8,128)S(1)}, u32[]{:S(2)}, u32[]{:S(2)}) collective-permute-start(f32[40,1024]{1,0:T(8,128)S(1)} %get-tuple-element.67), channel_id=1, source_target_pairs={{0,2},{2,4},{4,6},{6,0},{1,3},{3,5},{5,7},{7,1},{8,10},{10,12},{12... | collective-permute-start | bytes 491528 | tf_op jit(solution)/shard_map/ppermute | solution.py:22
  129.1 7.0 %collective-permute-start.19 = (f32[40,1024]{1,0:T(8,128)S(1)}, f32[40,1024]{1,0:T(8,128)S(1)}, u32[]{:S(2)}, u32[]{:S(2)}) collective-permute-start(f32[40,1024]{1,0:T(8,128)S(1)} %get-tuple-element.68), channel_id=1, source_target_pairs={{0,6},{2,0},{4,2},{6,4},{1,7},{3,1},{5,3},{7,5},{8,14},{10,8},{12,... | collective-permute-start | bytes 491528 | tf_op jit(solution)/shard_map/ppermute | solution.py:22
  130.3 7.6 %collective-permute-start.18 = (f32[40,1024]{1,0:T(8,128)S(1)}, f32[40,1024]{1,0:T(8,128)S(1)}, u32[]{:S(2)}, u32[]{:S(2)}) collective-permute-start(f32[40,1024]{1,0:T(8,128)S(1)} %get-tuple-element.69), channel_id=1, source_target_pairs={{0,4},{2,6},{4,0},{6,2},{1,5},{3,7},{5,1},{7,3},{8,12},{10,14},{12... | collective-permute-start | bytes 491528 | tf_op jit(solution)/shard_map/ppermute | solution.py:22
  133.3 18.0 %copy-start.1 = (bf16[1,64,36]{1,2,0:T(8,128)(2,1)S(1)}, bf16[1,64,36]{1,2,0:T(8,128)(2,1)}, u32[]{:S(2)}) copy-start(bf16[1,64,36]{1,2,0:T(8,128)(2,1)} %param.15) | copy-start | bytes 13828
  134.1 10.6 %copy-start.13 = (bf16[1152,36]{0,1:T(8,128)(2,1)S(1)}, bf16[1152,36]{0,1:T(8,128)(2,1)}, u32[]{:S(2)}) copy-start(bf16[1152,36]{0,1:T(8,128)(2,1)} %param.14) | copy-start | bytes 248836
  138.8 7.3 %collective-permute-start.27 = (f32[9,2304]{1,0:T(8,128)S(1)}, f32[9,2304]{1,0:T(8,128)S(1)}, u32[]{:S(2)}, u32[]{:S(2)}) collective-permute-start(f32[9,2304]{1,0:T(8,128)S(1)} %get-tuple-element.75), channel_id=1, source_target_pairs={{0,32},{32,64},{64,96},{96,0},{1,33},{33,65},{65,97},{97,1},{2,34}... | collective-permute-start | bytes 248840 | tf_op jit(solution)/shard_map/ppermute | solution.py:22
  140.8 7.9 %collective-permute-start.29 = (f32[9,2304]{1,0:T(8,128)S(1)}, f32[9,2304]{1,0:T(8,128)S(1)}, u32[]{:S(2)}, u32[]{:S(2)}) collective-permute-start(f32[9,2304]{1,0:T(8,128)S(1)} %get-tuple-element.76), channel_id=1, source_target_pairs={{0,96},{32,0},{64,32},{96,64},{1,97},{33,1},{65,33},{97,65},{2,98}... | collective-permute-start | bytes 248840 | tf_op jit(solution)/shard_map/ppermute | solution.py:22
  143.0 7.7 %collective-permute-start.28 = (f32[9,2304]{1,0:T(8,128)S(1)}, f32[9,2304]{1,0:T(8,128)S(1)}, u32[]{:S(2)}, u32[]{:S(2)}) collective-permute-start(f32[9,2304]{1,0:T(8,128)S(1)} %get-tuple-element.77), channel_id=1, source_target_pairs={{0,64},{32,96},{64,0},{96,32},{1,65},{33,97},{65,1},{97,33},{2,66}... | collective-permute-start | bytes 248840 | tf_op jit(solution)/shard_map/ppermute | solution.py:22
